TPU v7x, 256 devices: a whole 4x4x8 slice. The times are simulated.
256 devices in a mesh: dom: 64 (over z, y, core), rep: 4 (over x).
Axes of the slice: x: 4, y: 4, z: 8, core: 2. Of those that a mesh axis runs over, the one named last changes fastest.
Arguments:
- adjacency: bfloat16 [131072, 2048], P('dom'), may hold values from -0.09375 to 0.09375
- grad_out: bfloat16 [4, 131072, 128], P('rep', 'dom'), may hold values from -6 to 6
- row_owner: int32 [131072, 1], P('dom'), may hold values from 0 to 63; in each aligned block of 512 rows (0 to 511, 512 to 1023, ...) at most 16 rows name the same one
- table_slot: int32 [131072], P('dom'), may hold values from 0 to 511
- table_rows: float32 [32768, 128], P('dom'), may hold values from -6 to 6
- row_accumulators: float32 [32768], P('dom'), may hold values from 0.01 to 1
Outputs:
- new_table: float32 [32768, 128], P('dom')
- new_accumulators: float32 [32768], P('dom')
- fresh_rows: bfloat16 [131072, 128], P('dom')
Inputs may be any that keep to these rules, and one draw needn't show every extreme that they name: `row_owner`: in each aligned block of 512 rows no owner is named by more than 16 rows, a bound that some block reaches.
All inputs are finite; a program needn't handle non-finite values.
Results may differ from a plain program's by a relative error of at most 0.009.
Values may be sent and summed in bfloat16 or wider, within the bound.
No kernel may reach another device: no remote copies, remote signals or barrier semaphores. Data moves between devices by JAX's collectives and lax.ppermute only.
A program may use at most 64 MiB of HBM per device.

v0:
```python
import jax
import jax.numpy as jnp
from jax import lax
from jax.sharding import PartitionSpec as P

LAYERS = 3
LEARN_RATE = 0.5
LANES = 128
SPARE = 8


def adjoint(tile, piece):
    return lax.dot_general(
        tile, piece, (((0,), (0,)), ((), ())), preferred_element_type=jnp.float32
    )


def propagate(adjacency, start):
    state = start
    total = state.astype(jnp.float32)
    for layer in range(LAYERS):
        state = adjoint(adjacency, state).astype(jnp.bfloat16)
        total = total + state.astype(jnp.float32)
    return total / jnp.float32(LAYERS + 1)


def one_hot(values, count, axis):
    shape = (count, values.shape[0]) if axis == 0 else (values.shape[0], count)
    ids = lax.broadcasted_iota(jnp.int32, shape, axis)
    return (jnp.expand_dims(values, axis) == ids).astype(jnp.bfloat16)


def plan(owners, peers, capacity):
    count = owners.shape[0]
    owner_hot = one_hot(owners, peers, 1)
    lower = (
        lax.broadcasted_iota(jnp.int32, (count, count), 0)
        >= lax.broadcasted_iota(jnp.int32, (count, count), 1)
    ).astype(jnp.bfloat16)
    running = jnp.dot(lower, owner_hot, preferred_element_type=jnp.float32)
    ranks = jnp.sum(owner_hot.astype(jnp.float32) * (running - 1.0), axis=1).astype(jnp.int32)
    dispatch = one_hot(owners * capacity + ranks, peers * capacity, 1)
    return owner_hot, ranks, dispatch


def slot_rows(owner_hot, ranks, slots, capacity):
    lane = lax.broadcasted_iota(jnp.int32, (1, LANES), 1)
    part = jnp.where(lane < capacity, slots[:, None] // 16, slots[:, None] % 16)
    hit = (lane < 2 * capacity) & (ranks[:, None] == lane % capacity)
    spread = jnp.where(hit, part, 0).astype(jnp.bfloat16)
    rows = lax.dot_general(
        owner_hot, spread, (((0,), (0,)), ((), ())), preferred_element_type=jnp.float32
    )
    return rows.astype(jnp.bfloat16)


def on_device(adjacency, grad_out, row_owner, table_slot, table_rows, row_accumulators):
    peers = lax.axis_size("dom")
    replicas = lax.axis_size("rep")
    rows = adjacency.shape[0]
    width = grad_out.shape[2]
    shard = table_rows.shape[0]
    quarter = rows // replicas
    capacity = max(2, 2 * quarter // peers)
    here = lax.axis_index("rep") * quarter
    owners = lax.dynamic_slice(row_owner[:, 0], (here,), (quarter,))
    slots = lax.dynamic_slice(table_slot, (here,), (quarter,))
    owner_hot, ranks, dispatch = plan(owners, peers, capacity)
    slot_row = slot_rows(owner_hot, ranks, slots, capacity)

    term = propagate(adjacency, grad_out[0]).astype(jnp.bfloat16)
    terms = lax.all_to_all(
        term.reshape(replicas, quarter, width), "rep", split_axis=0, concat_axis=0, tiled=True
    )
    row_grad = jnp.sum(terms.astype(jnp.float32), axis=0).astype(jnp.bfloat16)

    outgoing = lax.dot_general(
        dispatch, row_grad, (((0,), (0,)), ((), ())), preferred_element_type=jnp.float32
    ).astype(jnp.bfloat16)
    message = jnp.concatenate(
        [
            outgoing.reshape(peers, capacity, width),
            jnp.broadcast_to(slot_row[:, None, :], (peers, SPARE, LANES)),
        ],
        axis=1,
    )
    incoming = lax.all_to_all(message, "dom", split_axis=0, concat_axis=0, tiled=True)
    got = incoming[:, capacity, : 2 * capacity].astype(jnp.int32)
    got_slots = (got[:, :capacity] * 16 + got[:, capacity:]).reshape(-1)
    receiver = one_hot(got_slots, shard, 0)
    partial = jnp.dot(
        receiver,
        incoming[:, :capacity].reshape(peers * capacity, width),
        preferred_element_type=jnp.float32,
    ).astype(jnp.bfloat16)
    partials = lax.all_to_all(
        jnp.broadcast_to(partial, (replicas, shard, width)),
        "rep", split_axis=0, concat_axis=0, tiled=True,
    )
    table_grad = jnp.sum(partials.astype(jnp.float32), axis=0)
    new_accumulators = row_accumulators + jnp.mean(table_grad * table_grad, axis=1)
    new_table = table_rows - LEARN_RATE * table_grad / jnp.sqrt(new_accumulators)[:, None]

    answer = lax.dot_general(
        receiver, new_table.astype(jnp.bfloat16), (((0,), (0,)), ((), ())),
        preferred_element_type=jnp.float32,
    ).astype(jnp.bfloat16)
    returned = lax.all_to_all(
        answer.reshape(peers, capacity, width), "dom", split_axis=0, concat_axis=0, tiled=True
    )
    fresh = jnp.dot(
        dispatch, returned.reshape(peers * capacity, width), preferred_element_type=jnp.float32
    ).astype(jnp.bfloat16)
    fresh_rows = lax.all_to_all(
        jnp.broadcast_to(fresh, (replicas, quarter, width)),
        "rep", split_axis=0, concat_axis=0, tiled=True,
    ).reshape(rows, width)
    return (new_table, new_accumulators, fresh_rows)


def solution(mesh):
    return jax.shard_map(
        on_device,
        mesh=mesh,
        in_specs=(
            P("dom", None),
            P("rep", "dom", None),
            P("dom", None),
            P("dom"),
            P("dom", None),
            P("dom"),
        ),
        out_specs=(P("dom", None), P("dom"), P("dom", None)),
        check_vma=False,
    )
```

profile of v0, /device:TPU:1, one launch (start us, length us, event | category | flops | bytes accessed | tf_op | source)
XLA Modules:
  0.0 102.8 jit_solution(1609463747012922693)
XLA Ops:
  0.6 6.0 %convolution_convert_fusion.2 = bf16[2048,128]{1,0:T(8,128)(2,1)S(1)} fusion(bf16[2048,2048]{1,0:T(8,128)(2,1)} %param.6, bf16[1,2048,128]{2,1,0:T(8,128)(2,1)} %param.7), kind=kOutput, calls=%fused_computation.6 | convolution fusion | flops 1074003968 | bytes 9437184 | tf_op jit(solution)/shard_map/dot_general | solution.py:13
  6.6 0.0 copy-done
  6.6 0.0 copy-start.4
  6.6 3.4 %convolution_convert_fusion.1 = bf16[128,2048]{0,1:T(8,128)(2,1)S(1)} fusion(bf16[2048,128]{1,0:T(8,128)(2,1)S(1)} %convolution_convert_fusion.2, bf16[2048,2048]{1,0:T(8,128)(2,1)S(1)} %copy-done), kind=kOutput, calls=%fused_computation.5 | convolution fusion | flops 1074003968 | bytes 9437184 | tf_op jit(solution)/shard_map/dot_general | solution.py:13
  10.0 0.0 copy-start.5
  10.0 0.0 copy-start.2
  10.0 3.6 %fusion.4 = bf16[2048,128]{1,0:T(8,128)(2,1)} fusion(bf16[128,2048]{0,1:T(8,128)(2,1)S(1)} %convolution_convert_fusion.1, bf16[2048,2048]{1,0:T(8,128)(2,1)S(1)} %copy-done, bf16[2048,128]{1,0:T(8,128)(2,1)S(1)} %convolution_convert_fusion.2, bf16[1,2048,128]{2,1,0:T(8,128)(2,1)S(1)} %copy-done.1), kind=kOutput, calls=%fused_computation.7 | convolution fusion | flops 1076363264 | bytes 10485760 | tf_op jit(solution)/shard_map/dot_general | solution.py:13
  13.6 4.8 %all-to-all-start = ((bf16[4,512,128]{2,1,0:T(8,128)(2,1)}), bf16[4,512,128]{2,1,0:T(8,128)(2,1)S(1)}, u32[]{:S(2)}, u32[]{:S(2)}) async-start(bf16[4,512,128]{2,1,0:T(8,128)(2,1)} %bitcast.6), calls=%async_computation | async-start | bytes 1048576 | tf_op jit(solution)/shard_map/all_to_all | solution.py:72
  18.5 0.0 copy-done.4
  18.5 0.3 fusion.14
  18.8 0.8 add_select_fusion.1
  19.6 0.4 convolution_convert_fusion.3
  20.0 5.8 %all-to-all-done = bf16[4,512,128]{2,1,0:T(8,128)(2,1)S(1)} async-done(((bf16[4,512,128]{2,1,0:T(8,128)(2,1)}), bf16[4,512,128]{2,1,0:T(8,128)(2,1)S(1)}, u32[]{:S(2)}, u32[]{:S(2)}) %all-to-all-start) | async-done | bytes 524320 | tf_op jit(solution)/shard_map/all_to_all | solution.py:72
  25.8 0.1 reduce_sum.40
  25.9 0.8 fusion.9
  26.8 29.6 %all_to_all.25 = bf16[64,24,128]{2,1,0:T(8,128)(2,1)S(1)} all-to-all(bf16[64,24,128]{2,1,0:T(8,128)(2,1)S(1)} %pad_maximum_fusion), channel_id=1, replica_groups=mesh['dom'=64,'rep'=4] {'dom'}, dimensions={0} | all-to-all | bytes 786432 | tf_op jit(solution)/shard_map/all_to_all | solution.py:87
  56.4 0.1 slice_add_fusion
  56.5 0.1 eq.56
  56.6 0.5 fusion.12
  57.1 0.1 broadcast_in_dim.51
  57.1 11.9 %all_to_all.26 = bf16[4,512,128]{2,1,0:T(8,128)(2,1)S(1)} all-to-all(bf16[4,512,128]{2,1,0:T(8,128)(2,1)S(1)} %broadcast_in_dim.51), channel_id=1, replica_groups=mesh['dom'=64,'rep'=4] {'rep'}, dimensions={0} | all-to-all | bytes 1048576 | tf_op jit(solution)/shard_map/all_to_all | solution.py:96
  69.0 0.1 convert_reduce_fusion
  69.1 0.1 multiply_reduce_fusion
  69.3 0.6 fusion.33
  69.8 0.1 divide_subtract_fusion
  70.0 0.0 copy-start.3
  70.0 0.7 fusion.10
  70.7 18.9 %all_to_all.27 = bf16[64,16,128]{2,1,0:T(8,128)(2,1)S(1)} all-to-all(bf16[64,16,128]{2,1,0:T(8,128)(2,1)S(1)} %bitcast.39), channel_id=1, replica_groups=mesh['dom'=64,'rep'=4] {'dom'}, dimensions={0} | all-to-all | bytes 524288 | tf_op jit(solution)/shard_map/all_to_all | solution.py:108
  89.7 0.5 fusion.11
  90.2 0.1 broadcast_in_dim.52
  90.3 11.7 %all_to_all.28 = bf16[4,512,128]{2,1,0:T(8,128)(2,1)S(1)} all-to-all(bf16[4,512,128]{2,1,0:T(8,128)(2,1)S(1)} %broadcast_in_dim.52), channel_id=1, replica_groups=mesh['dom'=64,'rep'=4] {'rep'}, dimensions={0} | all-to-all | bytes 1048576 | tf_op jit(solution)/shard_map/all_to_all | solution.py:114
  102.0 0.8 copy.21
  (15 shorter events, 0.2 us)
Async XLA Ops:
  0.6 6.0 %copy-start = (bf16[2048,2048]{1,0:T(8,128)(2,1)S(1)}, bf16[2048,2048]{1,0:T(8,128)(2,1)}, u32[]{:S(2)}) copy-start(bf16[2048,2048]{1,0:T(8,128)(2,1)} %param.6) | copy-start | bytes 25165828
  0.6 9.4 %copy-start.1 = (bf16[1,2048,128]{2,1,0:T(8,128)(2,1)S(1)}, bf16[1,2048,128]{2,1,0:T(8,128)(2,1)}, u32[]{:S(2)}) copy-start(bf16[1,2048,128]{2,1,0:T(8,128)(2,1)} %param.7) | copy-start | bytes 1572868
  6.6 11.8 %copy-start.4 = (s32[2048,1]{0,1:T(1,128)S(1)}, s32[2048,1]{0,1:T(1,128)}, u32[]{:S(2)}) copy-start(s32[2048,1]{0,1:T(1,128)} %param.8) | copy-start | bytes 24580
  10.0 59.2 %copy-start.5 = (f32[512]{0:T(512)S(1)}, f32[512]{0:T(512)}, u32[]{:S(2)}) copy-start(f32[512]{0:T(512)} %param.11) | copy-start | bytes 6148
  10.0 59.8 %copy-start.2 = (f32[512,128]{1,0:T(8,128)S(1)}, f32[512,128]{1,0:T(8,128)}, u32[]{:S(2)}) copy-start(f32[512,128]{1,0:T(8,128)} %param.10) | copy-start | bytes 786436
  13.6 12.2 %all-to-all-start = ((bf16[4,512,128]{2,1,0:T(8,128)(2,1)}), bf16[4,512,128]{2,1,0:T(8,128)(2,1)S(1)}, u32[]{:S(2)}, u32[]{:S(2)}) async-start(bf16[4,512,128]{2,1,0:T(8,128)(2,1)} %bitcast.6), calls=%async_computation | async-start | bytes 1048576 | tf_op jit(solution)/shard_map/all_to_all | solution.py:72
  70.0 32.8 %copy-start.3 = (f32[512,128]{1,0:T(8,128)}, f32[512,128]{1,0:T(8,128)S(1)}, u32[]{:S(2)}) copy-start(f32[512,128]{1,0:T(8,128)S(1)} %divide_subtract_fusion) | copy-start | bytes 786436
where the time goes:
time: 103 us
  blocking collectives  72.1 us (70%)
  matrix products  16.1 us (16%)
  waiting for transfers between devices  5.84 us (6%)
  starting transfers between devices  4.84 us (5%)
  other arithmetic  1.96 us (2%)
  local copies, waits for them, and re-layouts  1.09 us (1%)
    all_to_all x1, blocking collectives, on_device(): lax.all_to_all(message, 'dom', split_axis=0, concat_axis=0, tiled=True)  29.6 us
    all_to_all x1, blocking collectives, on_device(): lax.all_to_all(answer.reshape(peers, capacity, width), 'dom', split_axis=...  18.9 us
    dot_general x3, matrix products, adjoint(): lax.dot_general(tile, piece, (((0,), (0,)), ((), ())), preferred_element_...  12.9 us
    all_to_all x1, blocking collectives, on_device(): lax.all_to_all(jnp.broadcast_to(partial, (replicas, shard, width)), 'rep'...  11.9 us
    all_to_all x1, blocking collectives, on_device(): lax.all_to_all(jnp.broadcast_to(fresh, (replicas, quarter, width)), 'rep'...  11.7 us
    all_to_all x1, waiting for transfers between devices, on_device(): lax.all_to_all(term.reshape(replicas, quarter, width), 'rep', split_axis=...  5.84 us
    all_to_all x1, starting transfers between devices, on_device(): lax.all_to_all(term.reshape(replicas, quarter, width), 'rep', split_axis=...  4.84 us
  transfers between devices with their start and end apart: 1, of which 1 were waited for; matrix products, arithmetic and copies ran while one was open for 1% of the time, Pallas kernels for 0%

commit v1 on v0

--- a/solution.py
+++ b/solution.py
@@ -1,27 +1,101 @@
 import jax
 import jax.numpy as jnp
 from jax import lax
+from jax.experimental import pallas as pl
+from jax.experimental.pallas import tpu as pltpu
 from jax.sharding import PartitionSpec as P
 
 LAYERS = 3
 LEARN_RATE = 0.5
 LANES = 128
-SPARE = 8
-
-
-def adjoint(tile, piece):
-    return lax.dot_general(
-        tile, piece, (((0,), (0,)), ((), ())), preferred_element_type=jnp.float32
-    )
-
-
-def propagate(adjacency, start):
-    state = start
-    total = state.astype(jnp.float32)
-    for layer in range(LAYERS):
-        state = adjoint(adjacency, state).astype(jnp.bfloat16)
-        total = total + state.astype(jnp.float32)
-    return total / jnp.float32(LAYERS + 1)
+BLOCKS = 8
+
+
+def propagate_kernel(me_ref, tile_hbm, grad_ref, *refs):
+    outs = refs[:-4]
+    tile, state, total, arrived = refs[-4:]
+    blocks = arrived.shape[0]
+    replicas = len(outs)
+    rows = tile.shape[0]
+    depth = rows // blocks
+    quarter = rows // replicas
+    copies = []
+    for block in range(blocks):
+        part = pl.ds(block * depth, depth)
+        copies.append(
+            pltpu.make_async_copy(tile_hbm.at[part], tile.at[part], arrived.at[block])
+        )
+        copies[-1].start()
+    first = grad_ref[...].T
+    state[...] = first
+    for block in range(blocks):
+        copies[block].wait()
+        part = slice(block * depth, (block + 1) * depth)
+        product = jnp.dot(state[:, part], tile[part, :], preferred_element_type=jnp.float32)
+        if block == 0:
+            total[...] = product
+        else:
+            total[...] += product
+    second = total[...].astype(jnp.bfloat16)
+    total[...] = first.astype(jnp.float32) + second.astype(jnp.float32)
+    state[...] = second
+    third = [
+        jnp.dot(
+            state[...],
+            tile[:, part * quarter : (part + 1) * quarter],
+            preferred_element_type=jnp.float32,
+        ).astype(jnp.bfloat16)
+        for part in range(replicas)
+    ]
+    for part in range(replicas):
+        lanes = slice(part * quarter, (part + 1) * quarter)
+        state[:, lanes] = third[part]
+    for step in range(replicas):
+        start = lax.rem(me_ref[0] + step, replicas) * quarter
+        lanes = pl.ds(pl.multiple_of(start, quarter), quarter)
+        last = jnp.dot(state[...], tile[:, lanes], preferred_element_type=jnp.float32)
+        term = (
+            total[:, lanes]
+            + state[:, lanes].astype(jnp.float32)
+            + last.astype(jnp.bfloat16).astype(jnp.float32)
+        ) / jnp.float32(LAYERS + 1)
+        outs[step][...] = term.astype(jnp.bfloat16).T
+
+
+def propagate(adjacency, start, me, replicas):
+    rows, width = start.shape
+    whole = pl.BlockSpec(memory_space=pltpu.VMEM)
+    piece = jax.ShapeDtypeStruct((rows // replicas, width), jnp.bfloat16)
+    return pl.pallas_call(
+        propagate_kernel,
+        out_shape=[piece] * replicas,
+        in_specs=[
+            pl.BlockSpec(memory_space=pltpu.SMEM),
+            pl.BlockSpec(memory_space=pltpu.HBM),
+            whole,
+        ],
+        out_specs=[whole] * replicas,
+        scratch_shapes=[
+            pltpu.VMEM((rows, rows), jnp.bfloat16),
+            pltpu.VMEM((width, rows), jnp.bfloat16),
+            pltpu.VMEM((width, rows), jnp.float32),
+            pltpu.SemaphoreType.DMA((BLOCKS,)),
+        ],
+        compiler_params=pltpu.CompilerParams(vmem_limit_bytes=32 * 1024 * 1024),
+        cost_estimate=pl.CostEstimate(
+            flops=2 * LAYERS * rows * rows * width,
+            bytes_accessed=2 * rows * rows + 4 * rows * width,
+            transcendentals=0,
+        ),
+    )(me, adjacency, start)
+
+
+def send(piece, step, replicas):
+    return lax.ppermute(piece, "rep", [(i, (i + step) % replicas) for i in range(replicas)])
+
+
+def send_order(replicas):
+    return sorted(range(1, replicas), key=lambda step: -min(step, replicas - step))
 
 
 def one_hot(values, count, axis):
@@ -68,36 +142,37 @@
     owner_hot, ranks, dispatch = plan(owners, peers, capacity)
     slot_row = slot_rows(owner_hot, ranks, slots, capacity)
 
-    term = propagate(adjacency, grad_out[0]).astype(jnp.bfloat16)
-    terms = lax.all_to_all(
-        term.reshape(replicas, quarter, width), "rep", split_axis=0, concat_axis=0, tiled=True
-    )
-    row_grad = jnp.sum(terms.astype(jnp.float32), axis=0).astype(jnp.bfloat16)
+    me = lax.axis_index("rep")
+    terms = propagate(adjacency, grad_out[0], jnp.full((1,), me, jnp.int32), replicas)
+    got_terms = [send(terms[step], step, replicas) for step in send_order(replicas)]
+    row_grad = terms[0].astype(jnp.float32)
+    for piece in got_terms:
+        row_grad = row_grad + piece.astype(jnp.float32)
+    row_grad = row_grad.astype(jnp.bfloat16)
 
     outgoing = lax.dot_general(
         dispatch, row_grad, (((0,), (0,)), ((), ())), preferred_element_type=jnp.float32
     ).astype(jnp.bfloat16)
     message = jnp.concatenate(
         [
-            outgoing.reshape(peers, capacity, width),
-            jnp.broadcast_to(slot_row[:, None, :], (peers, SPARE, LANES)),
+            outgoing.reshape(peers, capacity // 2, 2, width),
+            jnp.broadcast_to(slot_row[:, None, None, :], (peers, 1, 2, LANES)),
         ],
         axis=1,
     )
     incoming = lax.all_to_all(message, "dom", split_axis=0, concat_axis=0, tiled=True)
-    got = incoming[:, capacity, : 2 * capacity].astype(jnp.int32)
+    got = incoming[:, capacity // 2, 0, : 2 * capacity].astype(jnp.int32)
     got_slots = (got[:, :capacity] * 16 + got[:, capacity:]).reshape(-1)
     receiver = one_hot(got_slots, shard, 0)
     partial = jnp.dot(
         receiver,
-        incoming[:, :capacity].reshape(peers * capacity, width),
+        incoming[:, : capacity // 2].reshape(peers * capacity, width),
         preferred_element_type=jnp.float32,
     ).astype(jnp.bfloat16)
-    partials = lax.all_to_all(
-        jnp.broadcast_to(partial, (replicas, shard, width)),
-        "rep", split_axis=0, concat_axis=0, tiled=True,
-    )
-    table_grad = jnp.sum(partials.astype(jnp.float32), axis=0)
+    opposite, *beside = [send(partial, step, replicas) for step in send_order(replicas)]
+    table_grad = (partial.astype(jnp.float32) + opposite.astype(jnp.float32)) + (
+        beside[0].astype(jnp.float32) + beside[1].astype(jnp.float32)
+    )
     new_accumulators = row_accumulators + jnp.mean(table_grad * table_grad, axis=1)
     new_table = table_rows - LEARN_RATE * table_grad / jnp.sqrt(new_accumulators)[:, None]
 
@@ -111,10 +186,11 @@
     fresh = jnp.dot(
         dispatch, returned.reshape(peers * capacity, width), preferred_element_type=jnp.float32
     ).astype(jnp.bfloat16)
-    fresh_rows = lax.all_to_all(
-        jnp.broadcast_to(fresh, (replicas, quarter, width)),
-        "rep", split_axis=0, concat_axis=0, tiled=True,
-    ).reshape(rows, width)
+    fresh_rows = jnp.zeros((rows, width), jnp.bfloat16)
+    for step in [*send_order(replicas), 0]:
+        piece = send(fresh, step, replicas) if step else fresh
+        source = lax.rem(me + replicas - step, replicas) * quarter
+        fresh_rows = lax.dynamic_update_slice(fresh_rows, piece, (source, 0))
     return (new_table, new_accumulators, fresh_rows)
 
 

time: 103 us -> 91.2 us (0.89)
  blocking collectives: 72.1 us -> 46.4 us
  matrix products: 16.1 us -> 3.07 us
  waiting for transfers between devices: 5.84 us -> 15.9 us
  starting transfers between devices: 4.84 us -> 11 us
  local copies, waits for them, and re-layouts: 1.09 us -> 6.63 us
  Pallas kernels: 0 us -> 5 us
    all_to_all x2 -> x0, blocking collectives: 23.6 us -> none  [the longest x1 11.9 us: on_device(): lax.all_to_all(jnp.broadcast_to(partial, (replicas, shard, width)), 'rep'...]
    ppermute x0 -> x9, waiting for transfers between devices: none -> 15.9 us  [send(): lax.ppermute(piece, 'rep', [(i, (i + step) % replicas) for i in range(rep...]
    dot_general x4 -> x1, matrix products: 13.4 us -> 0.56 us  [on_device(): jnp.dot(receiver, incoming[:, :capacity // 2].reshape(peers * capacity, w...]
    ppermute x0 -> x9, starting transfers between devices: none -> 11 us  [send(): lax.ppermute(piece, 'rep', [(i, (i + step) % replicas) for i in range(rep...]
    all_to_all x1 -> x0, waiting for transfers between devices: 5.84 us -> none  [on_device(): lax.all_to_all(term.reshape(replicas, quarter, width), 'rep', split_axis=...]
    unnamed x13 -> x14, local copies, waits for them, and re-layouts: 0.83 us -> 6.18 us
    pallas_call x0 -> x1, Pallas kernels: none -> 5 us  [propagate(): pl.pallas_call(propagate_kernel, out_shape=[piece] * replicas, in_specs=[...]
    all_to_all x1 -> x0, starting transfers between devices: 4.84 us -> none  [on_device(): lax.all_to_all(term.reshape(replicas, quarter, width), 'rep', split_axis=...]
  transfers between devices with their start and end apart: 1 -> 9, of which waited for: 1 -> 5; matrix products, arithmetic and copies ran while one was open for 1% -> 3% of each run, Pallas kernels for 0% -> 0%
where the time goes in v1:
time: 91.2 us; the launch traced here: 91 us
  blocking collectives  46.4 us (51%)
  waiting for transfers between devices  15.9 us (17%)
  starting transfers between devices  11 us (12%)
  local copies, waits for them, and re-layouts  6.63 us (7%)
  Pallas kernels  5 us (5%)
  matrix products  3.07 us (3%)
  other arithmetic  2.06 us (2%)
    all_to_all x1, blocking collectives, on_device(): lax.all_to_all(message, 'dom', split_axis=0, concat_axis=0, tiled=True)  27.9 us
    all_to_all x1, blocking collectives, on_device(): lax.all_to_all(answer.reshape(peers, capacity, width), 'dom', split_axis=...  18.5 us
    ppermute x9, waiting for transfers between devices, send(): lax.ppermute(piece, 'rep', [(i, (i + step) % replicas) for i in range(rep...  15.9 us
    ppermute x9, starting transfers between devices, send(): lax.ppermute(piece, 'rep', [(i, (i + step) % replicas) for i in range(rep...  11 us
    unnamed x14, local copies, waits for them, and re-layouts  6.18 us
    pallas_call x1, Pallas kernels, propagate(): pl.pallas_call(propagate_kernel, out_shape=[piece] * replicas, in_specs=[...  5 us
  transfers between devices with their start and end apart: 9, of which 5 were waited for; matrix products, arithmetic and copies ran while one was open for 3% of the time, Pallas kernels for 0%

profile of v1, /device:TPU:1, one launch (start us, length us, event | category | flops | bytes accessed | tf_op | source)
XLA Modules:
  0.0 91.0 jit_solution(15190930112387303877)
XLA Ops:
  0.6 3.4 %copy-done = bf16[2048,2048]{1,0:T(8,128)(2,1)S(1)} copy-done((bf16[2048,2048]{1,0:T(8,128)(2,1)S(1)}, bf16[2048,2048]{1,0:T(8,128)(2,1)}, u32[]{:S(2)}) %copy-start) | copy-done | bytes 8388632
  4.0 1.0 %copy-done.1 = bf16[1,2048,128]{2,1,0:T(8,128)(2,1)S(1)} copy-done((bf16[1,2048,128]{2,1,0:T(8,128)(2,1)S(1)}, bf16[1,2048,128]{2,1,0:T(8,128)(2,1)}, u32[]{:S(2)}) %copy-start.1) | copy-done | bytes 524312
  5.1 5.0 %shard_map.85 = (bf16[512,128]{1,0:T(8,128)(2,1)S(1)}, bf16[512,128]{1,0:T(8,128)(2,1)S(1)}, bf16[512,128]{1,0:T(8,128)(2,1)S(1)}, bf16[512,128]{1,0:T(8,128)(2,1)S(1)}) custom-call(s32[1]{0:T(128)} %bitcast.3.me_ref, bf16[2048,2048]{1,0:T(8,128)(2,1)S(1)} %copy-done, bf16[2048,128]{1,0:T(8,128)(2,1)S(1)} %bitcast.12), custom_call_target="tpu_custom_call" | custom-call | flops 3221225472 | bytes 9437184 | tf_op jit(solution)/shard_map/pallas_call | solution.py:69
  10.1 3.4 %collective-permute-start.2 = (bf16[512,128]{1,0:T(8,128)(2,1)S(1)}, bf16[512,128]{1,0:T(8,128)(2,1)S(1)}, u32[]{:S(2)}, u32[]{:S(2)}) collective-permute-start(bf16[512,128]{1,0:T(8,128)(2,1)S(1)} %get-tuple-element.10), channel_id=1, source_target_pairs={{0,3},{1,0},{2,1},{3,2},{4,7},{5,4},{6,5},{7,6},{8,11},{9,8},{10,9... | collective-permute-start | bytes 393224 | tf_op jit(solution)/shard_map/ppermute | solution.py:94
  13.5 1.7 %collective-permute-start = (bf16[512,128]{1,0:T(8,128)(2,1)S(1)}, bf16[512,128]{1,0:T(8,128)(2,1)S(1)}, u32[]{:S(2)}, u32[]{:S(2)}) collective-permute-start(bf16[512,128]{1,0:T(8,128)(2,1)S(1)} %get-tuple-element.8), channel_id=1, source_target_pairs={{0,2},{1,3},{2,0},{3,1},{4,6},{5,7},{6,4},{7,5},{8,10},{9,11},{10,... | collective-permute-start | bytes 393224 | tf_op jit(solution)/shard_map/ppermute | solution.py:94
  15.2 0.8 add_select_fusion.1
  16.0 0.3 fusion.8
  16.3 0.4 convolution_convert_fusion.1
  16.7 3.9 %collective-permute-done.1 = bf16[512,128]{1,0:T(8,128)(2,1)S(1)} collective-permute-done((bf16[512,128]{1,0:T(8,128)(2,1)S(1)}, bf16[512,128]{1,0:T(8,128)(2,1)S(1)}, u32[]{:S(2)}, u32[]{:S(2)}) %collective-permute-start.1) | collective-permute-done | bytes 131104 | tf_op jit(solution)/shard_map/ppermute | solution.py:94
  20.6 0.8 fusion.4
  21.5 0.4 pad_maximum_fusion
  21.9 27.9 %all_to_all.10 = bf16[64,9,2,128]{3,2,1,0:T(2,128)(2,1)S(1)} all-to-all(bf16[64,9,2,128]{3,2,1,0:T(2,128)(2,1)S(1)} %pad_maximum_fusion), channel_id=1, replica_groups=mesh['dom'=64,'rep'=4] {'dom'}, dimensions={0} | all-to-all | bytes 589824 | tf_op jit(solution)/shard_map/all_to_all | solution.py:163
  50.0 0.2 slice.19
  50.2 0.6 fusion.6
  50.8 0.5 collective-permute-start.5
  51.3 1.0 %collective-permute-start.4 = (bf16[512,128]{0,1:T(8,128)(2,1)S(1)}, bf16[512,128]{0,1:T(8,128)(2,1)S(1)}, u32[]{:S(2)}, u32[]{:S(2)}) collective-permute-start(bf16[512,128]{0,1:T(8,128)(2,1)S(1)} %fusion.6), channel_id=1, source_target_pairs={{0,1},{1,2},{2,3},{3,0},{4,5},{5,6},{6,7},{7,4},{8,9},{9,10},{10,1... | collective-permute-start | bytes 393224 | tf_op jit(solution)/shard_map/ppermute | solution.py:94
  52.3 0.3 collective-permute-start.3
  52.6 0.1 copy.14
  52.8 3.1 %collective-permute-done.5 = bf16[512,128]{0,1:T(8,128)(2,1)S(1)} collective-permute-done((bf16[512,128]{0,1:T(8,128)(2,1)S(1)}, bf16[512,128]{0,1:T(8,128)(2,1)S(1)}, u32[]{:S(2)}, u32[]{:S(2)}) %collective-permute-start.5) | collective-permute-done | bytes 131104 | tf_op jit(solution)/shard_map/ppermute | solution.py:94
  55.8 4.1 %collective-permute-done.4 = bf16[512,128]{0,1:T(8,128)(2,1)S(1)} collective-permute-done((bf16[512,128]{0,1:T(8,128)(2,1)S(1)}, bf16[512,128]{0,1:T(8,128)(2,1)S(1)}, u32[]{:S(2)}, u32[]{:S(2)}) %collective-permute-start.4) | collective-permute-done | bytes 131104 | tf_op jit(solution)/shard_map/ppermute | solution.py:94
  60.0 0.1 multiply_reduce_fusion
  60.1 0.6 fusion.27
  60.6 0.1 divide_subtract_fusion
  60.7 0.5 convolution_convert_fusion
  61.2 18.5 %all_to_all.11 = bf16[64,16,128]{2,1,0:T(8,128)(2,1)S(1)} all-to-all(bf16[64,16,128]{2,1,0:T(8,128)(2,1)S(1)} %bitcast.17), channel_id=1, replica_groups=mesh['dom'=64,'rep'=4] {'dom'}, dimensions={0} | all-to-all | bytes 524288 | tf_op jit(solution)/shard_map/all_to_all | solution.py:183
  79.7 0.5 fusion.5
  80.3 1.4 %collective-permute-start.6 = (bf16[512,128]{1,0:T(8,128)(2,1)S(1)}, bf16[512,128]{1,0:T(8,128)(2,1)S(1)}, u32[]{:S(2)}, u32[]{:S(2)}) collective-permute-start(bf16[512,128]{1,0:T(8,128)(2,1)S(1)} %fusion.5), channel_id=1, source_target_pairs={{0,2},{1,3},{2,0},{3,1},{4,6},{5,7},{6,4},{7,5},{8,10},{9,11},{10,... | collective-permute-start | bytes 393224 | tf_op jit(solution)/shard_map/ppermute | solution.py:94
  81.7 0.8 copy.15
  82.5 2.7 %collective-permute-start.8 = (bf16[512,128]{1,0:T(8,128)(2,1)S(1)}, bf16[512,128]{1,0:T(8,128)(2,1)S(1)}, u32[]{:S(2)}, u32[]{:S(2)}) collective-permute-start(bf16[512,128]{1,0:T(8,128)(2,1)S(1)} %fusion.5), channel_id=1, source_target_pairs={{0,3},{1,0},{2,1},{3,2},{4,7},{5,4},{6,5},{7,6},{8,11},{9,8},{10,9... | collective-permute-start | bytes 393224 | tf_op jit(solution)/shard_map/ppermute | solution.py:94
  85.2 1.5 %collective-permute-done.6 = bf16[512,128]{1,0:T(8,128)(2,1)S(1)} collective-permute-done((bf16[512,128]{1,0:T(8,128)(2,1)S(1)}, bf16[512,128]{1,0:T(8,128)(2,1)S(1)}, u32[]{:S(2)}, u32[]{:S(2)}) %collective-permute-start.6) | collective-permute-done | bytes 131104 | tf_op jit(solution)/shard_map/ppermute | solution.py:94
  86.8 3.3 %collective-permute-done.7 = bf16[512,128]{1,0:T(8,128)(2,1)S(1)} collective-permute-done((bf16[512,128]{1,0:T(8,128)(2,1)S(1)}, bf16[512,128]{1,0:T(8,128)(2,1)S(1)}, u32[]{:S(2)}, u32[]{:S(2)}) %collective-permute-start.7) | collective-permute-done | bytes 131104 | tf_op jit(solution)/shard_map/ppermute | solution.py:94
  90.2 0.8 copy-done.2
  (29 shorter events, 0.4 us)
Async XLA Ops:
  0.6 3.4 %copy-start = (bf16[2048,2048]{1,0:T(8,128)(2,1)S(1)}, bf16[2048,2048]{1,0:T(8,128)(2,1)}, u32[]{:S(2)}) copy-start(bf16[2048,2048]{1,0:T(8,128)(2,1)} %tile_hbm.1) | copy-start | bytes 25165828
  4.0 1.0 %copy-start.1 = (bf16[1,2048,128]{2,1,0:T(8,128)(2,1)S(1)}, bf16[1,2048,128]{2,1,0:T(8,128)(2,1)}, u32[]{:S(2)}) copy-start(bf16[1,2048,128]{2,1,0:T(8,128)(2,1)} %param.7) | copy-start | bytes 1572868
  5.1 10.9 %copy-start.4 = (s32[2048,1]{0,1:T(1,128)S(1)}, s32[2048,1]{0,1:T(1,128)}, u32[]{:S(2)}) copy-start(s32[2048,1]{0,1:T(1,128)} %param.8) | copy-start | bytes 24580
  10.1 6.6 %collective-permute-start.2 = (bf16[512,128]{1,0:T(8,128)(2,1)S(1)}, bf16[512,128]{1,0:T(8,128)(2,1)S(1)}, u32[]{:S(2)}, u32[]{:S(2)}) collective-permute-start(bf16[512,128]{1,0:T(8,128)(2,1)S(1)} %get-tuple-element.10), channel_id=1, source_target_pairs={{0,3},{1,0},{2,1},{3,2},{4,7},{5,4},{6,5},{7,6},{8,11},{9,8},{10,9... | collective-permute-start | bytes 393224 | tf_op jit(solution)/shard_map/ppermute | solution.py:94
  13.5 7.2 %collective-permute-start.1 = (bf16[512,128]{1,0:T(8,128)(2,1)S(1)}, bf16[512,128]{1,0:T(8,128)(2,1)S(1)}, u32[]{:S(2)}, u32[]{:S(2)}) collective-permute-start(bf16[512,128]{1,0:T(8,128)(2,1)S(1)} %get-tuple-element.9), channel_id=1, source_target_pairs={{0,1},{1,2},{2,3},{3,0},{4,5},{5,6},{6,7},{7,4},{8,9},{9,10},{10,1... | collective-permute-start | bytes 393224 | tf_op jit(solution)/shard_map/ppermute | solution.py:94
  13.5 7.2 %collective-permute-start = (bf16[512,128]{1,0:T(8,128)(2,1)S(1)}, bf16[512,128]{1,0:T(8,128)(2,1)S(1)}, u32[]{:S(2)}, u32[]{:S(2)}) collective-permute-start(bf16[512,128]{1,0:T(8,128)(2,1)S(1)} %get-tuple-element.8), channel_id=1, source_target_pairs={{0,2},{1,3},{2,0},{3,1},{4,6},{5,7},{6,4},{7,5},{8,10},{9,11},{10,... | collective-permute-start | bytes 393224 | tf_op jit(solution)/shard_map/ppermute | solution.py:94
  20.6 32.0 %copy-start.3 = (f32[512,128]{1,0:T(8,128)S(1)}, f32[512,128]{1,0:T(8,128)}, u32[]{:S(2)}) copy-start(f32[512,128]{1,0:T(8,128)} %param.10) | copy-start | bytes 786436
  21.5 38.6 %copy-start.5 = (f32[512]{0:T(512)S(1)}, f32[512]{0:T(512)}, u32[]{:S(2)}) copy-start(f32[512]{0:T(512)} %param.11) | copy-start | bytes 6148
  50.8 5.0 %collective-permute-start.5 = (bf16[512,128]{0,1:T(8,128)(2,1)S(1)}, bf16[512,128]{0,1:T(8,128)(2,1)S(1)}, u32[]{:S(2)}, u32[]{:S(2)}) collective-permute-start(bf16[512,128]{0,1:T(8,128)(2,1)S(1)} %fusion.6), channel_id=1, source_target_pairs={{0,3},{1,0},{2,1},{3,2},{4,7},{5,4},{6,5},{7,6},{8,11},{9,8},{10,9... | collective-permute-start | bytes 393224 | tf_op jit(solution)/shard_map/ppermute | solution.py:94
  51.3 8.7 %collective-permute-start.4 = (bf16[512,128]{0,1:T(8,128)(2,1)S(1)}, bf16[512,128]{0,1:T(8,128)(2,1)S(1)}, u32[]{:S(2)}, u32[]{:S(2)}) collective-permute-start(bf16[512,128]{0,1:T(8,128)(2,1)S(1)} %fusion.6), channel_id=1, source_target_pairs={{0,1},{1,2},{2,3},{3,0},{4,5},{5,6},{6,7},{7,4},{8,9},{9,10},{10,1... | collective-permute-start | bytes 393224 | tf_op jit(solution)/shard_map/ppermute | solution.py:94
  52.3 7.6 %collective-permute-start.3 = (bf16[512,128]{0,1:T(8,128)(2,1)S(1)}, bf16[512,128]{0,1:T(8,128)(2,1)S(1)}, u32[]{:S(2)}, u32[]{:S(2)}) collective-permute-start(bf16[512,128]{0,1:T(8,128)(2,1)S(1)} %fusion.6), channel_id=1, source_target_pairs={{0,2},{1,3},{2,0},{3,1},{4,6},{5,7},{6,4},{7,5},{8,10},{9,11},{10,... | collective-permute-start | bytes 393224 | tf_op jit(solution)/shard_map/ppermute | solution.py:94
  80.3 6.4 %collective-permute-start.6 = (bf16[512,128]{1,0:T(8,128)(2,1)S(1)}, bf16[512,128]{1,0:T(8,128)(2,1)S(1)}, u32[]{:S(2)}, u32[]{:S(2)}) collective-permute-start(bf16[512,128]{1,0:T(8,128)(2,1)S(1)} %fusion.5), channel_id=1, source_target_pairs={{0,2},{1,3},{2,0},{3,1},{4,6},{5,7},{6,4},{7,5},{8,10},{9,11},{10,... | collective-permute-start | bytes 393224 | tf_op jit(solution)/shard_map/ppermute | solution.py:94
  81.7 8.4 %collective-permute-start.7 = (bf16[512,128]{1,0:T(8,128)(2,1)S(1)}, bf16[512,128]{1,0:T(8,128)(2,1)S(1)}, u32[]{:S(2)}, u32[]{:S(2)}) collective-permute-start(bf16[512,128]{1,0:T(8,128)(2,1)S(1)} %fusion.5), channel_id=1, source_target_pairs={{0,1},{1,2},{2,3},{3,0},{4,5},{5,6},{6,7},{7,4},{8,9},{9,10},{10,1... | collective-permute-start | bytes 393224 | tf_op jit(solution)/shard_map/ppermute | solution.py:94
  82.5 7.6 %collective-permute-start.8 = (bf16[512,128]{1,0:T(8,128)(2,1)S(1)}, bf16[512,128]{1,0:T(8,128)(2,1)S(1)}, u32[]{:S(2)}, u32[]{:S(2)}) collective-permute-start(bf16[512,128]{1,0:T(8,128)(2,1)S(1)} %fusion.5), channel_id=1, source_target_pairs={{0,3},{1,0},{2,1},{3,2},{4,7},{5,4},{6,5},{7,6},{8,11},{9,8},{10,9... | collective-permute-start | bytes 393224 | tf_op jit(solution)/shard_map/ppermute | solution.py:94
  90.2 0.8 copy-start.2

commit v2 on v0

v2 whole, which is shorter than its diff:
```python
import jax
import jax.numpy as jnp
from jax import lax
from jax.experimental import pallas as pl
from jax.experimental.pallas import tpu as pltpu
from jax.sharding import PartitionSpec as P

LAYERS = 3
LEARN_RATE = 0.5
LANES = 128
BLOCKS = 8
RADIX_BITS = 4
MEBI = 1024 * 1024

VMEM = pl.BlockSpec(memory_space=pltpu.VMEM)
SMEM = pl.BlockSpec(memory_space=pltpu.SMEM)
HBM = pl.BlockSpec(memory_space=pltpu.HBM)
BF16 = jnp.bfloat16
F32 = jnp.float32


def ids(shape, axis):
    return lax.broadcasted_iota(jnp.int32, shape, axis)


def product(left, right):
    return jnp.dot(left, right, preferred_element_type=F32)


def shaped(shape, dtype):
    return jax.ShapeDtypeStruct(shape, dtype)


def call(kernel, out_shape, in_specs, out_specs, scratch=(), mebi=16, flops=0, moved=0):
    return pl.pallas_call(
        kernel,
        out_shape=out_shape,
        in_specs=in_specs,
        out_specs=out_specs,
        scratch_shapes=list(scratch),
        compiler_params=pltpu.CompilerParams(vmem_limit_bytes=mebi * MEBI),
        cost_estimate=pl.CostEstimate(flops=flops, bytes_accessed=moved, transcendentals=0),
    )


def propagate_kernel(me_ref, tile_hbm, grad_hbm, *refs):
    outs = refs[:-6]
    tile, grad, state, total, arrived, grad_arrived = refs[-6:]
    blocks = arrived.shape[0]
    replicas = len(outs)
    rows = tile.shape[0]
    depth = rows // blocks
    quarter = rows // replicas
    grad_copy = pltpu.make_async_copy(grad_hbm, grad, grad_arrived)
    grad_copy.start()
    copies = []
    for block in range(blocks):
        part = pl.ds(block * depth, depth)
        copies.append(
            pltpu.make_async_copy(tile_hbm.at[part], tile.at[part], arrived.at[block])
        )
        copies[-1].start()
    grad_copy.wait()
    first = grad[...].T
    state[...] = first
    for block in range(blocks):
        copies[block].wait()
        part = slice(block * depth, (block + 1) * depth)
        added = product(state[:, part], tile[part, :])
        if block == 0:
            total[...] = added
        else:
            total[...] += added
    second = total[...].astype(BF16)
    total[...] = first.astype(F32) + second.astype(F32)
    state[...] = second
    third = [
        product(state[...], tile[:, part * quarter : (part + 1) * quarter]).astype(BF16)
        for part in range(replicas)
    ]
    for part in range(replicas):
        state[:, part * quarter : (part + 1) * quarter] = third[part]
    for step in range(replicas):
        start = lax.rem(me_ref[0] + step, replicas) * quarter
        lanes = pl.ds(pl.multiple_of(start, quarter), quarter)
        last = product(state[...], tile[:, lanes]).astype(BF16)
        term = total[:, lanes] + state[:, lanes].astype(F32) + last.astype(F32)
        outs[step][...] = (term / F32(LAYERS + 1)).astype(BF16).T


def propagate(me, adjacency, start, replicas):
    rows, width = start.shape
    piece = shaped((rows // replicas, width), BF16)
    return call(
        propagate_kernel,
        [piece] * replicas,
        [SMEM, HBM, HBM],
        [VMEM] * replicas,
        scratch=[
            pltpu.VMEM((rows, rows), BF16),
            pltpu.VMEM((rows, width), BF16),
            pltpu.VMEM((width, rows), BF16),
            pltpu.VMEM((width, rows), F32),
            pltpu.SemaphoreType.DMA((BLOCKS,)),
            pltpu.SemaphoreType.DMA,
        ],
        mebi=60,
        flops=2 * LAYERS * rows * rows * width,
        moved=2 * rows * rows + 4 * rows * width,
    )(me, adjacency, start)


def plan_kernel(capacity, me_ref, owner_ref, slot_ref, pack_ref, unpack_ref, slots_ref):
    places, quarter = pack_ref.shape
    peers = places // capacity
    lanes = pl.ds(pl.multiple_of(me_ref[0] * quarter, quarter), quarter)
    owner = owner_ref[:, lanes]
    slot = slot_ref[:, lanes]
    hot = ids((peers, quarter), 0) == owner
    owner_hot = jnp.where(hot, 1.0, 0.0).astype(BF16)
    square = (quarter, quarter)
    upper = jnp.where(ids(square, 0) <= ids(square, 1), 1.0, 0.0).astype(BF16)
    running = product(owner_hot, upper)
    rank = jnp.sum(jnp.where(hot, running, 0.0), axis=0, keepdims=True).astype(jnp.int32) - 1
    place = owner * capacity + rank
    pack_ref[...] = jnp.where(ids(pack_ref.shape, 0) == place, 1.0, 0.0).astype(BF16)
    column = jnp.broadcast_to(place.astype(F32), (LANES, quarter)).T.astype(jnp.int32)
    for part in range(places // LANES):
        here = column == ids(column.shape, 1) + part * LANES
        unpack_ref[:, part * LANES : (part + 1) * LANES] = jnp.where(here, 1.0, 0.0).astype(BF16)
    index = ids((LANES, quarter), 0)
    digit = jnp.where(index < capacity, slot >> RADIX_BITS, slot & ((1 << RADIX_BITS) - 1))
    wanted = (index < 2 * capacity) & (lax.rem(index, capacity) == rank)
    spread = jnp.where(wanted, digit, 0).astype(F32).astype(BF16)
    lists = lax.dot_general(
        owner_hot, spread, (((1,), (1,)), ((), ())), preferred_element_type=F32
    )
    slots_ref[...] = lists.astype(BF16)


def plan(me, row_owner, table_slot, quarter, peers, capacity):
    rows = table_slot.shape[0]
    places = peers * capacity

    def kernel(*refs):
        plan_kernel(capacity, *refs)

    return call(
        kernel,
        [
            shaped((places, quarter), BF16),
            shaped((quarter, places), BF16),
            shaped((peers, LANES), BF16),
        ],
        [SMEM, VMEM, VMEM],
        [VMEM] * 3,
        flops=2 * quarter * quarter * peers,
        moved=4 * places * quarter,
    )(me, row_owner.reshape(1, rows), table_slot.reshape(1, rows))


def pack_kernel(pack_ref, slots_ref, *refs):
    *terms, out_ref = refs
    row_grad = terms[0][...].astype(F32)
    for term in terms[1:]:
        row_grad = row_grad + term[...].astype(F32)
    peers, pairs = out_ref.shape[:2]
    packed = product(pack_ref[...], row_grad.astype(BF16)).astype(BF16)
    out_ref[:, : pairs - 1] = packed.reshape(peers, pairs - 1, 2, LANES)
    lists = slots_ref[...]
    out_ref[:, pairs - 1] = jnp.broadcast_to(lists[:, None, :], (peers, 2, LANES))


def pack(matrix, slots, terms, capacity):
    peers = slots.shape[0]
    return call(
        pack_kernel,
        shaped((peers, capacity // 2 + 1, 2, LANES), BF16),
        [VMEM] * (2 + len(terms)),
        VMEM,
        flops=2 * matrix.shape[0] * matrix.shape[1] * LANES,
        moved=2 * matrix.shape[0] * (matrix.shape[1] + LANES),
    )(matrix, slots, *terms)


def accumulate_kernel(message_ref, partial_ref, receiver_ref):
    shard, places = receiver_ref.shape
    peers, pairs = message_ref.shape[:2]
    capacity = places // peers
    digits = message_ref[:, pairs - 1, 0, :]
    lane, place = ids((LANES, places), 0), ids((LANES, places), 1)
    rank = lax.rem(place, capacity)
    weight = jnp.where(
        lane == rank, float(1 << RADIX_BITS), jnp.where(lane == rank + capacity, 1.0, 0.0)
    ).astype(BF16)
    lists = product(digits, weight)
    mine = ids((peers, places), 0) == ids((peers, places), 1) // capacity
    slot = jnp.sum(jnp.where(mine, lists, 0.0), axis=0, keepdims=True).astype(jnp.int32)
    receiver_ref[...] = jnp.where(ids((shard, places), 0) == slot, 1.0, 0.0).astype(BF16)
    data = message_ref[:, : pairs - 1].reshape(places, LANES)
    partial_ref[...] = product(receiver_ref[...], data).astype(BF16)


def accumulate(message, shard, capacity):
    places = message.shape[0] * capacity
    return call(
        accumulate_kernel,
        [shaped((shard, LANES), BF16), shaped((shard, places), BF16)],
        [VMEM],
        [VMEM] * 2,
        flops=2 * shard * places * LANES,
        moved=2 * places * (shard + LANES),
    )(message)


def update_kernel(
    own_ref, across_ref, left_ref, right_ref, receiver_ref, table_ref, sums_ref,
    new_table_ref, new_sums_ref, answer_ref,
):
    grad = (own_ref[...].astype(F32) + across_ref[...].astype(F32)) + (
        left_ref[...].astype(F32) + right_ref[...].astype(F32)
    )
    mean = jnp.mean((grad * grad).T, axis=0, keepdims=True)
    sums = sums_ref[...] + mean
    new_sums_ref[...] = sums
    scale = jnp.broadcast_to(LEARN_RATE / jnp.sqrt(sums), (LANES, sums.shape[1])).T
    new_table = table_ref[...] - grad * scale
    new_table_ref[...] = new_table
    answer = product(new_table.T.astype(BF16), receiver_ref[...])
    answer_ref[...] = answer.T.astype(BF16)


def update(partials, receiver, table_rows, row_accumulators):
    shard, places = receiver.shape
    new_table, sums, answer = call(
        update_kernel,
        [shaped((shard, LANES), F32), shaped((1, shard), F32), shaped((places, LANES), BF16)],
        [VMEM] * 7,
        [VMEM] * 3,
        flops=2 * shard * places * LANES,
        moved=2 * places * (shard + LANES),
    )(*partials, receiver, table_rows, row_accumulators.reshape(1, shard))
    return new_table, sums.reshape(shard), answer


def unpack_kernel(matrix_ref, returned_ref, out_ref):
    out_ref[...] = product(matrix_ref[...], returned_ref[...]).astype(BF16)


def unpack(matrix, returned):
    quarter, places = matrix.shape
    return call(
        unpack_kernel,
        shaped((quarter, LANES), BF16),
        [VMEM] * 2,
        VMEM,
        flops=2 * quarter * places * LANES,
        moved=2 * places * (quarter + LANES),
    )(matrix, returned)


def place_kernel(steps, replicas, me_ref, *refs):
    pieces = refs[: len(steps)]
    out_hbm, sent = refs[-2:]
    quarter = pieces[0].shape[0]
    copies = []
    for index, step in enumerate(steps):
        source = lax.rem(me_ref[0] + replicas - step, replicas) * quarter
        rows = pl.ds(pl.multiple_of(source, quarter), quarter)
        copies.append(pltpu.make_async_copy(pieces[index], out_hbm.at[rows], sent.at[index]))
        copies[-1].start()
    for copy in copies:
        copy.wait()


def place(me, steps, pieces, replicas, rows, before=None):
    def kernel(*refs):
        place_kernel(steps, replicas, *refs)

    earlier = [] if before is None else [before]
    quarter, width = pieces[0].shape
    return pl.pallas_call(
        kernel,
        out_shape=shaped((rows, width), BF16),
        in_specs=[SMEM] + [VMEM] * len(pieces) + [HBM] * len(earlier),
        out_specs=HBM,
        scratch_shapes=[pltpu.SemaphoreType.DMA((len(pieces),))],
        input_output_aliases={1 + len(pieces): 0} if earlier else {},
        cost_estimate=pl.CostEstimate(
            flops=0, bytes_accessed=4 * quarter * width * len(pieces), transcendentals=0
        ),
    )(me, *pieces, *earlier)


def send(piece, step, replicas):
    return lax.ppermute(piece, "rep", [(i, (i + step) % replicas) for i in range(replicas)])


def send_order(replicas):
    return sorted(range(1, replicas), key=lambda step: -min(step, replicas - step))


def on_device(adjacency, grad_out, row_owner, table_slot, table_rows, row_accumulators):
    peers = lax.axis_size("dom")
    replicas = lax.axis_size("rep")
    rows = adjacency.shape[0]
    width = grad_out.shape[2]
    shard = table_rows.shape[0]
    quarter = rows // replicas
    capacity = max(2, 2 * quarter // peers)
    order = send_order(replicas)
    me = jnp.full((1,), lax.axis_index("rep"), jnp.int32)

    terms = propagate(me, adjacency, grad_out[0], replicas)
    got_terms = [send(terms[step], step, replicas) for step in order]
    later, _ = lax.optimization_barrier((me, terms[0]))
    to_places, from_places, slots = plan(later, row_owner, table_slot, quarter, peers, capacity)
    message = pack(to_places, slots, [terms[0], *got_terms], capacity)

    incoming = lax.all_to_all(message, "dom", split_axis=0, concat_axis=0, tiled=True)
    partial, receiver = accumulate(incoming, shard, capacity)
    partials = [partial] + [send(partial, step, replicas) for step in order]
    new_table, new_accumulators, answer = update(
        partials, receiver, table_rows, row_accumulators
    )

    returned = lax.all_to_all(
        answer.reshape(peers, capacity, width), "dom", split_axis=0, concat_axis=0, tiled=True
    )
    fresh = unpack(from_places, returned.reshape(peers * capacity, width))
    pieces = [send(fresh, step, replicas) for step in order]
    fresh_rows = place(me, [0, *order[:-1]], [fresh, *pieces[:-1]], replicas, rows)
    fresh_rows = place(me, order[-1:], pieces[-1:], replicas, rows, before=fresh_rows)
    return (new_table, new_accumulators, fresh_rows)


def solution(mesh):
    return jax.shard_map(
        on_device,
        mesh=mesh,
        in_specs=(
            P("dom", None),
            P("rep", "dom", None),
            P("dom", None),
            P("dom"),
            P("dom", None),
            P("dom"),
        ),
        out_specs=(P("dom", None), P("dom"), P("dom", None)),
        check_vma=False,
    )
```

time: 103 us -> 94.1 us (0.914)
  blocking collectives: 72.1 us -> 44.3 us
  matrix products: 16.1 us -> 0 us
  Pallas kernels: 0 us -> 15.4 us
  waiting for transfers between devices: 5.84 us -> 17.3 us
  starting transfers between devices: 4.84 us -> 13 us
  other arithmetic: 1.96 us -> 0 us
  local copies, waits for them, and re-layouts: 1.09 us -> 2.85 us
    all_to_all x2 -> x0, blocking collectives: 23.6 us -> none  [the longest x1 11.9 us: on_device(): lax.all_to_all(jnp.broadcast_to(partial, (replicas, shard, width)), 'rep'...]
    ppermute x0 -> x9, waiting for transfers between devices: none -> 17.3 us  [send(): lax.ppermute(piece, 'rep', [(i, (i + step) % replicas) for i in range(rep...]
    dot_general x9 -> x0, matrix products: 16.1 us -> none  [the longest x3 12.9 us: adjoint(): lax.dot_general(tile, piece, (((0,), (0,)), ((), ())), preferred_element_...]
    pallas_call x0 -> x8, Pallas kernels: none -> 15.4 us  [the longest x1 8.35 us: propagate(): call(propagate_kernel, [piece] * replicas, [SMEM, HBM, HBM], [VMEM] * rep...]
    ppermute x0 -> x9, starting transfers between devices: none -> 13 us  [send(): lax.ppermute(piece, 'rep', [(i, (i + step) % replicas) for i in range(rep...]
    all_to_all x1 -> x0, waiting for transfers between devices: 5.84 us -> none  [on_device(): lax.all_to_all(term.reshape(replicas, quarter, width), 'rep', split_axis=...]
    all_to_all x1 -> x0, starting transfers between devices: 4.84 us -> none  [on_device(): lax.all_to_all(term.reshape(replicas, quarter, width), 'rep', split_axis=...]
    all_to_all x1, blocking collectives: 29.6 us -> 25.8 us  [on_device(): lax.all_to_all(message, 'dom', split_axis=0, concat_axis=0, tiled=True)]
  transfers between devices with their start and end apart: 1 -> 9, of which waited for: 1 -> 4; matrix products, arithmetic and copies ran while one was open for 1% -> 0% of each run, Pallas kernels for 0% -> 3%
where the time goes in v2:
time: 94.1 us; the launch traced here: 93.9 us
  blocking collectives  44.3 us (47%)
  waiting for transfers between devices  17.3 us (18%)
  Pallas kernels  15.4 us (16%)
  starting transfers between devices  13 us (14%)
  local copies, waits for them, and re-layouts  2.85 us (3%)
    all_to_all x1, blocking collectives, on_device(): lax.all_to_all(message, 'dom', split_axis=0, concat_axis=0, tiled=True)  25.8 us
    all_to_all x1, blocking collectives, on_device(): lax.all_to_all(answer.reshape(peers, capacity, width), 'dom', split_axis=...  18.5 us
    ppermute x9, waiting for transfers between devices, send(): lax.ppermute(piece, 'rep', [(i, (i + step) % replicas) for i in range(rep...  17.3 us
    ppermute x9, starting transfers between devices, send(): lax.ppermute(piece, 'rep', [(i, (i + step) % replicas) for i in range(rep...  13 us
    pallas_call x1, Pallas kernels, propagate(): call(propagate_kernel, [piece] * replicas, [SMEM, HBM, HBM], [VMEM] * rep...  8.35 us
    pallas_call x2, Pallas kernels, place(): pl.pallas_call(kernel, out_shape=shaped((rows, width), BF16), in_specs=[S...  3.36 us
    unnamed x18, local copies, waits for them, and re-layouts  2.85 us
  transfers between devices with their start and end apart: 9, of which 4 were waited for; matrix products, arithmetic and copies ran while one was open for 0% of the time, Pallas kernels for 3%

profile of v2, /device:TPU:1, one launch (start us, length us, event | category | flops | bytes accessed | tf_op | source)
XLA Modules:
  0.0 93.9 jit_solution(379794203374142477)
XLA Ops:
  0.7 8.4 %shard_map.85 = (bf16[512,128]{1,0:T(8,128)(2,1)}, bf16[512,128]{1,0:T(8,128)(2,1)}, bf16[512,128]{1,0:T(8,128)(2,1)}, bf16[512,128]{1,0:T(8,128)(2,1)}) custom-call(s32[1]{0:T(128)} %bitcast.me_ref.refs_0_, bf16[2048,2048]{1,0:T(8,128)(2,1)} %tile_hbm.1, bf16[2048,128]{1,0:T(8,128)(2,1)} %bitcast.13), custom_call_target="tpu_custom_call" | custom-call | flops 3221225472 | bytes 9437184 | tf_op jit(solution)/shard_map/pallas_call | solution.py:94
  9.0 3.7 %collective-permute-start = (bf16[512,128]{1,0:T(8,128)(2,1)}, bf16[512,128]{1,0:T(8,128)(2,1)S(1)}, u32[]{:S(2)}, u32[]{:S(2)}) collective-permute-start(bf16[512,128]{1,0:T(8,128)(2,1)} %get-tuple-element.20), channel_id=1, source_target_pairs={{0,2},{1,3},{2,0},{3,1},{4,6},{5,7},{6,4},{7,5},{8,10},{9,11},{10,... | collective-permute-start | bytes 393224 | tf_op jit(solution)/shard_map/ppermute | solution.py:296
  12.7 0.3 collective-permute-start.1
  13.0 2.4 %collective-permute-start.2 = (bf16[512,128]{1,0:T(8,128)(2,1)}, bf16[512,128]{1,0:T(8,128)(2,1)S(1)}, u32[]{:S(2)}, u32[]{:S(2)}) collective-permute-start(bf16[512,128]{1,0:T(8,128)(2,1)} %get-tuple-element.22), channel_id=1, source_target_pairs={{0,3},{1,0},{2,1},{3,2},{4,7},{5,4},{6,5},{7,6},{8,11},{9,8},{10,9... | collective-permute-start | bytes 393224 | tf_op jit(solution)/shard_map/ppermute | solution.py:296
  15.4 1.0 %shard_map.86 = (bf16[1024,512]{1,0:T(8,128)(2,1)S(1)}, bf16[512,1024]{1,0:T(8,128)(2,1)S(1)}, bf16[64,128]{1,0:T(8,128)(2,1)S(1)}) custom-call(s32[1]{0:T(128)} %bitcast.me_ref.refs_0_, s32[1,2048]{1,0:T(1,128)S(1)} %bitcast.11, s32[1,2048]{1,0:T(1,128)S(1)} %bitcast.12), custom_call_target="tpu_custom_call" | custom-call | flops 33554432 | bytes 2097152 | tf_op jit(solution)/shard_map/pallas_call | solution.py:148
  16.4 0.0 collective-permute-done.refs_1_
  16.4 3.7 %collective-permute-done.1.refs_2_ = bf16[512,128]{1,0:T(8,128)(2,1)S(1)} collective-permute-done((bf16[512,128]{1,0:T(8,128)(2,1)}, bf16[512,128]{1,0:T(8,128)(2,1)S(1)}, u32[]{:S(2)}, u32[]{:S(2)}) %collective-permute-start.1) | collective-permute-done | bytes 131104 | tf_op jit(solution)/shard_map/ppermute | solution.py:296
  20.1 0.0 collective-permute-done.2.refs_3_
  20.1 0.9 copy-done.2
  21.0 0.5 shard_map.87
  21.5 25.8 %all_to_all.10.message_ref = bf16[64,9,2,128]{3,2,1,0:T(2,128)(2,1)S(1)} all-to-all(bf16[64,9,2,128]{3,2,1,0:T(2,128)(2,1)S(1)} %shard_map.87), channel_id=1, replica_groups=mesh['dom'=64,'rep'=4] {'dom'}, dimensions={0} | all-to-all | bytes 589824 | tf_op jit(solution)/shard_map/all_to_all | solution.py:320
  47.3 0.8 shard_map.88
  48.1 2.7 %collective-permute-start.5 = (bf16[512,128]{1,0:T(8,128)(2,1)S(1)}, bf16[512,128]{1,0:T(8,128)(2,1)S(1)}, u32[]{:S(2)}, u32[]{:S(2)}) collective-permute-start(bf16[512,128]{1,0:T(8,128)(2,1)S(1)} %get-tuple-element.23.own_ref), channel_id=1, source_target_pairs={{0,3},{1,0},{2,1},{3,2},{4,7},{5,4},{6,5},{7,6},{8,11},{9,8},{10,9... | collective-permute-start | bytes 393224 | tf_op jit(solution)/shard_map/ppermute | solution.py:296
  50.8 0.0 collective-permute-start.4
  50.8 1.3 %collective-permute-start.3 = (bf16[512,128]{1,0:T(8,128)(2,1)S(1)}, bf16[512,128]{1,0:T(8,128)(2,1)S(1)}, u32[]{:S(2)}, u32[]{:S(2)}) collective-permute-start(bf16[512,128]{1,0:T(8,128)(2,1)S(1)} %get-tuple-element.23.own_ref), channel_id=1, source_target_pairs={{0,2},{1,3},{2,0},{3,1},{4,6},{5,7},{6,4},{7,5},{8,10},{9,11},{10,... | collective-permute-start | bytes 393224 | tf_op jit(solution)/shard_map/ppermute | solution.py:296
  52.1 1.5 %collective-permute-done.5.right_ref = bf16[512,128]{1,0:T(8,128)(2,1)S(1)} collective-permute-done((bf16[512,128]{1,0:T(8,128)(2,1)S(1)}, bf16[512,128]{1,0:T(8,128)(2,1)S(1)}, u32[]{:S(2)}, u32[]{:S(2)}) %collective-permute-start.5) | collective-permute-done | bytes 131104 | tf_op jit(solution)/shard_map/ppermute | solution.py:296
  53.6 5.9 %collective-permute-done.4.left_ref = bf16[512,128]{1,0:T(8,128)(2,1)S(1)} collective-permute-done((bf16[512,128]{1,0:T(8,128)(2,1)S(1)}, bf16[512,128]{1,0:T(8,128)(2,1)S(1)}, u32[]{:S(2)}, u32[]{:S(2)}) %collective-permute-start.4) | collective-permute-done | bytes 131104 | tf_op jit(solution)/shard_map/ppermute | solution.py:296
  59.5 0.0 collective-permute-done.3.across_ref
  59.5 1.0 %shard_map.89 = (f32[512,128]{1,0:T(8,128)}, f32[1,512]{1,0:T(1,128)}, bf16[1024,128]{1,0:T(8,128)(2,1)S(1)}) custom-call(bf16[512,128]{1,0:T(8,128)(2,1)S(1)} %get-tuple-element.23.own_ref, bf16[512,128]{1,0:T(8,128)(2,1)S(1)} %collective-permute-done.3.across_ref, bf16[512,128]{1,0:T(8,128)(2,1)S(1)} %collective-permute-done.4.left_ref, ...), custom_call_target="tpu_custom_call" | custom-call | flops 134217728 | bytes 1310720 | tf_op jit(solution)/shard_map/pallas_call | solution.py:235
  60.5 18.5 %all_to_all.11 = bf16[64,16,128]{2,1,0:T(8,128)(2,1)S(1)} all-to-all(bf16[64,16,128]{2,1,0:T(8,128)(2,1)S(1)} %bitcast.9), channel_id=1, replica_groups=mesh['dom'=64,'rep'=4] {'dom'}, dimensions={0} | all-to-all | bytes 524288 | tf_op jit(solution)/shard_map/all_to_all | solution.py:327
  79.0 0.4 shard_map.90.refs_1_
  79.4 0.1 collective-permute-start.8
  79.5 1.5 %collective-permute-start.7 = (bf16[512,128]{1,0:T(8,128)(2,1)S(1)}, bf16[512,128]{1,0:T(8,128)(2,1)S(1)}, u32[]{:S(2)}, u32[]{:S(2)}) collective-permute-start(bf16[512,128]{1,0:T(8,128)(2,1)S(1)} %shard_map.90.refs_1_), channel_id=1, source_target_pairs={{0,2},{1,3},{2,0},{3,1},{4,6},{5,7},{6,4},{7,5},{8,10},{9,11},{10,... | collective-permute-start | bytes 393224 | tf_op jit(solution)/shard_map/ppermute | solution.py:296
  81.0 1.2 %collective-permute-start.6 = (bf16[512,128]{1,0:T(8,128)(2,1)S(1)}, bf16[512,128]{1,0:T(8,128)(2,1)S(1)}, u32[]{:S(2)}, u32[]{:S(2)}) collective-permute-start(bf16[512,128]{1,0:T(8,128)(2,1)S(1)} %shard_map.90.refs_1_), channel_id=1, source_target_pairs={{0,3},{1,0},{2,1},{3,2},{4,7},{5,4},{6,5},{7,6},{8,11},{9,8},{10,9... | collective-permute-start | bytes 393224 | tf_op jit(solution)/shard_map/ppermute | solution.py:296
  82.2 6.2 %collective-permute-done.8.refs_3_ = bf16[512,128]{1,0:T(8,128)(2,1)S(1)} collective-permute-done((bf16[512,128]{1,0:T(8,128)(2,1)S(1)}, bf16[512,128]{1,0:T(8,128)(2,1)S(1)}, u32[]{:S(2)}, u32[]{:S(2)}) %collective-permute-start.8) | collective-permute-done | bytes 131104 | tf_op jit(solution)/shard_map/ppermute | solution.py:296
  88.4 0.0 collective-permute-done.7.refs_2_
  88.4 0.6 copy-done.6
  89.0 0.6 copy-done.8
  89.7 1.8 %shard_map.91.refs_2_ = bf16[2048,128]{1,0:T(8,128)(2,1)} custom-call(s32[1]{0:T(128)} %bitcast.me_ref.refs_0_, bf16[512,128]{1,0:T(8,128)(2,1)} %copy-done, bf16[512,128]{1,0:T(8,128)(2,1)} %copy-done.8, bf16[512,128]{1,0:T(8,128)(2,1)} %copy-done.6), custom_call_target="tpu_custom_call" | custom-call | bytes 786432 | tf_op jit(solution)/shard_map/pallas_call | solution.py:282
  91.5 0.0 collective-permute-done.6.refs_1_
  91.5 0.6 copy-done.7
  92.1 1.6 %shard_map.92 = bf16[2048,128]{1,0:T(8,128)(2,1)} custom-call(s32[1]{0:T(128)} %bitcast.me_ref.refs_0_, bf16[512,128]{1,0:T(8,128)(2,1)} %copy-done.7, bf16[2048,128]{1,0:T(8,128)(2,1)} %shard_map.91.refs_2_), custom_call_target="tpu_custom_call", output_to_operand_aliasing={{}: (2, {})} | custom-call | bytes 262144 | tf_op jit(solution)/shard_map/pallas_call | solution.py:282
  (14 shorter events, 0.0 us)
Async XLA Ops:
  0.6 14.7 %copy-start.5 = (s32[2048]{0:T(1024)S(1)}, s32[2048]{0:T(1024)}, u32[]{:S(2)}) copy-start(s32[2048]{0:T(1024)} %param.9) | copy-start | bytes 24580
  0.6 14.7 %copy-start.4 = (s32[2048,1]{0,1:T(1,128)S(1)}, s32[2048,1]{0,1:T(1,128)}, u32[]{:S(2)}) copy-start(s32[2048,1]{0,1:T(1,128)} %param.8) | copy-start | bytes 24580
  0.7 58.8 %copy-start.3 = (f32[512]{0:T(512)S(1)}, f32[512]{0:T(512)}, u32[]{:S(2)}) copy-start(f32[512]{0:T(512)} %param.11) | copy-start | bytes 6148
  0.7 58.8 %copy-start.1 = (f32[512,128]{1,0:T(8,128)S(1)}, f32[512,128]{1,0:T(8,128)}, u32[]{:S(2)}) copy-start(f32[512,128]{1,0:T(8,128)} %table_ref.1) | copy-start | bytes 786436
  9.0 7.3 %collective-permute-start = (bf16[512,128]{1,0:T(8,128)(2,1)}, bf16[512,128]{1,0:T(8,128)(2,1)S(1)}, u32[]{:S(2)}, u32[]{:S(2)}) collective-permute-start(bf16[512,128]{1,0:T(8,128)(2,1)} %get-tuple-element.20), channel_id=1, source_target_pairs={{0,2},{1,3},{2,0},{3,1},{4,6},{5,7},{6,4},{7,5},{8,10},{9,11},{10,... | collective-permute-start | bytes 393224 | tf_op jit(solution)/shard_map/ppermute | solution.py:296
  12.7 7.4 %collective-permute-start.1 = (bf16[512,128]{1,0:T(8,128)(2,1)}, bf16[512,128]{1,0:T(8,128)(2,1)S(1)}, u32[]{:S(2)}, u32[]{:S(2)}) collective-permute-start(bf16[512,128]{1,0:T(8,128)(2,1)} %get-tuple-element.21), channel_id=1, source_target_pairs={{0,1},{1,2},{2,3},{3,0},{4,5},{5,6},{6,7},{7,4},{8,9},{9,10},{10,1... | collective-permute-start | bytes 393224 | tf_op jit(solution)/shard_map/ppermute | solution.py:296
  13.0 7.1 %collective-permute-start.2 = (bf16[512,128]{1,0:T(8,128)(2,1)}, bf16[512,128]{1,0:T(8,128)(2,1)S(1)}, u32[]{:S(2)}, u32[]{:S(2)}) collective-permute-start(bf16[512,128]{1,0:T(8,128)(2,1)} %get-tuple-element.22), channel_id=1, source_target_pairs={{0,3},{1,0},{2,1},{3,2},{4,7},{5,4},{6,5},{7,6},{8,11},{9,8},{10,9... | collective-permute-start | bytes 393224 | tf_op jit(solution)/shard_map/ppermute | solution.py:296
  20.1 0.9 copy-start.2
  48.1 5.5 %collective-permute-start.5 = (bf16[512,128]{1,0:T(8,128)(2,1)S(1)}, bf16[512,128]{1,0:T(8,128)(2,1)S(1)}, u32[]{:S(2)}, u32[]{:S(2)}) collective-permute-start(bf16[512,128]{1,0:T(8,128)(2,1)S(1)} %get-tuple-element.23.own_ref), channel_id=1, source_target_pairs={{0,3},{1,0},{2,1},{3,2},{4,7},{5,4},{6,5},{7,6},{8,11},{9,8},{10,9... | collective-permute-start | bytes 393224 | tf_op jit(solution)/shard_map/ppermute | solution.py:296
  50.8 8.7 %collective-permute-start.4 = (bf16[512,128]{1,0:T(8,128)(2,1)S(1)}, bf16[512,128]{1,0:T(8,128)(2,1)S(1)}, u32[]{:S(2)}, u32[]{:S(2)}) collective-permute-start(bf16[512,128]{1,0:T(8,128)(2,1)S(1)} %get-tuple-element.23.own_ref), channel_id=1, source_target_pairs={{0,1},{1,2},{2,3},{3,0},{4,5},{5,6},{6,7},{7,4},{8,9},{9,10},{10,1... | collective-permute-start | bytes 393224 | tf_op jit(solution)/shard_map/ppermute | solution.py:296
  50.8 8.7 %collective-permute-start.3 = (bf16[512,128]{1,0:T(8,128)(2,1)S(1)}, bf16[512,128]{1,0:T(8,128)(2,1)S(1)}, u32[]{:S(2)}, u32[]{:S(2)}) collective-permute-start(bf16[512,128]{1,0:T(8,128)(2,1)S(1)} %get-tuple-element.23.own_ref), channel_id=1, source_target_pairs={{0,2},{1,3},{2,0},{3,1},{4,6},{5,7},{6,4},{7,5},{8,10},{9,11},{10,... | collective-permute-start | bytes 393224 | tf_op jit(solution)/shard_map/ppermute | solution.py:296
  79.4 9.0 %copy-start = (bf16[512,128]{1,0:T(8,128)(2,1)}, bf16[512,128]{1,0:T(8,128)(2,1)S(1)}, u32[]{:S(2)}) copy-start(bf16[512,128]{1,0:T(8,128)(2,1)S(1)} %shard_map.90.refs_1_) | copy-start | bytes 393220
  79.4 8.9 %collective-permute-start.8 = (bf16[512,128]{1,0:T(8,128)(2,1)S(1)}, bf16[512,128]{1,0:T(8,128)(2,1)S(1)}, u32[]{:S(2)}, u32[]{:S(2)}) collective-permute-start(bf16[512,128]{1,0:T(8,128)(2,1)S(1)} %shard_map.90.refs_1_), channel_id=1, source_target_pairs={{0,1},{1,2},{2,3},{3,0},{4,5},{5,6},{6,7},{7,4},{8,9},{9,10},{10,1... | collective-permute-start | bytes 393224 | tf_op jit(solution)/shard_map/ppermute | solution.py:296
  79.5 8.9 %collective-permute-start.7 = (bf16[512,128]{1,0:T(8,128)(2,1)S(1)}, bf16[512,128]{1,0:T(8,128)(2,1)S(1)}, u32[]{:S(2)}, u32[]{:S(2)}) collective-permute-start(bf16[512,128]{1,0:T(8,128)(2,1)S(1)} %shard_map.90.refs_1_), channel_id=1, source_target_pairs={{0,2},{1,3},{2,0},{3,1},{4,6},{5,7},{6,4},{7,5},{8,10},{9,11},{10,... | collective-permute-start | bytes 393224 | tf_op jit(solution)/shard_map/ppermute | solution.py:296
  81.0 10.4 %collective-permute-start.6 = (bf16[512,128]{1,0:T(8,128)(2,1)S(1)}, bf16[512,128]{1,0:T(8,128)(2,1)S(1)}, u32[]{:S(2)}, u32[]{:S(2)}) collective-permute-start(bf16[512,128]{1,0:T(8,128)(2,1)S(1)} %shard_map.90.refs_1_), channel_id=1, source_target_pairs={{0,3},{1,0},{2,1},{3,2},{4,7},{5,4},{6,5},{7,6},{8,11},{9,8},{10,9... | collective-permute-start | bytes 393224 | tf_op jit(solution)/shard_map/ppermute | solution.py:296
  88.4 0.6 copy-start.6
  89.0 0.6 copy-start.8
  91.5 0.6 copy-start.7

commit v3 on v2

--- a/solution.py
+++ b/solution.py
@@ -13,7 +13,6 @@
 MEBI = 1024 * 1024
 
 VMEM = pl.BlockSpec(memory_space=pltpu.VMEM)
-SMEM = pl.BlockSpec(memory_space=pltpu.SMEM)
 HBM = pl.BlockSpec(memory_space=pltpu.HBM)
 BF16 = jnp.bfloat16
 F32 = jnp.float32
@@ -43,7 +42,7 @@
     )
 
 
-def propagate_kernel(me_ref, tile_hbm, grad_hbm, *refs):
+def propagate_kernel(tile_hbm, grad_hbm, *refs):
     outs = refs[:-6]
     tile, grad, state, total, arrived, grad_arrived = refs[-6:]
     blocks = arrived.shape[0]
@@ -81,20 +80,20 @@
     for part in range(replicas):
         state[:, part * quarter : (part + 1) * quarter] = third[part]
     for step in range(replicas):
-        start = lax.rem(me_ref[0] + step, replicas) * quarter
+        start = lax.rem(lax.axis_index("rep") + step, replicas) * quarter
         lanes = pl.ds(pl.multiple_of(start, quarter), quarter)
         last = product(state[...], tile[:, lanes]).astype(BF16)
         term = total[:, lanes] + state[:, lanes].astype(F32) + last.astype(F32)
         outs[step][...] = (term / F32(LAYERS + 1)).astype(BF16).T
 
 
-def propagate(me, adjacency, start, replicas):
+def propagate(adjacency, start, replicas):
     rows, width = start.shape
     piece = shaped((rows // replicas, width), BF16)
     return call(
         propagate_kernel,
         [piece] * replicas,
-        [SMEM, HBM, HBM],
+        [HBM, HBM],
         [VMEM] * replicas,
         scratch=[
             pltpu.VMEM((rows, rows), BF16),
@@ -104,16 +103,16 @@
             pltpu.SemaphoreType.DMA((BLOCKS,)),
             pltpu.SemaphoreType.DMA,
         ],
-        mebi=60,
+        mebi=50,
         flops=2 * LAYERS * rows * rows * width,
         moved=2 * rows * rows + 4 * rows * width,
-    )(me, adjacency, start)
-
-
-def plan_kernel(capacity, me_ref, owner_ref, slot_ref, pack_ref, unpack_ref, slots_ref):
+    )(adjacency, start)
+
+
+def plan_kernel(capacity, owner_ref, slot_ref, pack_ref, unpack_ref, slots_ref):
     places, quarter = pack_ref.shape
     peers = places // capacity
-    lanes = pl.ds(pl.multiple_of(me_ref[0] * quarter, quarter), quarter)
+    lanes = pl.ds(pl.multiple_of(lax.axis_index("rep") * quarter, quarter), quarter)
     owner = owner_ref[:, lanes]
     slot = slot_ref[:, lanes]
     hot = ids((peers, quarter), 0) == owner
@@ -138,7 +137,7 @@
     slots_ref[...] = lists.astype(BF16)
 
 
-def plan(me, row_owner, table_slot, quarter, peers, capacity):
+def plan(row_owner, table_slot, quarter, peers, capacity):
     rows = table_slot.shape[0]
     places = peers * capacity
 
@@ -152,11 +151,11 @@
             shaped((quarter, places), BF16),
             shaped((peers, LANES), BF16),
         ],
-        [SMEM, VMEM, VMEM],
+        [VMEM, VMEM],
         [VMEM] * 3,
         flops=2 * quarter * quarter * peers,
         moved=4 * places * quarter,
-    )(me, row_owner.reshape(1, rows), table_slot.reshape(1, rows))
+    )(row_owner.reshape(1, rows), table_slot.reshape(1, rows))
 
 
 def pack_kernel(pack_ref, slots_ref, *refs):
@@ -259,39 +258,6 @@
     )(matrix, returned)
 
 
-def place_kernel(steps, replicas, me_ref, *refs):
-    pieces = refs[: len(steps)]
-    out_hbm, sent = refs[-2:]
-    quarter = pieces[0].shape[0]
-    copies = []
-    for index, step in enumerate(steps):
-        source = lax.rem(me_ref[0] + replicas - step, replicas) * quarter
-        rows = pl.ds(pl.multiple_of(source, quarter), quarter)
-        copies.append(pltpu.make_async_copy(pieces[index], out_hbm.at[rows], sent.at[index]))
-        copies[-1].start()
-    for copy in copies:
-        copy.wait()
-
-
-def place(me, steps, pieces, replicas, rows, before=None):
-    def kernel(*refs):
-        place_kernel(steps, replicas, *refs)
-
-    earlier = [] if before is None else [before]
-    quarter, width = pieces[0].shape
-    return pl.pallas_call(
-        kernel,
-        out_shape=shaped((rows, width), BF16),
-        in_specs=[SMEM] + [VMEM] * len(pieces) + [HBM] * len(earlier),
-        out_specs=HBM,
-        scratch_shapes=[pltpu.SemaphoreType.DMA((len(pieces),))],
-        input_output_aliases={1 + len(pieces): 0} if earlier else {},
-        cost_estimate=pl.CostEstimate(
-            flops=0, bytes_accessed=4 * quarter * width * len(pieces), transcendentals=0
-        ),
-    )(me, *pieces, *earlier)
-
-
 def send(piece, step, replicas):
     return lax.ppermute(piece, "rep", [(i, (i + step) % replicas) for i in range(replicas)])
 
@@ -309,12 +275,12 @@
     quarter = rows // replicas
     capacity = max(2, 2 * quarter // peers)
     order = send_order(replicas)
-    me = jnp.full((1,), lax.axis_index("rep"), jnp.int32)
-
-    terms = propagate(me, adjacency, grad_out[0], replicas)
+    me = lax.axis_index("rep")
+
+    terms = propagate(adjacency, grad_out[0], replicas)
     got_terms = [send(terms[step], step, replicas) for step in order]
-    later, _ = lax.optimization_barrier((me, terms[0]))
-    to_places, from_places, slots = plan(later, row_owner, table_slot, quarter, peers, capacity)
+    owners, _ = lax.optimization_barrier((row_owner, terms[0]))
+    to_places, from_places, slots = plan(owners, table_slot, quarter, peers, capacity)
     message = pack(to_places, slots, [terms[0], *got_terms], capacity)
 
     incoming = lax.all_to_all(message, "dom", split_axis=0, concat_axis=0, tiled=True)
@@ -329,8 +295,10 @@
     )
     fresh = unpack(from_places, returned.reshape(peers * capacity, width))
     pieces = [send(fresh, step, replicas) for step in order]
-    fresh_rows = place(me, [0, *order[:-1]], [fresh, *pieces[:-1]], replicas, rows)
-    fresh_rows = place(me, order[-1:], pieces[-1:], replicas, rows, before=fresh_rows)
+    fresh_rows = jnp.zeros((rows, width), BF16)
+    for step, piece in zip([0, *order], [fresh, *pieces]):
+        source = lax.rem(me + replicas - step, replicas) * quarter
+        fresh_rows = lax.dynamic_update_slice(fresh_rows, piece, (source, 0))
     return (new_table, new_accumulators, fresh_rows)
 
 

time: 94.1 us -> 86.1 us (0.915)
  Pallas kernels: 15.4 us -> 10 us
  waiting for transfers between devices: 17.3 us -> 14.7 us
  starting transfers between devices: 13 us -> 14.7 us
    pallas_call x3 -> x1, Pallas kernels: 11.7 us -> 6.32 us  [propagate(): call(propagate_kernel, [piece] * replicas, [HBM, HBM], [VMEM] * replicas,...]
    ppermute x9, waiting for transfers between devices: 17.3 us -> 14.7 us  [send(): lax.ppermute(piece, 'rep', [(i, (i + step) % replicas) for i in range(rep...]
    ppermute x9, starting transfers between devices: 13 us -> 14.7 us  [send(): lax.ppermute(piece, 'rep', [(i, (i + step) % replicas) for i in range(rep...]
    unnamed x18 -> x12, local copies, waits for them, and re-layouts: 2.85 us -> 1.88 us
  transfers between devices with their start and end apart: 9 -> 9, of which waited for: 4 -> 5; matrix products, arithmetic and copies ran while one was open for 0% -> 0% of each run, Pallas kernels for 3% -> 1%
where the time goes in v3:
time: 86.1 us; the launch traced here: 85.9 us
  blocking collectives  43.7 us (51%)
  starting transfers between devices  14.7 us (17%)
  waiting for transfers between devices  14.7 us (17%)
  Pallas kernels  10 us (12%)
  local copies, waits for them, and re-layouts  2.04 us (2%)
    all_to_all x1, blocking collectives, on_device(): lax.all_to_all(message, 'dom', split_axis=0, concat_axis=0, tiled=True)  25.8 us
    all_to_all x1, blocking collectives, on_device(): lax.all_to_all(answer.reshape(peers, capacity, width), 'dom', split_axis=...  17.9 us
    ppermute x9, waiting for transfers between devices, send(): lax.ppermute(piece, 'rep', [(i, (i + step) % replicas) for i in range(rep...  14.7 us
    ppermute x9, starting transfers between devices, send(): lax.ppermute(piece, 'rep', [(i, (i + step) % replicas) for i in range(rep...  14.7 us
    pallas_call x1, Pallas kernels, propagate(): call(propagate_kernel, [piece] * replicas, [HBM, HBM], [VMEM] * replicas,...  6.32 us
    unnamed x12, local copies, waits for them, and re-layouts  1.88 us
  transfers between devices with their start and end apart: 9, of which 5 were waited for; matrix products, arithmetic and copies ran while one was open for 0% of the time, Pallas kernels for 1%

profile of v3, /device:TPU:1, one launch (start us, length us, event | category | flops | bytes accessed | tf_op | source)
XLA Modules:
  0.0 85.9 jit_solution(6456999532954170716)
XLA Ops:
  0.6 0.0 copy-start.1
  0.7 1.1 %copy-done.2 = bf16[1,2048,128]{2,1,0:T(8,128)(2,1)S(1)} copy-done((bf16[1,2048,128]{2,1,0:T(8,128)(2,1)S(1)}, bf16[1,2048,128]{2,1,0:T(8,128)(2,1)}, u32[]{:S(2)}) %copy-start.2) | copy-done | bytes 524312
  1.7 6.3 %shard_map.85 = (bf16[512,128]{1,0:T(8,128)(2,1)S(1)}, bf16[512,128]{1,0:T(8,128)(2,1)S(1)}, bf16[512,128]{1,0:T(8,128)(2,1)S(1)}, bf16[512,128]{1,0:T(8,128)(2,1)S(1)}) custom-call(bf16[2048,2048]{1,0:T(8,128)(2,1)} %tile_hbm.1, bf16[2048,128]{1,0:T(8,128)(2,1)S(1)} %bitcast.10), custom_call_target="tpu_custom_call" | custom-call | flops 3221225472 | bytes 9437184 | tf_op jit(solution)/shard_map/pallas_call | solution.py:93
  8.1 3.7 %collective-permute-start = (bf16[512,128]{1,0:T(8,128)(2,1)S(1)}, bf16[512,128]{1,0:T(8,128)(2,1)S(1)}, u32[]{:S(2)}, u32[]{:S(2)}) collective-permute-start(bf16[512,128]{1,0:T(8,128)(2,1)S(1)} %get-tuple-element.20), channel_id=1, source_target_pairs={{0,2},{1,3},{2,0},{3,1},{4,6},{5,7},{6,4},{7,5},{8,10},{9,11},{10,... | collective-permute-start | bytes 393224 | tf_op jit(solution)/shard_map/ppermute | solution.py:262
  11.7 0.3 collective-permute-start.1
  12.0 2.4 %collective-permute-start.2 = (bf16[512,128]{1,0:T(8,128)(2,1)S(1)}, bf16[512,128]{1,0:T(8,128)(2,1)S(1)}, u32[]{:S(2)}, u32[]{:S(2)}) collective-permute-start(bf16[512,128]{1,0:T(8,128)(2,1)S(1)} %get-tuple-element.22), channel_id=1, source_target_pairs={{0,3},{1,0},{2,1},{3,2},{4,7},{5,4},{6,5},{7,6},{8,11},{9,8},{10,9... | collective-permute-start | bytes 393224 | tf_op jit(solution)/shard_map/ppermute | solution.py:262
  14.4 1.0 %shard_map.86 = (bf16[1024,512]{1,0:T(8,128)(2,1)S(1)}, bf16[512,1024]{1,0:T(8,128)(2,1)S(1)}, bf16[64,128]{1,0:T(8,128)(2,1)S(1)}) custom-call(s32[1,2048]{1,0:T(1,128)S(1)} %bitcast.11, s32[1,2048]{1,0:T(1,128)S(1)} %bitcast.12), custom_call_target="tpu_custom_call" | custom-call | flops 33554432 | bytes 2097152 | tf_op jit(solution)/shard_map/pallas_call | solution.py:147
  15.4 0.0 collective-permute-done.refs_1_
  15.4 3.5 %collective-permute-done.1.refs_2_ = bf16[512,128]{1,0:T(8,128)(2,1)S(1)} collective-permute-done((bf16[512,128]{1,0:T(8,128)(2,1)S(1)}, bf16[512,128]{1,0:T(8,128)(2,1)S(1)}, u32[]{:S(2)}, u32[]{:S(2)}) %collective-permute-start.1) | collective-permute-done | bytes 131104 | tf_op jit(solution)/shard_map/ppermute | solution.py:262
  18.9 0.0 collective-permute-done.2.refs_3_
  18.9 0.5 shard_map.87
  19.5 25.8 %all_to_all.10.message_ref = bf16[64,9,2,128]{3,2,1,0:T(2,128)(2,1)S(1)} all-to-all(bf16[64,9,2,128]{3,2,1,0:T(2,128)(2,1)S(1)} %shard_map.87), channel_id=1, replica_groups=mesh['dom'=64,'rep'=4] {'dom'}, dimensions={0} | all-to-all | bytes 589824 | tf_op jit(solution)/shard_map/all_to_all | solution.py:286
  45.2 0.8 shard_map.88
  46.0 1.6 %collective-permute-start.3 = (bf16[512,128]{1,0:T(8,128)(2,1)S(1)}, bf16[512,128]{1,0:T(8,128)(2,1)S(1)}, u32[]{:S(2)}, u32[]{:S(2)}) collective-permute-start(bf16[512,128]{1,0:T(8,128)(2,1)S(1)} %get-tuple-element.23.own_ref), channel_id=1, source_target_pairs={{0,2},{1,3},{2,0},{3,1},{4,6},{5,7},{6,4},{7,5},{8,10},{9,11},{10,... | collective-permute-start | bytes 393224 | tf_op jit(solution)/shard_map/ppermute | solution.py:262
  47.6 1.7 %collective-permute-start.4 = (bf16[512,128]{1,0:T(8,128)(2,1)S(1)}, bf16[512,128]{1,0:T(8,128)(2,1)S(1)}, u32[]{:S(2)}, u32[]{:S(2)}) collective-permute-start(bf16[512,128]{1,0:T(8,128)(2,1)S(1)} %get-tuple-element.23.own_ref), channel_id=1, source_target_pairs={{0,1},{1,2},{2,3},{3,0},{4,5},{5,6},{6,7},{7,4},{8,9},{9,10},{10,1... | collective-permute-start | bytes 393224 | tf_op jit(solution)/shard_map/ppermute | solution.py:262
  49.3 1.0 %collective-permute-start.5 = (bf16[512,128]{1,0:T(8,128)(2,1)S(1)}, bf16[512,128]{1,0:T(8,128)(2,1)S(1)}, u32[]{:S(2)}, u32[]{:S(2)}) collective-permute-start(bf16[512,128]{1,0:T(8,128)(2,1)S(1)} %get-tuple-element.23.own_ref), channel_id=1, source_target_pairs={{0,3},{1,0},{2,1},{3,2},{4,7},{5,4},{6,5},{7,6},{8,11},{9,8},{10,9... | collective-permute-start | bytes 393224 | tf_op jit(solution)/shard_map/ppermute | solution.py:262
  50.3 2.3 %collective-permute-done.3.across_ref = bf16[512,128]{1,0:T(8,128)(2,1)S(1)} collective-permute-done((bf16[512,128]{1,0:T(8,128)(2,1)S(1)}, bf16[512,128]{1,0:T(8,128)(2,1)S(1)}, u32[]{:S(2)}, u32[]{:S(2)}) %collective-permute-start.3) | collective-permute-done | bytes 131104 | tf_op jit(solution)/shard_map/ppermute | solution.py:262
  52.6 3.3 %collective-permute-done.4.left_ref = bf16[512,128]{1,0:T(8,128)(2,1)S(1)} collective-permute-done((bf16[512,128]{1,0:T(8,128)(2,1)S(1)}, bf16[512,128]{1,0:T(8,128)(2,1)S(1)}, u32[]{:S(2)}, u32[]{:S(2)}) %collective-permute-start.4) | collective-permute-done | bytes 131104 | tf_op jit(solution)/shard_map/ppermute | solution.py:262
  55.8 0.0 collective-permute-done.5.right_ref
  55.8 0.0 copy-done
  55.8 1.0 %shard_map.89 = (f32[512,128]{1,0:T(8,128)}, f32[1,512]{1,0:T(1,128)}, bf16[1024,128]{1,0:T(8,128)(2,1)S(1)}) custom-call(bf16[512,128]{1,0:T(8,128)(2,1)S(1)} %get-tuple-element.23.own_ref, bf16[512,128]{1,0:T(8,128)(2,1)S(1)} %collective-permute-done.3.across_ref, bf16[512,128]{1,0:T(8,128)(2,1)S(1)} %collective-permute-done.4.left_ref, ...), custom_call_target="tpu_custom_call" | custom-call | flops 134217728 | bytes 1310720 | tf_op jit(solution)/shard_map/pallas_call | solution.py:234
  56.9 17.9 %all_to_all.11 = bf16[64,16,128]{2,1,0:T(8,128)(2,1)S(1)} all-to-all(bf16[64,16,128]{2,1,0:T(8,128)(2,1)S(1)} %bitcast.8), channel_id=1, replica_groups=mesh['dom'=64,'rep'=4] {'dom'}, dimensions={0} | all-to-all | bytes 524288 | tf_op jit(solution)/shard_map/all_to_all | solution.py:293
  74.8 0.4 shard_map.90
  75.2 1.4 %collective-permute-start.6 = (bf16[512,128]{1,0:T(8,128)(2,1)S(1)}, bf16[512,128]{1,0:T(8,128)(2,1)S(1)}, u32[]{:S(2)}, u32[]{:S(2)}) collective-permute-start(bf16[512,128]{1,0:T(8,128)(2,1)S(1)} %shard_map.90), channel_id=1, source_target_pairs={{0,2},{1,3},{2,0},{3,1},{4,6},{5,7},{6,4},{7,5},{8,10},{9,11},{10,... | collective-permute-start | bytes 393224 | tf_op jit(solution)/shard_map/ppermute | solution.py:262
  76.6 1.7 %collective-permute-start.7 = (bf16[512,128]{1,0:T(8,128)(2,1)S(1)}, bf16[512,128]{1,0:T(8,128)(2,1)S(1)}, u32[]{:S(2)}, u32[]{:S(2)}) collective-permute-start(bf16[512,128]{1,0:T(8,128)(2,1)S(1)} %shard_map.90), channel_id=1, source_target_pairs={{0,1},{1,2},{2,3},{3,0},{4,5},{5,6},{6,7},{7,4},{8,9},{9,10},{10,1... | collective-permute-start | bytes 393224 | tf_op jit(solution)/shard_map/ppermute | solution.py:262
  78.3 1.0 %collective-permute-start.8 = (bf16[512,128]{1,0:T(8,128)(2,1)S(1)}, bf16[512,128]{1,0:T(8,128)(2,1)S(1)}, u32[]{:S(2)}, u32[]{:S(2)}) collective-permute-start(bf16[512,128]{1,0:T(8,128)(2,1)S(1)} %shard_map.90), channel_id=1, source_target_pairs={{0,3},{1,0},{2,1},{3,2},{4,7},{5,4},{6,5},{7,6},{8,11},{9,8},{10,9... | collective-permute-start | bytes 393224 | tf_op jit(solution)/shard_map/ppermute | solution.py:262
  79.3 0.1 broadcast_in_dim.3
  79.4 2.2 %collective-permute-done.6 = bf16[512,128]{1,0:T(8,128)(2,1)S(1)} collective-permute-done((bf16[512,128]{1,0:T(8,128)(2,1)S(1)}, bf16[512,128]{1,0:T(8,128)(2,1)S(1)}, u32[]{:S(2)}, u32[]{:S(2)}) %collective-permute-start.6) | collective-permute-done | bytes 131104 | tf_op jit(solution)/shard_map/ppermute | solution.py:262
  81.7 3.4 %collective-permute-done.7 = bf16[512,128]{1,0:T(8,128)(2,1)S(1)} collective-permute-done((bf16[512,128]{1,0:T(8,128)(2,1)S(1)}, bf16[512,128]{1,0:T(8,128)(2,1)S(1)}, u32[]{:S(2)}, u32[]{:S(2)}) %collective-permute-start.7) | collective-permute-done | bytes 131104 | tf_op jit(solution)/shard_map/ppermute | solution.py:262
  85.1 0.0 collective-permute-done.8
  85.1 0.0 copy-start.5
  85.1 0.8 copy-done.5
  (11 shorter events, 0.1 us)
Async XLA Ops:
  0.6 55.2 %copy-start.1 = (f32[512]{0:T(512)S(1)}, f32[512]{0:T(512)}, u32[]{:S(2)}) copy-start(f32[512]{0:T(512)} %param.11) | copy-start | bytes 6148
  0.6 55.2 %copy-start = (f32[512,128]{1,0:T(8,128)S(1)}, f32[512,128]{1,0:T(8,128)}, u32[]{:S(2)}) copy-start(f32[512,128]{1,0:T(8,128)} %table_ref.1) | copy-start | bytes 786436
  0.7 1.1 %copy-start.2 = (bf16[1,2048,128]{2,1,0:T(8,128)(2,1)S(1)}, bf16[1,2048,128]{2,1,0:T(8,128)(2,1)}, u32[]{:S(2)}) copy-start(bf16[1,2048,128]{2,1,0:T(8,128)(2,1)} %param.7) | copy-start | bytes 1572868
  1.7 12.7 %copy-start.3 = (s32[2048,1]{0,1:T(1,128)S(1)}, s32[2048,1]{0,1:T(1,128)}, u32[]{:S(2)}) copy-start(s32[2048,1]{0,1:T(1,128)} %param.8) | copy-start | bytes 24580
  1.7 12.7 %copy-start.4 = (s32[2048]{0:T(1024)S(1)}, s32[2048]{0:T(1024)}, u32[]{:S(2)}) copy-start(s32[2048]{0:T(1024)} %param.9) | copy-start | bytes 24580
  8.1 7.3 %collective-permute-start = (bf16[512,128]{1,0:T(8,128)(2,1)S(1)}, bf16[512,128]{1,0:T(8,128)(2,1)S(1)}, u32[]{:S(2)}, u32[]{:S(2)}) collective-permute-start(bf16[512,128]{1,0:T(8,128)(2,1)S(1)} %get-tuple-element.20), channel_id=1, source_target_pairs={{0,2},{1,3},{2,0},{3,1},{4,6},{5,7},{6,4},{7,5},{8,10},{9,11},{10,... | collective-permute-start | bytes 393224 | tf_op jit(solution)/shard_map/ppermute | solution.py:262
  11.7 7.2 %collective-permute-start.1 = (bf16[512,128]{1,0:T(8,128)(2,1)S(1)}, bf16[512,128]{1,0:T(8,128)(2,1)S(1)}, u32[]{:S(2)}, u32[]{:S(2)}) collective-permute-start(bf16[512,128]{1,0:T(8,128)(2,1)S(1)} %get-tuple-element.21), channel_id=1, source_target_pairs={{0,1},{1,2},{2,3},{3,0},{4,5},{5,6},{6,7},{7,4},{8,9},{9,10},{10,1... | collective-permute-start | bytes 393224 | tf_op jit(solution)/shard_map/ppermute | solution.py:262
  12.0 6.9 %collective-permute-start.2 = (bf16[512,128]{1,0:T(8,128)(2,1)S(1)}, bf16[512,128]{1,0:T(8,128)(2,1)S(1)}, u32[]{:S(2)}, u32[]{:S(2)}) collective-permute-start(bf16[512,128]{1,0:T(8,128)(2,1)S(1)} %get-tuple-element.22), channel_id=1, source_target_pairs={{0,3},{1,0},{2,1},{3,2},{4,7},{5,4},{6,5},{7,6},{8,11},{9,8},{10,9... | collective-permute-start | bytes 393224 | tf_op jit(solution)/shard_map/ppermute | solution.py:262
  46.0 6.6 %collective-permute-start.3 = (bf16[512,128]{1,0:T(8,128)(2,1)S(1)}, bf16[512,128]{1,0:T(8,128)(2,1)S(1)}, u32[]{:S(2)}, u32[]{:S(2)}) collective-permute-start(bf16[512,128]{1,0:T(8,128)(2,1)S(1)} %get-tuple-element.23.own_ref), channel_id=1, source_target_pairs={{0,2},{1,3},{2,0},{3,1},{4,6},{5,7},{6,4},{7,5},{8,10},{9,11},{10,... | collective-permute-start | bytes 393224 | tf_op jit(solution)/shard_map/ppermute | solution.py:262
  47.6 8.2 %collective-permute-start.4 = (bf16[512,128]{1,0:T(8,128)(2,1)S(1)}, bf16[512,128]{1,0:T(8,128)(2,1)S(1)}, u32[]{:S(2)}, u32[]{:S(2)}) collective-permute-start(bf16[512,128]{1,0:T(8,128)(2,1)S(1)} %get-tuple-element.23.own_ref), channel_id=1, source_target_pairs={{0,1},{1,2},{2,3},{3,0},{4,5},{5,6},{6,7},{7,4},{8,9},{9,10},{10,1... | collective-permute-start | bytes 393224 | tf_op jit(solution)/shard_map/ppermute | solution.py:262
  49.3 6.6 %collective-permute-start.5 = (bf16[512,128]{1,0:T(8,128)(2,1)S(1)}, bf16[512,128]{1,0:T(8,128)(2,1)S(1)}, u32[]{:S(2)}, u32[]{:S(2)}) collective-permute-start(bf16[512,128]{1,0:T(8,128)(2,1)S(1)} %get-tuple-element.23.own_ref), channel_id=1, source_target_pairs={{0,3},{1,0},{2,1},{3,2},{4,7},{5,4},{6,5},{7,6},{8,11},{9,8},{10,9... | collective-permute-start | bytes 393224 | tf_op jit(solution)/shard_map/ppermute | solution.py:262
  75.2 6.4 %collective-permute-start.6 = (bf16[512,128]{1,0:T(8,128)(2,1)S(1)}, bf16[512,128]{1,0:T(8,128)(2,1)S(1)}, u32[]{:S(2)}, u32[]{:S(2)}) collective-permute-start(bf16[512,128]{1,0:T(8,128)(2,1)S(1)} %shard_map.90), channel_id=1, source_target_pairs={{0,2},{1,3},{2,0},{3,1},{4,6},{5,7},{6,4},{7,5},{8,10},{9,11},{10,... | collective-permute-start | bytes 393224 | tf_op jit(solution)/shard_map/ppermute | solution.py:262
  76.6 8.4 %collective-permute-start.7 = (bf16[512,128]{1,0:T(8,128)(2,1)S(1)}, bf16[512,128]{1,0:T(8,128)(2,1)S(1)}, u32[]{:S(2)}, u32[]{:S(2)}) collective-permute-start(bf16[512,128]{1,0:T(8,128)(2,1)S(1)} %shard_map.90), channel_id=1, source_target_pairs={{0,1},{1,2},{2,3},{3,0},{4,5},{5,6},{6,7},{7,4},{8,9},{9,10},{10,1... | collective-permute-start | bytes 393224 | tf_op jit(solution)/shard_map/ppermute | solution.py:262
  78.3 6.8 %collective-permute-start.8 = (bf16[512,128]{1,0:T(8,128)(2,1)S(1)}, bf16[512,128]{1,0:T(8,128)(2,1)S(1)}, u32[]{:S(2)}, u32[]{:S(2)}) collective-permute-start(bf16[512,128]{1,0:T(8,128)(2,1)S(1)} %shard_map.90), channel_id=1, source_target_pairs={{0,3},{1,0},{2,1},{3,2},{4,7},{5,4},{6,5},{7,6},{8,11},{9,8},{10,9... | collective-permute-start | bytes 393224 | tf_op jit(solution)/shard_map/ppermute | solution.py:262
  85.1 0.8 copy-start.5

commit v4 on v0

v4 whole, which is shorter than its diff:
```python
import jax
import jax.numpy as jnp
from jax import lax
from jax.experimental import pallas as pl
from jax.experimental.pallas import tpu as pltpu
from jax.sharding import PartitionSpec as P

LAYERS = 3
LEARN_RATE = 0.5
LANES = 128
SUBLANES = 8
PACKED = 16
CHUNKS = 4
RADIX_BITS = 4
MEBI = 1024 * 1024

VMEM = pl.BlockSpec(memory_space=pltpu.VMEM)
HBM = pl.BlockSpec(memory_space=pltpu.HBM)
BF16 = jnp.bfloat16
F32 = jnp.float32


def ids(shape, axis):
    return lax.broadcasted_iota(jnp.int32, shape, axis)


def product(left, right):
    return jnp.dot(left, right, preferred_element_type=F32)


def shaped(shape, dtype):
    return jax.ShapeDtypeStruct(shape, dtype)


def call(kernel, out_shape, in_specs, out_specs, scratch=(), mebi=16, flops=0, moved=0):
    return pl.pallas_call(
        kernel,
        out_shape=out_shape,
        in_specs=in_specs,
        out_specs=out_specs,
        scratch_shapes=list(scratch),
        compiler_params=pltpu.CompilerParams(vmem_limit_bytes=mebi * MEBI),
        cost_estimate=pl.CostEstimate(flops=flops, bytes_accessed=moved, transcendentals=0),
    )


def split_kernel(grad_hbm, owner_hbm, slot_hbm, *refs):
    *pieces, owner, slot, grad, turned, arrived, lists_arrived = refs
    lists = [
        pltpu.make_async_copy(owner_hbm, owner, lists_arrived.at[0]),
        pltpu.make_async_copy(slot_hbm, slot, lists_arrived.at[1]),
    ]
    chunks = arrived.shape[0]
    depth = grad.shape[0] // chunks
    copies = []
    for chunk in range(chunks):
        part = pl.ds(chunk * depth, depth)
        copies.append(
            pltpu.make_async_copy(grad_hbm.at[part], grad.at[part], arrived.at[chunk])
        )
        copies[-1].start()
    for copy in lists:
        copy.start()
    for chunk in range(chunks):
        copies[chunk].wait()
        part = slice(chunk * depth, (chunk + 1) * depth)
        turned[:, part] = grad[part, :].T
    replicas, columns = len(pieces), pieces[0].shape[0]
    for step, piece in enumerate(pieces):
        start = lax.rem(lax.axis_index("rep") + step, replicas) * columns
        piece[...] = turned[pl.ds(pl.multiple_of(start, columns), columns), :]
    for copy in lists:
        copy.wait()


def split(grad, row_owner, table_slot, replicas):
    rows, width = grad.shape
    held = [grad, row_owner.reshape(1, rows), table_slot.reshape(1, rows)]
    *pieces, owner, slot = call(
        split_kernel,
        [shaped((width // replicas, rows), BF16)] * replicas
        + [pltpu.VMEM((1, rows), jnp.int32)] * 2,
        [HBM] * 3,
        [VMEM] * (replicas + 2),
        scratch=[
            pltpu.VMEM((rows, width), BF16),
            pltpu.VMEM((width, rows), BF16),
            pltpu.SemaphoreType.DMA((CHUNKS,)),
            pltpu.SemaphoreType.DMA((2,)),
        ],
    )(*[pltpu.with_memory_space_constraint(array, pltpu.HBM) for array in held])
    return pieces, owner, slot


def plan_kernel(
    capacity, tile_hbm, owner_ref, slot_ref, tile_ref, places_ref, slots_ref, weight_ref, mine_ref, arrived
):
    tile_copy = pltpu.make_async_copy(tile_hbm, tile_ref, arrived)
    tile_copy.start()
    quarters, quarter, places = places_ref.shape
    peers = places // capacity
    square = (quarter, quarter)
    upper = jnp.where(ids(square, 0) <= ids(square, 1), 1.0, 0.0).astype(BF16)
    index = ids((LANES, quarter), 0)
    lane = ids(mine_ref.shape, 0)
    lists = None
    for number in range(quarters):
        lanes = slice(number * quarter, (number + 1) * quarter)
        owner, slot = owner_ref[:, lanes], slot_ref[:, lanes]
        hot = ids((peers, quarter), 0) == owner
        owner_hot = jnp.where(hot, 1.0, 0.0).astype(BF16)
        running = product(owner_hot, upper)
        rank = jnp.sum(jnp.where(hot, running, 0.0), axis=0, keepdims=True).astype(jnp.int32) - 1
        place = (owner * capacity + rank).astype(F32)
        column = jnp.broadcast_to(place, (LANES, quarter)).T.astype(jnp.int32)
        for part in range(places // LANES):
            here = column == ids(column.shape, 1) + part * LANES
            places_ref[number, :, part * LANES : (part + 1) * LANES] = jnp.where(
                here, 1.0, 0.0
            ).astype(BF16)
        high, low = slot >> RADIX_BITS, slot & ((1 << RADIX_BITS) - 1)
        first = number * capacity + rank
        spread = jnp.where(
            index == first, high, jnp.where(index == first + quarters * capacity, low, 0)
        )
        added = lax.dot_general(
            owner_hot,
            spread.astype(F32).astype(BF16),
            (((1,), (1,)), ((), ())),
            preferred_element_type=F32,
        )
        lists = added if lists is None else lists + added
        lane, turn = ids((LANES, places), 0), lax.rem(ids((LANES, places), 1), capacity)
        turn = turn + number * capacity
        units = jnp.where(lane == turn + quarters * capacity, 1.0, 0.0)
        weight_ref[number] = jnp.where(lane == turn, float(1 << RADIX_BITS), units).astype(BF16)
    slots_ref[...] = lists.astype(BF16)
    mine = ids(mine_ref.shape, 0) == ids(mine_ref.shape, 1) // capacity
    mine_ref[...] = jnp.where(mine, 1.0, 0.0)
    tile_copy.wait()


def plan(adjacency, owner, slot, quarters, peers, capacity):
    rows = slot.shape[1]
    places = peers * capacity

    def kernel(*refs):
        plan_kernel(capacity, *refs)

    return call(
        kernel,
        [
            pltpu.VMEM(adjacency.shape, BF16),
            shaped((quarters, rows // quarters, places), BF16),
            shaped((peers, LANES), BF16),
            shaped((quarters, LANES, places), BF16),
            shaped((peers, places), F32),
        ],
        [HBM, VMEM, VMEM],
        [VMEM] * 5,
        scratch=[pltpu.SemaphoreType.DMA],
    )(pltpu.with_memory_space_constraint(adjacency, pltpu.HBM), owner, slot)


def propagate_kernel(*refs):
    *pieces, tile_ref, places_ref, slots_ref, out_ref = refs
    total = pieces[0][...].astype(F32)
    for piece in pieces[1:]:
        total = total + piece[...].astype(F32)
    state = total.astype(BF16)
    for _ in range(LAYERS):
        state = product(state, tile_ref[...]).astype(BF16)
        total = total + state.astype(F32)
    term = (total / F32(LAYERS + 1)).astype(BF16)
    quarters, quarter, _ = places_ref.shape
    packed = jnp.concatenate(
        [
            product(term[:, number * quarter : (number + 1) * quarter], places_ref[number])
            for number in range(quarters)
        ],
        axis=0,
    )
    peers, pairs = out_ref.shape[:2]
    out_ref[:, : pairs - 1] = packed.T.astype(BF16).reshape(peers, pairs - 1, 2, LANES)
    lists = slots_ref[...]
    out_ref[:, pairs - 1] = jnp.broadcast_to(lists[:, None, :], (peers, 2, LANES))


def propagate(pieces, tile, places, slots, capacity):
    peers = slots.shape[0]
    rows = tile.shape[0]
    return call(
        propagate_kernel,
        shaped((peers, capacity // 2 + 1, 2, LANES), BF16),
        [VMEM] * (len(pieces) + 3),
        VMEM,
        flops=2 * LAYERS * rows * rows * LANES,
        moved=2 * rows * rows,
    )(*pieces, tile, places, slots)


def accumulate_kernel(shard, message_ref, weight_ref, mine_ref, piece_ref, rows_ref):
    quarters, _, places = weight_ref.shape
    pairs = message_ref.shape[1]
    columns = LANES // quarters
    digits = message_ref[:, pairs - 1, 0, :]
    data = message_ref[:, : pairs - 1].reshape(places, LANES)
    block = ids((shard, LANES), 1) // columns
    index = ids((shard, places), 0).astype(jnp.int16)
    sums = None
    for number in range(quarters):
        lists = product(digits, weight_ref[number])
        slot = jnp.sum(lists * mine_ref[...], axis=0, keepdims=True).astype(jnp.int32)
        rows_ref[number] = jnp.broadcast_to(slot, rows_ref.shape[1:])
        wide = jnp.broadcast_to(slot, (PACKED, places)).astype(jnp.int16)
        hot = index == jnp.concatenate([wide] * (shard // PACKED), axis=0)
        receiver = jnp.where(hot, jnp.ones(hot.shape, BF16), jnp.zeros(hot.shape, BF16))
        added = product(receiver, data)
        sums = added if sums is None else jnp.where(block == number, added, sums)
    turned = sums.T
    whole = turned[:columns]
    for number in range(1, quarters):
        whole = whole + turned[number * columns : (number + 1) * columns]
    piece_ref[...] = whole.astype(BF16)


def accumulate(message, weight, mine, shard):
    quarters, _, places = weight.shape

    def kernel(*refs):
        accumulate_kernel(shard, *refs)

    return call(
        kernel,
        [
            shaped((LANES // quarters, shard), BF16),
            shaped((quarters, SUBLANES, places), jnp.int32),
        ],
        [VMEM] * 3,
        [VMEM] * 2,
        flops=2 * quarters * shard * places * LANES,
        moved=2 * places * (shard + LANES),
    )(message, weight, mine)


def prepare_kernel(rows_ref, sender_ref):
    places, shard = sender_ref.shape
    slot = rows_ref[lax.axis_index("rep")].astype(F32)
    column = jnp.concatenate([slot] * (LANES // SUBLANES), axis=0).T.astype(jnp.int32)
    for part in range(shard // LANES):
        here = column == ids(column.shape, 1) + part * LANES
        sender_ref[:, part * LANES : (part + 1) * LANES] = jnp.where(here, 1.0, 0.0).astype(BF16)


def prepare(rows, shard):
    places = rows.shape[2]
    return call(
        prepare_kernel, shaped((places, shard), BF16), [VMEM], VMEM, moved=2 * places * shard
    )(rows)


def update_kernel(steps, *refs):
    pieces = refs[: len(steps)]
    sender_ref, table_ref, sums_ref, new_table_ref, new_sums_ref, answer_ref, grad = refs[len(steps) :]
    replicas, columns = len(steps), pieces[0].shape[0]
    for step, piece in zip(steps, pieces):
        start = lax.rem(lax.axis_index("rep") + replicas - step, replicas) * columns
        grad[pl.ds(pl.multiple_of(start, columns), columns), :] = piece[...].astype(F32)
    whole = grad[...]
    sums = sums_ref[...] + jnp.mean(whole * whole, axis=0, keepdims=True)
    new_sums_ref[...] = sums
    step = whole * (LEARN_RATE * lax.rsqrt(sums))
    new_table = table_ref[...] - step.T
    new_table_ref[...] = new_table
    answer_ref[...] = product(sender_ref[...], new_table.astype(BF16)).astype(BF16)


def update(steps, pieces, sender, table_rows, row_accumulators):
    places, shard = sender.shape

    def kernel(*refs):
        update_kernel(steps, *refs)

    new_table, sums, answer = call(
        kernel,
        [shaped((shard, LANES), F32), shaped((1, shard), F32), shaped((places, LANES), BF16)],
        [VMEM] * (len(pieces) + 3),
        [VMEM] * 3,
        scratch=[pltpu.VMEM((LANES, shard), F32)],
        flops=2 * shard * places * LANES,
        moved=2 * places * (shard + LANES),
    )(*pieces, sender, table_rows, row_accumulators.reshape(1, shard))
    return new_table, sums.reshape(shard), answer


def unpack_kernel(places_ref, returned_ref, out_ref):
    matrix = places_ref[lax.axis_index("rep")]
    out_ref[...] = product(matrix, returned_ref[...]).astype(BF16)


def unpack(matrices, returned):
    _, quarter, places = matrices.shape
    return call(
        unpack_kernel,
        shaped((quarter, LANES), BF16),
        [VMEM] * 2,
        VMEM,
        flops=2 * quarter * places * LANES,
        moved=2 * places * (quarter + LANES),
    )(matrices, returned)


def send(piece, step, replicas):
    return lax.ppermute(piece, "rep", [(i, (i + step) % replicas) for i in range(replicas)])


def send_order(replicas):
    return sorted(range(1, replicas), key=lambda step: -min(step, replicas - step))


def on_device(adjacency, grad_out, row_owner, table_slot, table_rows, row_accumulators):
    peers = lax.axis_size("dom")
    replicas = lax.axis_size("rep")
    rows = adjacency.shape[0]
    width = grad_out.shape[2]
    shard = table_rows.shape[0]
    quarter = rows // replicas
    capacity = max(2, 2 * quarter // peers)
    order = send_order(replicas)
    me = lax.axis_index("rep")

    columns, owner, slot = split(grad_out[0], row_owner, table_slot, replicas)
    pieces = [columns[0]] + [send(columns[step], step, replicas) for step in order]
    tile, places, slots, weight, mine = plan(adjacency, owner, slot, replicas, peers, capacity)
    message = propagate(pieces, tile, places, slots, capacity)

    incoming = lax.all_to_all(message, "dom", split_axis=0, concat_axis=0, tiled=True)
    piece, lists = accumulate(incoming, weight, mine, shard)
    pieces = [piece] + [send(piece, step, replicas) for step in order]
    sender = prepare(lists, shard)
    new_table, new_accumulators, answer = update(
        [0, *order], pieces, sender, table_rows, row_accumulators
    )

    returned = lax.all_to_all(
        answer.reshape(peers, capacity, width), "dom", split_axis=0, concat_axis=0, tiled=True
    )
    fresh = unpack(places, returned.reshape(peers * capacity, width))
    pieces = [send(fresh, step, replicas) for step in order]
    fresh_rows = jnp.zeros((rows, width), BF16)
    for step, piece in zip([0, *order], [fresh, *pieces]):
        source = lax.rem(me + replicas - step, replicas) * quarter
        fresh_rows = lax.dynamic_update_slice(fresh_rows, piece, (source, 0))
    return (new_table, new_accumulators, fresh_rows)


def solution(mesh):
    return jax.shard_map(
        on_device,
        mesh=mesh,
        in_specs=(
            P("dom", None),
            P("rep", "dom", None),
            P("dom", None),
            P("dom"),
            P("dom", None),
            P("dom"),
        ),
        out_specs=(P("dom", None), P("dom"), P("dom", None)),
        check_vma=False,
    )
```

time: 103 us -> 83.5 us (0.81)
  blocking collectives: 72.1 us -> 45 us
  matrix products: 16.1 us -> 0 us
  Pallas kernels: 0 us -> 13.4 us
  starting transfers between devices: 4.84 us -> 14.7 us
  waiting for transfers between devices: 5.84 us -> 8.46 us
  other arithmetic: 1.96 us -> 0 us
    all_to_all x2 -> x0, blocking collectives: 23.6 us -> none  [the longest x1 11.9 us: on_device(): lax.all_to_all(jnp.broadcast_to(partial, (replicas, shard, width)), 'rep'...]
    dot_general x9 -> x0, matrix products: 16.1 us -> none  [the longest x3 12.9 us: adjoint(): lax.dot_general(tile, piece, (((0,), (0,)), ((), ())), preferred_element_...]
    ppermute x0 -> x9, starting transfers between devices: none -> 14.7 us  [send(): lax.ppermute(piece, 'rep', [(i, (i + step) % replicas) for i in range(rep...]
    pallas_call x0 -> x7, Pallas kernels: none -> 13.4 us  [the longest x1 5.37 us: propagate(): call(propagate_kernel, shaped((peers, capacity // 2 + 1, 2, LANES), BF16)...]
    ppermute x0 -> x9, waiting for transfers between devices: none -> 8.46 us  [send(): lax.ppermute(piece, 'rep', [(i, (i + step) % replicas) for i in range(rep...]
    all_to_all x1 -> x0, waiting for transfers between devices: 5.84 us -> none  [on_device(): lax.all_to_all(term.reshape(replicas, quarter, width), 'rep', split_axis=...]
    all_to_all x1 -> x0, starting transfers between devices: 4.84 us -> none  [on_device(): lax.all_to_all(term.reshape(replicas, quarter, width), 'rep', split_axis=...]
    all_to_all x1, blocking collectives: 29.6 us -> 25.8 us  [on_device(): lax.all_to_all(message, 'dom', split_axis=0, concat_axis=0, tiled=True)]
  transfers between devices with their start and end apart: 1 -> 9, of which waited for: 1 -> 5; matrix products, arithmetic and copies ran while one was open for 1% -> 0% of each run, Pallas kernels for 0% -> 4%
where the time goes in v4:
time: 83.5 us; the launch traced here: 83.3 us
  blocking collectives  45 us (54%)
  starting transfers between devices  14.7 us (18%)
  Pallas kernels  13.4 us (16%)
  waiting for transfers between devices  8.46 us (10%)
  local copies, waits for them, and re-layouts  0.95 us (1%)
    all_to_all x1, blocking collectives, on_device(): lax.all_to_all(message, 'dom', split_axis=0, concat_axis=0, tiled=True)  25.8 us
    all_to_all x1, blocking collectives, on_device(): lax.all_to_all(answer.reshape(peers, capacity, width), 'dom', split_axis=...  19.2 us
    ppermute x9, starting transfers between devices, send(): lax.ppermute(piece, 'rep', [(i, (i + step) % replicas) for i in range(rep...  14.7 us
    ppermute x9, waiting for transfers between devices, send(): lax.ppermute(piece, 'rep', [(i, (i + step) % replicas) for i in range(rep...  8.46 us
    pallas_call x1, Pallas kernels, propagate(): call(propagate_kernel, shaped((peers, capacity // 2 + 1, 2, LANES), BF16)...  5.37 us
    pallas_call x1, Pallas kernels, plan(): call(kernel, [pltpu.VMEM(adjacency.shape, BF16), shaped((quarters, rows /...  3.39 us
  transfers between devices with their start and end apart: 9, of which 5 were waited for; matrix products, arithmetic and copies ran while one was open for 0% of the time, Pallas kernels for 4%

profile of v4, /device:TPU:1, one launch (start us, length us, event | category | flops | bytes accessed | tf_op | source)
XLA Modules:
  0.0 83.3 jit_solution(6901350664386968946)
XLA Ops:
  0.6 1.3 %shard_map.85 = (bf16[32,2048]{1,0:T(8,128)(2,1)S(1)}, bf16[32,2048]{1,0:T(8,128)(2,1)S(1)}, bf16[32,2048]{1,0:T(8,128)(2,1)S(1)}, bf16[32,2048]{1,0:T(8,128)(2,...) custom-call(bf16[2048,128]{1,0:T(8,128)(2,1)} %bitcast.10, s32[1,2048]{1,0:T(1,128)} %bitcast.11, s32[1,2048]{1,0:T(1,128)} %bitcast.12), custom_call_target="tpu_custom_call" | custom-call | tf_op jit(solution)/shard_map/pallas_call | solution.py:79
  2.0 3.7 %collective-permute-start = (bf16[32,2048]{1,0:T(8,128)(2,1)S(1)}, bf16[32,2048]{1,0:T(8,128)(2,1)S(1)}, u32[]{:S(2)}, u32[]{:S(2)}) collective-permute-start(bf16[32,2048]{1,0:T(8,128)(2,1)S(1)} %get-tuple-element.20), channel_id=1, source_target_pairs={{0,2},{1,3},{2,0},{3,1},{4,6},{5,7},{6,4},{7,5},{8,10},{9,11},{10,... | collective-permute-start | bytes 393224 | tf_op jit(solution)/shard_map/ppermute | solution.py:314
  5.6 0.3 collective-permute-start.1
  6.0 2.4 %collective-permute-start.2 = (bf16[32,2048]{1,0:T(8,128)(2,1)S(1)}, bf16[32,2048]{1,0:T(8,128)(2,1)S(1)}, u32[]{:S(2)}, u32[]{:S(2)}) collective-permute-start(bf16[32,2048]{1,0:T(8,128)(2,1)S(1)} %get-tuple-element.22), channel_id=1, source_target_pairs={{0,3},{1,0},{2,1},{3,2},{4,7},{5,4},{6,5},{7,6},{8,11},{9,8},{10,9... | collective-permute-start | bytes 393224 | tf_op jit(solution)/shard_map/ppermute | solution.py:314
  8.3 3.4 %shard_map.86 = (bf16[2048,2048]{1,0:T(8,128)(2,1)S(1)}, bf16[4,512,1024]{2,1,0:T(8,128)(2,1)S(1)}, bf16[64,128]{1,0:T(8,128)(2,1)S(1)}, bf16[4,128,1024]{2,1,0:T(8,128)(2,1)S(1)}, f32[64,1024]{1,0:T(8,128)S(1)}) custom-call(bf16[2048,2048]{1,0:T(8,128)(2,1)} %refs_0_.1, s32[1,2048]{1,0:T(1,128)S(1)} %get-tuple-element.23.refs_1_, ...), custom_call_target="tpu_custom_call" | custom-call | tf_op jit(solution)/shard_map/pallas_call | solution.py:150
  11.7 0.0 collective-permute-done.refs_1_
  11.7 1.1 %collective-permute-done.1.refs_2_ = bf16[32,2048]{1,0:T(8,128)(2,1)S(1)} collective-permute-done((bf16[32,2048]{1,0:T(8,128)(2,1)S(1)}, bf16[32,2048]{1,0:T(8,128)(2,1)S(1)}, u32[]{:S(2)}, u32[]{:S(2)}) %collective-permute-start.1) | collective-permute-done | bytes 131104 | tf_op jit(solution)/shard_map/ppermute | solution.py:314
  12.8 0.0 collective-permute-done.2.refs_3_
  12.9 5.4 %shard_map.87 = bf16[64,9,2,128]{3,2,1,0:T(2,128)(2,1)S(1)} custom-call(bf16[32,2048]{1,0:T(8,128)(2,1)S(1)} %get-tuple-element.19.refs_0_, bf16[32,2048]{1,0:T(8,128)(2,1)S(1)} %collective-permute-done.refs_1_, bf16[32,2048]{1,0:T(8,128)(2,1)S(1)} %collective-permute-done.1.refs_2_, bf16[32,2048]{1,0:T(8,128)(2,1)S(1)} %collective-permute-done.2.refs_3_, ...), custom_call_target="tpu_custom_call" | custom-call | flops 3221225472 | bytes 8388608 | tf_op jit(solution)/shard_map/pallas_call | solution.py:192
  18.2 25.8 %all_to_all.10.refs_0_ = bf16[64,9,2,128]{3,2,1,0:T(2,128)(2,1)S(1)} all-to-all(bf16[64,9,2,128]{3,2,1,0:T(2,128)(2,1)S(1)} %shard_map.87), channel_id=1, replica_groups=mesh['dom'=64,'rep'=4] {'dom'}, dimensions={0} | all-to-all | bytes 589824 | tf_op jit(solution)/shard_map/all_to_all | solution.py:337
  44.0 1.6 %shard_map.88 = (bf16[32,512]{1,0:T(8,128)(2,1)S(1)}, s32[4,8,1024]{2,1,0:T(8,128)S(1)}) custom-call(bf16[64,9,2,128]{3,2,1,0:T(2,128)(2,1)S(1)} %all_to_all.10.refs_0_, bf16[4,128,1024]{2,1,0:T(8,128)(2,1)S(1)} %get-tuple-element.28.refs_1_, f32[64,1024]{1,0:T(8,128)S(1)} %get-tuple-element.29.refs_2_), custom_call_target="tpu_custom_call" | custom-call | flops 536870912 | bytes 1310720 | tf_op jit(solution)/shard_map/pallas_call | solution.py:233
  45.7 1.6 %collective-permute-start.3 = (bf16[32,512]{1,0:T(8,128)(2,1)S(1)}, bf16[32,512]{1,0:T(8,128)(2,1)S(1)}, u32[]{:S(2)}, u32[]{:S(2)}) collective-permute-start(bf16[32,512]{1,0:T(8,128)(2,1)S(1)} %get-tuple-element.30.refs_0_), channel_id=1, source_target_pairs={{0,2},{1,3},{2,0},{3,1},{4,6},{5,7},{6,4},{7,5},{8,10},{9,11},{10,... | collective-permute-start | bytes 98312 | tf_op jit(solution)/shard_map/ppermute | solution.py:314
  47.3 1.7 %collective-permute-start.4 = (bf16[32,512]{1,0:T(8,128)(2,1)S(1)}, bf16[32,512]{1,0:T(8,128)(2,1)S(1)}, u32[]{:S(2)}, u32[]{:S(2)}) collective-permute-start(bf16[32,512]{1,0:T(8,128)(2,1)S(1)} %get-tuple-element.30.refs_0_), channel_id=1, source_target_pairs={{0,1},{1,2},{2,3},{3,0},{4,5},{5,6},{6,7},{7,4},{8,9},{9,10},{10,1... | collective-permute-start | bytes 98312 | tf_op jit(solution)/shard_map/ppermute | solution.py:314
  49.0 1.0 %collective-permute-start.5 = (bf16[32,512]{1,0:T(8,128)(2,1)S(1)}, bf16[32,512]{1,0:T(8,128)(2,1)S(1)}, u32[]{:S(2)}, u32[]{:S(2)}) collective-permute-start(bf16[32,512]{1,0:T(8,128)(2,1)S(1)} %get-tuple-element.30.refs_0_), channel_id=1, source_target_pairs={{0,3},{1,0},{2,1},{3,2},{4,7},{5,4},{6,5},{7,6},{8,11},{9,8},{10,9... | collective-permute-start | bytes 98312 | tf_op jit(solution)/shard_map/ppermute | solution.py:314
  50.0 0.3 shard_map.89.refs_4_
  50.3 0.0 collective-permute-done.3.refs_1_
  50.3 1.0 %collective-permute-done.4.refs_2_ = bf16[32,512]{1,0:T(8,128)(2,1)S(1)} collective-permute-done((bf16[32,512]{1,0:T(8,128)(2,1)S(1)}, bf16[32,512]{1,0:T(8,128)(2,1)S(1)}, u32[]{:S(2)}, u32[]{:S(2)}) %collective-permute-start.4) | collective-permute-done | bytes 32800 | tf_op jit(solution)/shard_map/ppermute | solution.py:314
  51.3 0.7 collective-permute-done.5.refs_3_
  52.0 0.0 copy-done
  52.0 0.0 copy-done.1
  52.0 0.9 %shard_map.90 = (f32[512,128]{1,0:T(8,128)}, f32[1,512]{1,0:T(1,128)}, bf16[1024,128]{1,0:T(8,128)(2,1)S(1)}) custom-call(bf16[32,512]{1,0:T(8,128)(2,1)S(1)} %get-tuple-element.30.refs_0_, bf16[32,512]{1,0:T(8,128)(2,1)S(1)} %collective-permute-done.3.refs_1_, bf16[32,512]{1,0:T(8,128)(2,1)S(1)} %collective-permute-done.4.refs_2_, ...), custom_call_target="tpu_custom_call" | custom-call | flops 134217728 | bytes 1310720 | tf_op jit(solution)/shard_map/pallas_call | solution.py:284
  52.9 19.2 %all_to_all.11 = bf16[64,16,128]{2,1,0:T(8,128)(2,1)S(1)} all-to-all(bf16[64,16,128]{2,1,0:T(8,128)(2,1)S(1)} %bitcast.8), channel_id=1, replica_groups=mesh['dom'=64,'rep'=4] {'dom'}, dimensions={0} | all-to-all | bytes 524288 | tf_op jit(solution)/shard_map/all_to_all | solution.py:345
  72.2 0.4 shard_map.91
  72.6 1.4 %collective-permute-start.6 = (bf16[512,128]{1,0:T(8,128)(2,1)S(1)}, bf16[512,128]{1,0:T(8,128)(2,1)S(1)}, u32[]{:S(2)}, u32[]{:S(2)}) collective-permute-start(bf16[512,128]{1,0:T(8,128)(2,1)S(1)} %shard_map.91), channel_id=1, source_target_pairs={{0,2},{1,3},{2,0},{3,1},{4,6},{5,7},{6,4},{7,5},{8,10},{9,11},{10,... | collective-permute-start | bytes 393224 | tf_op jit(solution)/shard_map/ppermute | solution.py:314
  74.0 1.5 %collective-permute-start.7 = (bf16[512,128]{1,0:T(8,128)(2,1)S(1)}, bf16[512,128]{1,0:T(8,128)(2,1)S(1)}, u32[]{:S(2)}, u32[]{:S(2)}) collective-permute-start(bf16[512,128]{1,0:T(8,128)(2,1)S(1)} %shard_map.91), channel_id=1, source_target_pairs={{0,1},{1,2},{2,3},{3,0},{4,5},{5,6},{6,7},{7,4},{8,9},{9,10},{10,1... | collective-permute-start | bytes 393224 | tf_op jit(solution)/shard_map/ppermute | solution.py:314
  75.5 1.2 %collective-permute-start.8 = (bf16[512,128]{1,0:T(8,128)(2,1)S(1)}, bf16[512,128]{1,0:T(8,128)(2,1)S(1)}, u32[]{:S(2)}, u32[]{:S(2)}) collective-permute-start(bf16[512,128]{1,0:T(8,128)(2,1)S(1)} %shard_map.91), channel_id=1, source_target_pairs={{0,3},{1,0},{2,1},{3,2},{4,7},{5,4},{6,5},{7,6},{8,11},{9,8},{10,9... | collective-permute-start | bytes 393224 | tf_op jit(solution)/shard_map/ppermute | solution.py:314
  76.7 0.1 broadcast_in_dim.3
  76.8 2.2 %collective-permute-done.6 = bf16[512,128]{1,0:T(8,128)(2,1)S(1)} collective-permute-done((bf16[512,128]{1,0:T(8,128)(2,1)S(1)}, bf16[512,128]{1,0:T(8,128)(2,1)S(1)}, u32[]{:S(2)}, u32[]{:S(2)}) %collective-permute-start.6) | collective-permute-done | bytes 131104 | tf_op jit(solution)/shard_map/ppermute | solution.py:314
  79.1 3.4 %collective-permute-done.7 = bf16[512,128]{1,0:T(8,128)(2,1)S(1)} collective-permute-done((bf16[512,128]{1,0:T(8,128)(2,1)S(1)}, bf16[512,128]{1,0:T(8,128)(2,1)S(1)}, u32[]{:S(2)}, u32[]{:S(2)}) %collective-permute-start.7) | collective-permute-done | bytes 131104 | tf_op jit(solution)/shard_map/ppermute | solution.py:314
  82.4 0.0 collective-permute-done.8
  82.5 0.0 copy-start.2
  82.5 0.8 copy-done.2
  (6 shorter events, 0.1 us)
Async XLA Ops:
  2.0 9.7 %collective-permute-start = (bf16[32,2048]{1,0:T(8,128)(2,1)S(1)}, bf16[32,2048]{1,0:T(8,128)(2,1)S(1)}, u32[]{:S(2)}, u32[]{:S(2)}) collective-permute-start(bf16[32,2048]{1,0:T(8,128)(2,1)S(1)} %get-tuple-element.20), channel_id=1, source_target_pairs={{0,2},{1,3},{2,0},{3,1},{4,6},{5,7},{6,4},{7,5},{8,10},{9,11},{10,... | collective-permute-start | bytes 393224 | tf_op jit(solution)/shard_map/ppermute | solution.py:314
  5.6 7.2 %collective-permute-start.1 = (bf16[32,2048]{1,0:T(8,128)(2,1)S(1)}, bf16[32,2048]{1,0:T(8,128)(2,1)S(1)}, u32[]{:S(2)}, u32[]{:S(2)}) collective-permute-start(bf16[32,2048]{1,0:T(8,128)(2,1)S(1)} %get-tuple-element.21), channel_id=1, source_target_pairs={{0,1},{1,2},{2,3},{3,0},{4,5},{5,6},{6,7},{7,4},{8,9},{9,10},{10,1... | collective-permute-start | bytes 393224 | tf_op jit(solution)/shard_map/ppermute | solution.py:314
  6.0 6.9 %collective-permute-start.2 = (bf16[32,2048]{1,0:T(8,128)(2,1)S(1)}, bf16[32,2048]{1,0:T(8,128)(2,1)S(1)}, u32[]{:S(2)}, u32[]{:S(2)}) collective-permute-start(bf16[32,2048]{1,0:T(8,128)(2,1)S(1)} %get-tuple-element.22), channel_id=1, source_target_pairs={{0,3},{1,0},{2,1},{3,2},{4,7},{5,4},{6,5},{7,6},{8,11},{9,8},{10,9... | collective-permute-start | bytes 393224 | tf_op jit(solution)/shard_map/ppermute | solution.py:314
  12.8 39.2 %copy-start = (f32[512,128]{1,0:T(8,128)S(1)}, f32[512,128]{1,0:T(8,128)}, u32[]{:S(2)}) copy-start(f32[512,128]{1,0:T(8,128)} %refs_5_.1) | copy-start | bytes 786436
  12.8 39.2 %copy-start.1 = (f32[512]{0:T(512)S(1)}, f32[512]{0:T(512)}, u32[]{:S(2)}) copy-start(f32[512]{0:T(512)} %param.11) | copy-start | bytes 6148
  45.7 4.6 %collective-permute-start.3 = (bf16[32,512]{1,0:T(8,128)(2,1)S(1)}, bf16[32,512]{1,0:T(8,128)(2,1)S(1)}, u32[]{:S(2)}, u32[]{:S(2)}) collective-permute-start(bf16[32,512]{1,0:T(8,128)(2,1)S(1)} %get-tuple-element.30.refs_0_), channel_id=1, source_target_pairs={{0,2},{1,3},{2,0},{3,1},{4,6},{5,7},{6,4},{7,5},{8,10},{9,11},{10,... | collective-permute-start | bytes 98312 | tf_op jit(solution)/shard_map/ppermute | solution.py:314
  47.3 4.0 %collective-permute-start.4 = (bf16[32,512]{1,0:T(8,128)(2,1)S(1)}, bf16[32,512]{1,0:T(8,128)(2,1)S(1)}, u32[]{:S(2)}, u32[]{:S(2)}) collective-permute-start(bf16[32,512]{1,0:T(8,128)(2,1)S(1)} %get-tuple-element.30.refs_0_), channel_id=1, source_target_pairs={{0,1},{1,2},{2,3},{3,0},{4,5},{5,6},{6,7},{7,4},{8,9},{9,10},{10,1... | collective-permute-start | bytes 98312 | tf_op jit(solution)/shard_map/ppermute | solution.py:314
  49.0 3.1 %collective-permute-start.5 = (bf16[32,512]{1,0:T(8,128)(2,1)S(1)}, bf16[32,512]{1,0:T(8,128)(2,1)S(1)}, u32[]{:S(2)}, u32[]{:S(2)}) collective-permute-start(bf16[32,512]{1,0:T(8,128)(2,1)S(1)} %get-tuple-element.30.refs_0_), channel_id=1, source_target_pairs={{0,3},{1,0},{2,1},{3,2},{4,7},{5,4},{6,5},{7,6},{8,11},{9,8},{10,9... | collective-permute-start | bytes 98312 | tf_op jit(solution)/shard_map/ppermute | solution.py:314
  72.6 6.4 %collective-permute-start.6 = (bf16[512,128]{1,0:T(8,128)(2,1)S(1)}, bf16[512,128]{1,0:T(8,128)(2,1)S(1)}, u32[]{:S(2)}, u32[]{:S(2)}) collective-permute-start(bf16[512,128]{1,0:T(8,128)(2,1)S(1)} %shard_map.91), channel_id=1, source_target_pairs={{0,2},{1,3},{2,0},{3,1},{4,6},{5,7},{6,4},{7,5},{8,10},{9,11},{10,... | collective-permute-start | bytes 393224 | tf_op jit(solution)/shard_map/ppermute | solution.py:314
  74.0 8.4 %collective-permute-start.7 = (bf16[512,128]{1,0:T(8,128)(2,1)S(1)}, bf16[512,128]{1,0:T(8,128)(2,1)S(1)}, u32[]{:S(2)}, u32[]{:S(2)}) collective-permute-start(bf16[512,128]{1,0:T(8,128)(2,1)S(1)} %shard_map.91), channel_id=1, source_target_pairs={{0,1},{1,2},{2,3},{3,0},{4,5},{5,6},{6,7},{7,4},{8,9},{9,10},{10,1... | collective-permute-start | bytes 393224 | tf_op jit(solution)/shard_map/ppermute | solution.py:314
  75.5 7.0 %collective-permute-start.8 = (bf16[512,128]{1,0:T(8,128)(2,1)S(1)}, bf16[512,128]{1,0:T(8,128)(2,1)S(1)}, u32[]{:S(2)}, u32[]{:S(2)}) collective-permute-start(bf16[512,128]{1,0:T(8,128)(2,1)S(1)} %shard_map.91), channel_id=1, source_target_pairs={{0,3},{1,0},{2,1},{3,2},{4,7},{5,4},{6,5},{7,6},{8,11},{9,8},{10,9... | collective-permute-start | bytes 393224 | tf_op jit(solution)/shard_map/ppermute | solution.py:314
  82.5 0.8 copy-start.2

commit v5 on v4

--- a/solution.py
+++ b/solution.py
@@ -175,13 +175,15 @@
     quarters, quarter, _ = places_ref.shape
     packed = jnp.concatenate(
         [
-            product(term[:, number * quarter : (number + 1) * quarter], places_ref[number])
+            product(
+                term[:, number * quarter : (number + 1) * quarter], places_ref[number]
+            ).astype(BF16)
             for number in range(quarters)
         ],
         axis=0,
     )
     peers, pairs = out_ref.shape[:2]
-    out_ref[:, : pairs - 1] = packed.T.astype(BF16).reshape(peers, pairs - 1, 2, LANES)
+    out_ref[:, : pairs - 1] = packed.T.reshape(peers, pairs - 1, 2, LANES)
     lists = slots_ref[...]
     out_ref[:, pairs - 1] = jnp.broadcast_to(lists[:, None, :], (peers, 2, LANES))
 
@@ -207,12 +209,14 @@
     data = message_ref[:, : pairs - 1].reshape(places, LANES)
     block = ids((shard, LANES), 1) // columns
     index = ids((shard, places), 0).astype(jnp.int16)
+    slots = []
+    for number in range(quarters):
+        lists = product(digits, weight_ref[number])
+        slots.append(jnp.sum(lists * mine_ref[...], axis=0, keepdims=True).astype(jnp.int32))
+        rows_ref[number] = jnp.broadcast_to(slots[number], rows_ref.shape[1:])
     sums = None
     for number in range(quarters):
-        lists = product(digits, weight_ref[number])
-        slot = jnp.sum(lists * mine_ref[...], axis=0, keepdims=True).astype(jnp.int32)
-        rows_ref[number] = jnp.broadcast_to(slot, rows_ref.shape[1:])
-        wide = jnp.broadcast_to(slot, (PACKED, places)).astype(jnp.int16)
+        wide = jnp.broadcast_to(slots[number], (PACKED, places)).astype(jnp.int16)
         hot = index == jnp.concatenate([wide] * (shard // PACKED), axis=0)
         receiver = jnp.where(hot, jnp.ones(hot.shape, BF16), jnp.zeros(hot.shape, BF16))
         added = product(receiver, data)
@@ -283,7 +287,11 @@
 
     new_table, sums, answer = call(
         kernel,
-        [shaped((shard, LANES), F32), shaped((1, shard), F32), shaped((places, LANES), BF16)],
+        [
+            pltpu.VMEM((shard, LANES), F32),
+            pltpu.VMEM((1, shard), F32),
+            shaped((places, LANES), BF16),
+        ],
         [VMEM] * (len(pieces) + 3),
         [VMEM] * 3,
         scratch=[pltpu.VMEM((LANES, shard), F32)],

time: 83.5 us -> 82.7 us (level)
  waiting for transfers between devices: 8.46 us -> 6.87 us
  local copies, waits for them, and re-layouts: 0.95 us -> 2.23 us
    ppermute x9, waiting for transfers between devices: 8.46 us -> 6.87 us  [send(): lax.ppermute(piece, 'rep', [(i, (i + step) % replicas) for i in range(rep...]
    unnamed x6 -> x8, local copies, waits for them, and re-layouts: 0.8 us -> 2.08 us
  transfers between devices with their start and end apart: 9 -> 9, of which waited for: 5 -> 5; matrix products, arithmetic and copies ran while one was open for 0% -> 2% of each run, Pallas kernels for 4% -> 4%
where the time goes in v5:
time: 82.7 us; the launch traced here: 82.5 us
  blocking collectives  45 us (54%)
  starting transfers between devices  14.7 us (18%)
  Pallas kernels  13 us (16%)
  waiting for transfers between devices  6.87 us (8%)
  local copies, waits for them, and re-layouts  2.23 us (3%)
    all_to_all x1, blocking collectives, on_device(): lax.all_to_all(message, 'dom', split_axis=0, concat_axis=0, tiled=True)  25.8 us
    all_to_all x1, blocking collectives, on_device(): lax.all_to_all(answer.reshape(peers, capacity, width), 'dom', split_axis=...  19.2 us
    ppermute x9, starting transfers between devices, send(): lax.ppermute(piece, 'rep', [(i, (i + step) % replicas) for i in range(rep...  14.7 us
    ppermute x9, waiting for transfers between devices, send(): lax.ppermute(piece, 'rep', [(i, (i + step) % replicas) for i in range(rep...  6.87 us
    pallas_call x1, Pallas kernels, propagate(): call(propagate_kernel, shaped((peers, capacity // 2 + 1, 2, LANES), BF16)...  5.35 us
    pallas_call x1, Pallas kernels, plan(): call(kernel, [pltpu.VMEM(adjacency.shape, BF16), shaped((quarters, rows /...  3.39 us
    unnamed x8, local copies, waits for them, and re-layouts  2.08 us
  transfers between devices with their start and end apart: 9, of which 5 were waited for; matrix products, arithmetic and copies ran while one was open for 2% of the time, Pallas kernels for 4%

profile of v5, /device:TPU:1, one launch (start us, length us, event | category | flops | bytes accessed | tf_op | source)
XLA Modules:
  0.0 82.5 jit_solution(11194343789849735303)
XLA Ops:
  0.6 1.3 %shard_map.85 = (bf16[32,2048]{1,0:T(8,128)(2,1)S(1)}, bf16[32,2048]{1,0:T(8,128)(2,1)S(1)}, bf16[32,2048]{1,0:T(8,128)(2,1)S(1)}, bf16[32,2048]{1,0:T(8,128)(2,...) custom-call(bf16[2048,128]{1,0:T(8,128)(2,1)} %bitcast.11, s32[1,2048]{1,0:T(1,128)} %bitcast.12, s32[1,2048]{1,0:T(1,128)} %bitcast.13), custom_call_target="tpu_custom_call" | custom-call | tf_op jit(solution)/shard_map/pallas_call | solution.py:79
  2.0 3.7 %collective-permute-start = (bf16[32,2048]{1,0:T(8,128)(2,1)S(1)}, bf16[32,2048]{1,0:T(8,128)(2,1)S(1)}, u32[]{:S(2)}, u32[]{:S(2)}) collective-permute-start(bf16[32,2048]{1,0:T(8,128)(2,1)S(1)} %get-tuple-element.20), channel_id=1, source_target_pairs={{0,2},{1,3},{2,0},{3,1},{4,6},{5,7},{6,4},{7,5},{8,10},{9,11},{10,... | collective-permute-start | bytes 393224 | tf_op jit(solution)/shard_map/ppermute | solution.py:322
  5.6 0.3 collective-permute-start.1
  6.0 2.4 %collective-permute-start.2 = (bf16[32,2048]{1,0:T(8,128)(2,1)S(1)}, bf16[32,2048]{1,0:T(8,128)(2,1)S(1)}, u32[]{:S(2)}, u32[]{:S(2)}) collective-permute-start(bf16[32,2048]{1,0:T(8,128)(2,1)S(1)} %get-tuple-element.22), channel_id=1, source_target_pairs={{0,3},{1,0},{2,1},{3,2},{4,7},{5,4},{6,5},{7,6},{8,11},{9,8},{10,9... | collective-permute-start | bytes 393224 | tf_op jit(solution)/shard_map/ppermute | solution.py:322
  8.3 3.4 %shard_map.86 = (bf16[2048,2048]{1,0:T(8,128)(2,1)S(1)}, bf16[4,512,1024]{2,1,0:T(8,128)(2,1)S(1)}, bf16[64,128]{1,0:T(8,128)(2,1)S(1)}, bf16[4,128,1024]{2,1,0:T(8,128)(2,1)S(1)}, f32[64,1024]{1,0:T(8,128)S(1)}) custom-call(bf16[2048,2048]{1,0:T(8,128)(2,1)} %refs_0_.1, s32[1,2048]{1,0:T(1,128)S(1)} %get-tuple-element.23.refs_1_, ...), custom_call_target="tpu_custom_call" | custom-call | tf_op jit(solution)/shard_map/pallas_call | solution.py:150
  11.7 0.0 collective-permute-done.refs_1_
  11.7 1.1 %collective-permute-done.1.refs_2_ = bf16[32,2048]{1,0:T(8,128)(2,1)S(1)} collective-permute-done((bf16[32,2048]{1,0:T(8,128)(2,1)S(1)}, bf16[32,2048]{1,0:T(8,128)(2,1)S(1)}, u32[]{:S(2)}, u32[]{:S(2)}) %collective-permute-start.1) | collective-permute-done | bytes 131104 | tf_op jit(solution)/shard_map/ppermute | solution.py:322
  12.8 0.0 collective-permute-done.2.refs_3_
  12.9 5.4 %shard_map.87 = bf16[64,9,2,128]{3,2,1,0:T(2,128)(2,1)S(1)} custom-call(bf16[32,2048]{1,0:T(8,128)(2,1)S(1)} %get-tuple-element.19.refs_0_, bf16[32,2048]{1,0:T(8,128)(2,1)S(1)} %collective-permute-done.refs_1_, bf16[32,2048]{1,0:T(8,128)(2,1)S(1)} %collective-permute-done.1.refs_2_, bf16[32,2048]{1,0:T(8,128)(2,1)S(1)} %collective-permute-done.2.refs_3_, ...), custom_call_target="tpu_custom_call" | custom-call | flops 3221225472 | bytes 8388608 | tf_op jit(solution)/shard_map/pallas_call | solution.py:194
  18.2 25.8 %all_to_all.10.refs_0_ = bf16[64,9,2,128]{3,2,1,0:T(2,128)(2,1)S(1)} all-to-all(bf16[64,9,2,128]{3,2,1,0:T(2,128)(2,1)S(1)} %shard_map.87), channel_id=1, replica_groups=mesh['dom'=64,'rep'=4] {'dom'}, dimensions={0} | all-to-all | bytes 589824 | tf_op jit(solution)/shard_map/all_to_all | solution.py:345
  44.0 1.5 %shard_map.88 = (bf16[32,512]{1,0:T(8,128)(2,1)S(1)}, s32[4,8,1024]{2,1,0:T(8,128)S(1)}) custom-call(bf16[64,9,2,128]{3,2,1,0:T(2,128)(2,1)S(1)} %all_to_all.10.refs_0_, bf16[4,128,1024]{2,1,0:T(8,128)(2,1)S(1)} %get-tuple-element.28.refs_1_, f32[64,1024]{1,0:T(8,128)S(1)} %get-tuple-element.29.refs_2_), custom_call_target="tpu_custom_call" | custom-call | flops 536870912 | bytes 1310720 | tf_op jit(solution)/shard_map/pallas_call | solution.py:237
  45.5 1.6 %collective-permute-start.3 = (bf16[32,512]{1,0:T(8,128)(2,1)S(1)}, bf16[32,512]{1,0:T(8,128)(2,1)S(1)}, u32[]{:S(2)}, u32[]{:S(2)}) collective-permute-start(bf16[32,512]{1,0:T(8,128)(2,1)S(1)} %get-tuple-element.30.refs_0_), channel_id=1, source_target_pairs={{0,2},{1,3},{2,0},{3,1},{4,6},{5,7},{6,4},{7,5},{8,10},{9,11},{10,... | collective-permute-start | bytes 98312 | tf_op jit(solution)/shard_map/ppermute | solution.py:322
  47.2 1.7 %collective-permute-start.4 = (bf16[32,512]{1,0:T(8,128)(2,1)S(1)}, bf16[32,512]{1,0:T(8,128)(2,1)S(1)}, u32[]{:S(2)}, u32[]{:S(2)}) collective-permute-start(bf16[32,512]{1,0:T(8,128)(2,1)S(1)} %get-tuple-element.30.refs_0_), channel_id=1, source_target_pairs={{0,1},{1,2},{2,3},{3,0},{4,5},{5,6},{6,7},{7,4},{8,9},{9,10},{10,1... | collective-permute-start | bytes 98312 | tf_op jit(solution)/shard_map/ppermute | solution.py:322
  48.8 1.0 %collective-permute-start.5 = (bf16[32,512]{1,0:T(8,128)(2,1)S(1)}, bf16[32,512]{1,0:T(8,128)(2,1)S(1)}, u32[]{:S(2)}, u32[]{:S(2)}) collective-permute-start(bf16[32,512]{1,0:T(8,128)(2,1)S(1)} %get-tuple-element.30.refs_0_), channel_id=1, source_target_pairs={{0,3},{1,0},{2,1},{3,2},{4,7},{5,4},{6,5},{7,6},{8,11},{9,8},{10,9... | collective-permute-start | bytes 98312 | tf_op jit(solution)/shard_map/ppermute | solution.py:322
  49.8 0.3 shard_map.89.refs_4_
  50.1 0.0 collective-permute-done.3.refs_1_
  50.2 1.0 %collective-permute-done.4.refs_2_ = bf16[32,512]{1,0:T(8,128)(2,1)S(1)} collective-permute-done((bf16[32,512]{1,0:T(8,128)(2,1)S(1)}, bf16[32,512]{1,0:T(8,128)(2,1)S(1)}, u32[]{:S(2)}, u32[]{:S(2)}) %collective-permute-start.4) | collective-permute-done | bytes 32800 | tf_op jit(solution)/shard_map/ppermute | solution.py:322
  51.1 0.7 collective-permute-done.5.refs_3_
  51.9 0.6 shard_map.90
  52.5 19.2 %all_to_all.11 = bf16[64,16,128]{2,1,0:T(8,128)(2,1)S(1)} all-to-all(bf16[64,16,128]{2,1,0:T(8,128)(2,1)S(1)} %bitcast.9), channel_id=1, replica_groups=mesh['dom'=64,'rep'=4] {'dom'}, dimensions={0} | all-to-all | bytes 524288 | tf_op jit(solution)/shard_map/all_to_all | solution.py:353
  71.7 0.4 shard_map.91
  72.2 1.4 %collective-permute-start.6 = (bf16[512,128]{1,0:T(8,128)(2,1)S(1)}, bf16[512,128]{1,0:T(8,128)(2,1)S(1)}, u32[]{:S(2)}, u32[]{:S(2)}) collective-permute-start(bf16[512,128]{1,0:T(8,128)(2,1)S(1)} %shard_map.91), channel_id=1, source_target_pairs={{0,2},{1,3},{2,0},{3,1},{4,6},{5,7},{6,4},{7,5},{8,10},{9,11},{10,... | collective-permute-start | bytes 393224 | tf_op jit(solution)/shard_map/ppermute | solution.py:322
  73.6 0.7 copy.13
  74.3 0.6 copy.14
  74.8 1.5 %collective-permute-start.7 = (bf16[512,128]{1,0:T(8,128)(2,1)S(1)}, bf16[512,128]{1,0:T(8,128)(2,1)S(1)}, u32[]{:S(2)}, u32[]{:S(2)}) collective-permute-start(bf16[512,128]{1,0:T(8,128)(2,1)S(1)} %shard_map.91), channel_id=1, source_target_pairs={{0,1},{1,2},{2,3},{3,0},{4,5},{5,6},{6,7},{7,4},{8,9},{9,10},{10,1... | collective-permute-start | bytes 393224 | tf_op jit(solution)/shard_map/ppermute | solution.py:322
  76.3 1.2 %collective-permute-start.8 = (bf16[512,128]{1,0:T(8,128)(2,1)S(1)}, bf16[512,128]{1,0:T(8,128)(2,1)S(1)}, u32[]{:S(2)}, u32[]{:S(2)}) collective-permute-start(bf16[512,128]{1,0:T(8,128)(2,1)S(1)} %shard_map.91), channel_id=1, source_target_pairs={{0,3},{1,0},{2,1},{3,2},{4,7},{5,4},{6,5},{7,6},{8,11},{9,8},{10,9... | collective-permute-start | bytes 393224 | tf_op jit(solution)/shard_map/ppermute | solution.py:322
  77.5 0.1 broadcast_in_dim.3
  77.6 1.0 %collective-permute-done.6 = bf16[512,128]{1,0:T(8,128)(2,1)S(1)} collective-permute-done((bf16[512,128]{1,0:T(8,128)(2,1)S(1)}, bf16[512,128]{1,0:T(8,128)(2,1)S(1)}, u32[]{:S(2)}, u32[]{:S(2)}) %collective-permute-start.6) | collective-permute-done | bytes 131104 | tf_op jit(solution)/shard_map/ppermute | solution.py:322
  78.6 3.0 %collective-permute-done.7 = bf16[512,128]{1,0:T(8,128)(2,1)S(1)} collective-permute-done((bf16[512,128]{1,0:T(8,128)(2,1)S(1)}, bf16[512,128]{1,0:T(8,128)(2,1)S(1)}, u32[]{:S(2)}, u32[]{:S(2)}) %collective-permute-start.7) | collective-permute-done | bytes 131104 | tf_op jit(solution)/shard_map/ppermute | solution.py:322
  81.7 0.0 collective-permute-done.8
  81.7 0.0 copy-start.2
  81.7 0.8 copy-done.2
  (8 shorter events, 0.1 us)
Async XLA Ops:
  2.0 9.7 %collective-permute-start = (bf16[32,2048]{1,0:T(8,128)(2,1)S(1)}, bf16[32,2048]{1,0:T(8,128)(2,1)S(1)}, u32[]{:S(2)}, u32[]{:S(2)}) collective-permute-start(bf16[32,2048]{1,0:T(8,128)(2,1)S(1)} %get-tuple-element.20), channel_id=1, source_target_pairs={{0,2},{1,3},{2,0},{3,1},{4,6},{5,7},{6,4},{7,5},{8,10},{9,11},{10,... | collective-permute-start | bytes 393224 | tf_op jit(solution)/shard_map/ppermute | solution.py:322
  5.6 7.2 %collective-permute-start.1 = (bf16[32,2048]{1,0:T(8,128)(2,1)S(1)}, bf16[32,2048]{1,0:T(8,128)(2,1)S(1)}, u32[]{:S(2)}, u32[]{:S(2)}) collective-permute-start(bf16[32,2048]{1,0:T(8,128)(2,1)S(1)} %get-tuple-element.21), channel_id=1, source_target_pairs={{0,1},{1,2},{2,3},{3,0},{4,5},{5,6},{6,7},{7,4},{8,9},{9,10},{10,1... | collective-permute-start | bytes 393224 | tf_op jit(solution)/shard_map/ppermute | solution.py:322
  6.0 6.9 %collective-permute-start.2 = (bf16[32,2048]{1,0:T(8,128)(2,1)S(1)}, bf16[32,2048]{1,0:T(8,128)(2,1)S(1)}, u32[]{:S(2)}, u32[]{:S(2)}) collective-permute-start(bf16[32,2048]{1,0:T(8,128)(2,1)S(1)} %get-tuple-element.22), channel_id=1, source_target_pairs={{0,3},{1,0},{2,1},{3,2},{4,7},{5,4},{6,5},{7,6},{8,11},{9,8},{10,9... | collective-permute-start | bytes 393224 | tf_op jit(solution)/shard_map/ppermute | solution.py:322
  12.8 39.0 %copy-start = (f32[512,128]{1,0:T(8,128)S(1)}, f32[512,128]{1,0:T(8,128)}, u32[]{:S(2)}) copy-start(f32[512,128]{1,0:T(8,128)} %refs_5_.1) | copy-start | bytes 786436
  12.8 39.0 %copy-start.1 = (f32[512]{0:T(512)S(1)}, f32[512]{0:T(512)}, u32[]{:S(2)}) copy-start(f32[512]{0:T(512)} %param.11) | copy-start | bytes 6148
  45.5 4.6 %collective-permute-start.3 = (bf16[32,512]{1,0:T(8,128)(2,1)S(1)}, bf16[32,512]{1,0:T(8,128)(2,1)S(1)}, u32[]{:S(2)}, u32[]{:S(2)}) collective-permute-start(bf16[32,512]{1,0:T(8,128)(2,1)S(1)} %get-tuple-element.30.refs_0_), channel_id=1, source_target_pairs={{0,2},{1,3},{2,0},{3,1},{4,6},{5,7},{6,4},{7,5},{8,10},{9,11},{10,... | collective-permute-start | bytes 98312 | tf_op jit(solution)/shard_map/ppermute | solution.py:322
  47.2 4.0 %collective-permute-start.4 = (bf16[32,512]{1,0:T(8,128)(2,1)S(1)}, bf16[32,512]{1,0:T(8,128)(2,1)S(1)}, u32[]{:S(2)}, u32[]{:S(2)}) collective-permute-start(bf16[32,512]{1,0:T(8,128)(2,1)S(1)} %get-tuple-element.30.refs_0_), channel_id=1, source_target_pairs={{0,1},{1,2},{2,3},{3,0},{4,5},{5,6},{6,7},{7,4},{8,9},{9,10},{10,1... | collective-permute-start | bytes 98312 | tf_op jit(solution)/shard_map/ppermute | solution.py:322
  48.8 3.1 %collective-permute-start.5 = (bf16[32,512]{1,0:T(8,128)(2,1)S(1)}, bf16[32,512]{1,0:T(8,128)(2,1)S(1)}, u32[]{:S(2)}, u32[]{:S(2)}) collective-permute-start(bf16[32,512]{1,0:T(8,128)(2,1)S(1)} %get-tuple-element.30.refs_0_), channel_id=1, source_target_pairs={{0,3},{1,0},{2,1},{3,2},{4,7},{5,4},{6,5},{7,6},{8,11},{9,8},{10,9... | collective-permute-start | bytes 98312 | tf_op jit(solution)/shard_map/ppermute | solution.py:322
  72.2 6.4 %collective-permute-start.6 = (bf16[512,128]{1,0:T(8,128)(2,1)S(1)}, bf16[512,128]{1,0:T(8,128)(2,1)S(1)}, u32[]{:S(2)}, u32[]{:S(2)}) collective-permute-start(bf16[512,128]{1,0:T(8,128)(2,1)S(1)} %shard_map.91), channel_id=1, source_target_pairs={{0,2},{1,3},{2,0},{3,1},{4,6},{5,7},{6,4},{7,5},{8,10},{9,11},{10,... | collective-permute-start | bytes 393224 | tf_op jit(solution)/shard_map/ppermute | solution.py:322
  74.8 6.8 %collective-permute-start.7 = (bf16[512,128]{1,0:T(8,128)(2,1)S(1)}, bf16[512,128]{1,0:T(8,128)(2,1)S(1)}, u32[]{:S(2)}, u32[]{:S(2)}) collective-permute-start(bf16[512,128]{1,0:T(8,128)(2,1)S(1)} %shard_map.91), channel_id=1, source_target_pairs={{0,1},{1,2},{2,3},{3,0},{4,5},{5,6},{6,7},{7,4},{8,9},{9,10},{10,1... | collective-permute-start | bytes 393224 | tf_op jit(solution)/shard_map/ppermute | solution.py:322
  76.3 5.4 %collective-permute-start.8 = (bf16[512,128]{1,0:T(8,128)(2,1)S(1)}, bf16[512,128]{1,0:T(8,128)(2,1)S(1)}, u32[]{:S(2)}, u32[]{:S(2)}) collective-permute-start(bf16[512,128]{1,0:T(8,128)(2,1)S(1)} %shard_map.91), channel_id=1, source_target_pairs={{0,3},{1,0},{2,1},{3,2},{4,7},{5,4},{6,5},{7,6},{8,11},{9,8},{10,9... | collective-permute-start | bytes 393224 | tf_op jit(solution)/shard_map/ppermute | solution.py:322
  81.7 0.8 copy-start.2

commit v6 on v5

--- a/solution.py
+++ b/solution.py
@@ -168,16 +168,19 @@
     for piece in pieces[1:]:
         total = total + piece[...].astype(F32)
     state = total.astype(BF16)
+    columns = state.shape[0]
+    quarters, quarter, _ = places_ref.shape
     for _ in range(LAYERS):
-        state = product(state, tile_ref[...]).astype(BF16)
+        full = jnp.concatenate([state] * (LANES // columns), axis=0)
+        state = product(full, tile_ref[...])[:columns].astype(BF16)
         total = total + state.astype(F32)
     term = (total / F32(LAYERS + 1)).astype(BF16)
-    quarters, quarter, _ = places_ref.shape
+    full = jnp.concatenate(
+        [term[:, number * quarter : (number + 1) * quarter] for number in range(quarters)], axis=0
+    )
     packed = jnp.concatenate(
         [
-            product(
-                term[:, number * quarter : (number + 1) * quarter], places_ref[number]
-            ).astype(BF16)
+            product(full, places_ref[number])[number * columns : (number + 1) * columns].astype(BF16)
             for number in range(quarters)
         ],
         axis=0,

time: 82.7 us -> 81.7 us (0.988)
  Pallas kernels: 13 us -> 11.9 us
    pallas_call x1, Pallas kernels: 5.35 us -> 4.3 us  [propagate(): call(propagate_kernel, shaped((peers, capacity // 2 + 1, 2, LANES), BF16)...]
  transfers between devices with their start and end apart: 9 -> 9, of which waited for: 5 -> 5; matrix products, arithmetic and copies ran while one was open for 2% -> 2% of each run, Pallas kernels for 4% -> 5%
where the time goes in v6:
time: 81.7 us; the launch traced here: 81.5 us
  blocking collectives  45 us (55%)
  starting transfers between devices  14.7 us (18%)
  Pallas kernels  11.9 us (15%)
  waiting for transfers between devices  6.87 us (8%)
  local copies, waits for them, and re-layouts  2.23 us (3%)
    all_to_all x1, blocking collectives, on_device(): lax.all_to_all(message, 'dom', split_axis=0, concat_axis=0, tiled=True)  25.8 us
    all_to_all x1, blocking collectives, on_device(): lax.all_to_all(answer.reshape(peers, capacity, width), 'dom', split_axis=...  19.2 us
    ppermute x9, starting transfers between devices, send(): lax.ppermute(piece, 'rep', [(i, (i + step) % replicas) for i in range(rep...  14.7 us
    ppermute x9, waiting for transfers between devices, send(): lax.ppermute(piece, 'rep', [(i, (i + step) % replicas) for i in range(rep...  6.87 us
    pallas_call x1, Pallas kernels, propagate(): call(propagate_kernel, shaped((peers, capacity // 2 + 1, 2, LANES), BF16)...  4.3 us
    pallas_call x1, Pallas kernels, plan(): call(kernel, [pltpu.VMEM(adjacency.shape, BF16), shaped((quarters, rows /...  3.39 us
    unnamed x8, local copies, waits for them, and re-layouts  2.08 us
  transfers between devices with their start and end apart: 9, of which 5 were waited for; matrix products, arithmetic and copies ran while one was open for 2% of the time, Pallas kernels for 5%

profile of v6, /device:TPU:1, one launch (start us, length us, event | category | flops | bytes accessed | tf_op | source)
XLA Modules:
  0.0 81.5 jit_solution(15652872170006577236)
XLA Ops:
  0.6 1.3 %shard_map.85 = (bf16[32,2048]{1,0:T(8,128)(2,1)S(1)}, bf16[32,2048]{1,0:T(8,128)(2,1)S(1)}, bf16[32,2048]{1,0:T(8,128)(2,1)S(1)}, bf16[32,2048]{1,0:T(8,128)(2,...) custom-call(bf16[2048,128]{1,0:T(8,128)(2,1)} %bitcast.11, s32[1,2048]{1,0:T(1,128)} %bitcast.12, s32[1,2048]{1,0:T(1,128)} %bitcast.13), custom_call_target="tpu_custom_call" | custom-call | tf_op jit(solution)/shard_map/pallas_call | solution.py:79
  2.0 3.7 %collective-permute-start = (bf16[32,2048]{1,0:T(8,128)(2,1)S(1)}, bf16[32,2048]{1,0:T(8,128)(2,1)S(1)}, u32[]{:S(2)}, u32[]{:S(2)}) collective-permute-start(bf16[32,2048]{1,0:T(8,128)(2,1)S(1)} %get-tuple-element.20), channel_id=1, source_target_pairs={{0,2},{1,3},{2,0},{3,1},{4,6},{5,7},{6,4},{7,5},{8,10},{9,11},{10,... | collective-permute-start | bytes 393224 | tf_op jit(solution)/shard_map/ppermute | solution.py:325
  5.6 0.3 collective-permute-start.1
  6.0 2.4 %collective-permute-start.2 = (bf16[32,2048]{1,0:T(8,128)(2,1)S(1)}, bf16[32,2048]{1,0:T(8,128)(2,1)S(1)}, u32[]{:S(2)}, u32[]{:S(2)}) collective-permute-start(bf16[32,2048]{1,0:T(8,128)(2,1)S(1)} %get-tuple-element.22), channel_id=1, source_target_pairs={{0,3},{1,0},{2,1},{3,2},{4,7},{5,4},{6,5},{7,6},{8,11},{9,8},{10,9... | collective-permute-start | bytes 393224 | tf_op jit(solution)/shard_map/ppermute | solution.py:325
  8.3 3.4 %shard_map.86 = (bf16[2048,2048]{1,0:T(8,128)(2,1)S(1)}, bf16[4,512,1024]{2,1,0:T(8,128)(2,1)S(1)}, bf16[64,128]{1,0:T(8,128)(2,1)S(1)}, bf16[4,128,1024]{2,1,0:T(8,128)(2,1)S(1)}, f32[64,1024]{1,0:T(8,128)S(1)}) custom-call(bf16[2048,2048]{1,0:T(8,128)(2,1)} %refs_0_.1, s32[1,2048]{1,0:T(1,128)S(1)} %get-tuple-element.23.refs_1_, ...), custom_call_target="tpu_custom_call" | custom-call | tf_op jit(solution)/shard_map/pallas_call | solution.py:150
  11.7 0.0 collective-permute-done.refs_1_
  11.7 1.1 %collective-permute-done.1.refs_2_ = bf16[32,2048]{1,0:T(8,128)(2,1)S(1)} collective-permute-done((bf16[32,2048]{1,0:T(8,128)(2,1)S(1)}, bf16[32,2048]{1,0:T(8,128)(2,1)S(1)}, u32[]{:S(2)}, u32[]{:S(2)}) %collective-permute-start.1) | collective-permute-done | bytes 131104 | tf_op jit(solution)/shard_map/ppermute | solution.py:325
  12.8 0.0 collective-permute-done.2.refs_3_
  12.9 4.3 %shard_map.87 = bf16[64,9,2,128]{3,2,1,0:T(2,128)(2,1)S(1)} custom-call(bf16[32,2048]{1,0:T(8,128)(2,1)S(1)} %get-tuple-element.19.refs_0_, bf16[32,2048]{1,0:T(8,128)(2,1)S(1)} %collective-permute-done.refs_1_, bf16[32,2048]{1,0:T(8,128)(2,1)S(1)} %collective-permute-done.1.refs_2_, bf16[32,2048]{1,0:T(8,128)(2,1)S(1)} %collective-permute-done.2.refs_3_, ...), custom_call_target="tpu_custom_call" | custom-call | flops 3221225472 | bytes 8388608 | tf_op jit(solution)/shard_map/pallas_call | solution.py:197
  17.2 25.8 %all_to_all.10.refs_0_ = bf16[64,9,2,128]{3,2,1,0:T(2,128)(2,1)S(1)} all-to-all(bf16[64,9,2,128]{3,2,1,0:T(2,128)(2,1)S(1)} %shard_map.87), channel_id=1, replica_groups=mesh['dom'=64,'rep'=4] {'dom'}, dimensions={0} | all-to-all | bytes 589824 | tf_op jit(solution)/shard_map/all_to_all | solution.py:348
  43.0 1.5 %shard_map.88 = (bf16[32,512]{1,0:T(8,128)(2,1)S(1)}, s32[4,8,1024]{2,1,0:T(8,128)S(1)}) custom-call(bf16[64,9,2,128]{3,2,1,0:T(2,128)(2,1)S(1)} %all_to_all.10.refs_0_, bf16[4,128,1024]{2,1,0:T(8,128)(2,1)S(1)} %get-tuple-element.28.refs_1_, f32[64,1024]{1,0:T(8,128)S(1)} %get-tuple-element.29.refs_2_), custom_call_target="tpu_custom_call" | custom-call | flops 536870912 | bytes 1310720 | tf_op jit(solution)/shard_map/pallas_call | solution.py:240
  44.5 1.6 %collective-permute-start.3 = (bf16[32,512]{1,0:T(8,128)(2,1)S(1)}, bf16[32,512]{1,0:T(8,128)(2,1)S(1)}, u32[]{:S(2)}, u32[]{:S(2)}) collective-permute-start(bf16[32,512]{1,0:T(8,128)(2,1)S(1)} %get-tuple-element.30.refs_0_), channel_id=1, source_target_pairs={{0,2},{1,3},{2,0},{3,1},{4,6},{5,7},{6,4},{7,5},{8,10},{9,11},{10,... | collective-permute-start | bytes 98312 | tf_op jit(solution)/shard_map/ppermute | solution.py:325
  46.1 1.7 %collective-permute-start.4 = (bf16[32,512]{1,0:T(8,128)(2,1)S(1)}, bf16[32,512]{1,0:T(8,128)(2,1)S(1)}, u32[]{:S(2)}, u32[]{:S(2)}) collective-permute-start(bf16[32,512]{1,0:T(8,128)(2,1)S(1)} %get-tuple-element.30.refs_0_), channel_id=1, source_target_pairs={{0,1},{1,2},{2,3},{3,0},{4,5},{5,6},{6,7},{7,4},{8,9},{9,10},{10,1... | collective-permute-start | bytes 98312 | tf_op jit(solution)/shard_map/ppermute | solution.py:325
  47.8 1.0 %collective-permute-start.5 = (bf16[32,512]{1,0:T(8,128)(2,1)S(1)}, bf16[32,512]{1,0:T(8,128)(2,1)S(1)}, u32[]{:S(2)}, u32[]{:S(2)}) collective-permute-start(bf16[32,512]{1,0:T(8,128)(2,1)S(1)} %get-tuple-element.30.refs_0_), channel_id=1, source_target_pairs={{0,3},{1,0},{2,1},{3,2},{4,7},{5,4},{6,5},{7,6},{8,11},{9,8},{10,9... | collective-permute-start | bytes 98312 | tf_op jit(solution)/shard_map/ppermute | solution.py:325
  48.8 0.3 shard_map.89.refs_4_
  49.1 0.0 collective-permute-done.3.refs_1_
  49.1 1.0 %collective-permute-done.4.refs_2_ = bf16[32,512]{1,0:T(8,128)(2,1)S(1)} collective-permute-done((bf16[32,512]{1,0:T(8,128)(2,1)S(1)}, bf16[32,512]{1,0:T(8,128)(2,1)S(1)}, u32[]{:S(2)}, u32[]{:S(2)}) %collective-permute-start.4) | collective-permute-done | bytes 32800 | tf_op jit(solution)/shard_map/ppermute | solution.py:325
  50.1 0.7 collective-permute-done.5.refs_3_
  50.8 0.6 shard_map.90
  51.4 19.2 %all_to_all.11 = bf16[64,16,128]{2,1,0:T(8,128)(2,1)S(1)} all-to-all(bf16[64,16,128]{2,1,0:T(8,128)(2,1)S(1)} %bitcast.9), channel_id=1, replica_groups=mesh['dom'=64,'rep'=4] {'dom'}, dimensions={0} | all-to-all | bytes 524288 | tf_op jit(solution)/shard_map/all_to_all | solution.py:356
  70.7 0.4 shard_map.91
  71.1 1.4 %collective-permute-start.6 = (bf16[512,128]{1,0:T(8,128)(2,1)S(1)}, bf16[512,128]{1,0:T(8,128)(2,1)S(1)}, u32[]{:S(2)}, u32[]{:S(2)}) collective-permute-start(bf16[512,128]{1,0:T(8,128)(2,1)S(1)} %shard_map.91), channel_id=1, source_target_pairs={{0,2},{1,3},{2,0},{3,1},{4,6},{5,7},{6,4},{7,5},{8,10},{9,11},{10,... | collective-permute-start | bytes 393224 | tf_op jit(solution)/shard_map/ppermute | solution.py:325
  72.5 0.7 copy.13
  73.2 0.6 copy.14
  73.8 1.5 %collective-permute-start.7 = (bf16[512,128]{1,0:T(8,128)(2,1)S(1)}, bf16[512,128]{1,0:T(8,128)(2,1)S(1)}, u32[]{:S(2)}, u32[]{:S(2)}) collective-permute-start(bf16[512,128]{1,0:T(8,128)(2,1)S(1)} %shard_map.91), channel_id=1, source_target_pairs={{0,1},{1,2},{2,3},{3,0},{4,5},{5,6},{6,7},{7,4},{8,9},{9,10},{10,1... | collective-permute-start | bytes 393224 | tf_op jit(solution)/shard_map/ppermute | solution.py:325
  75.3 1.2 %collective-permute-start.8 = (bf16[512,128]{1,0:T(8,128)(2,1)S(1)}, bf16[512,128]{1,0:T(8,128)(2,1)S(1)}, u32[]{:S(2)}, u32[]{:S(2)}) collective-permute-start(bf16[512,128]{1,0:T(8,128)(2,1)S(1)} %shard_map.91), channel_id=1, source_target_pairs={{0,3},{1,0},{2,1},{3,2},{4,7},{5,4},{6,5},{7,6},{8,11},{9,8},{10,9... | collective-permute-start | bytes 393224 | tf_op jit(solution)/shard_map/ppermute | solution.py:325
  76.5 0.1 broadcast_in_dim.3
  76.6 1.0 %collective-permute-done.6 = bf16[512,128]{1,0:T(8,128)(2,1)S(1)} collective-permute-done((bf16[512,128]{1,0:T(8,128)(2,1)S(1)}, bf16[512,128]{1,0:T(8,128)(2,1)S(1)}, u32[]{:S(2)}, u32[]{:S(2)}) %collective-permute-start.6) | collective-permute-done | bytes 131104 | tf_op jit(solution)/shard_map/ppermute | solution.py:325
  77.6 3.0 %collective-permute-done.7 = bf16[512,128]{1,0:T(8,128)(2,1)S(1)} collective-permute-done((bf16[512,128]{1,0:T(8,128)(2,1)S(1)}, bf16[512,128]{1,0:T(8,128)(2,1)S(1)}, u32[]{:S(2)}, u32[]{:S(2)}) %collective-permute-start.7) | collective-permute-done | bytes 131104 | tf_op jit(solution)/shard_map/ppermute | solution.py:325
  80.6 0.0 collective-permute-done.8
  80.7 0.0 copy-start.2
  80.7 0.8 copy-done.2
  (8 shorter events, 0.1 us)
Async XLA Ops:
  2.0 9.7 %collective-permute-start = (bf16[32,2048]{1,0:T(8,128)(2,1)S(1)}, bf16[32,2048]{1,0:T(8,128)(2,1)S(1)}, u32[]{:S(2)}, u32[]{:S(2)}) collective-permute-start(bf16[32,2048]{1,0:T(8,128)(2,1)S(1)} %get-tuple-element.20), channel_id=1, source_target_pairs={{0,2},{1,3},{2,0},{3,1},{4,6},{5,7},{6,4},{7,5},{8,10},{9,11},{10,... | collective-permute-start | bytes 393224 | tf_op jit(solution)/shard_map/ppermute | solution.py:325
  5.6 7.2 %collective-permute-start.1 = (bf16[32,2048]{1,0:T(8,128)(2,1)S(1)}, bf16[32,2048]{1,0:T(8,128)(2,1)S(1)}, u32[]{:S(2)}, u32[]{:S(2)}) collective-permute-start(bf16[32,2048]{1,0:T(8,128)(2,1)S(1)} %get-tuple-element.21), channel_id=1, source_target_pairs={{0,1},{1,2},{2,3},{3,0},{4,5},{5,6},{6,7},{7,4},{8,9},{9,10},{10,1... | collective-permute-start | bytes 393224 | tf_op jit(solution)/shard_map/ppermute | solution.py:325
  6.0 6.9 %collective-permute-start.2 = (bf16[32,2048]{1,0:T(8,128)(2,1)S(1)}, bf16[32,2048]{1,0:T(8,128)(2,1)S(1)}, u32[]{:S(2)}, u32[]{:S(2)}) collective-permute-start(bf16[32,2048]{1,0:T(8,128)(2,1)S(1)} %get-tuple-element.22), channel_id=1, source_target_pairs={{0,3},{1,0},{2,1},{3,2},{4,7},{5,4},{6,5},{7,6},{8,11},{9,8},{10,9... | collective-permute-start | bytes 393224 | tf_op jit(solution)/shard_map/ppermute | solution.py:325
  12.8 38.0 %copy-start = (f32[512,128]{1,0:T(8,128)S(1)}, f32[512,128]{1,0:T(8,128)}, u32[]{:S(2)}) copy-start(f32[512,128]{1,0:T(8,128)} %refs_5_.1) | copy-start | bytes 786436
  12.8 38.0 %copy-start.1 = (f32[512]{0:T(512)S(1)}, f32[512]{0:T(512)}, u32[]{:S(2)}) copy-start(f32[512]{0:T(512)} %param.11) | copy-start | bytes 6148
  44.5 4.6 %collective-permute-start.3 = (bf16[32,512]{1,0:T(8,128)(2,1)S(1)}, bf16[32,512]{1,0:T(8,128)(2,1)S(1)}, u32[]{:S(2)}, u32[]{:S(2)}) collective-permute-start(bf16[32,512]{1,0:T(8,128)(2,1)S(1)} %get-tuple-element.30.refs_0_), channel_id=1, source_target_pairs={{0,2},{1,3},{2,0},{3,1},{4,6},{5,7},{6,4},{7,5},{8,10},{9,11},{10,... | collective-permute-start | bytes 98312 | tf_op jit(solution)/shard_map/ppermute | solution.py:325
  46.1 4.0 %collective-permute-start.4 = (bf16[32,512]{1,0:T(8,128)(2,1)S(1)}, bf16[32,512]{1,0:T(8,128)(2,1)S(1)}, u32[]{:S(2)}, u32[]{:S(2)}) collective-permute-start(bf16[32,512]{1,0:T(8,128)(2,1)S(1)} %get-tuple-element.30.refs_0_), channel_id=1, source_target_pairs={{0,1},{1,2},{2,3},{3,0},{4,5},{5,6},{6,7},{7,4},{8,9},{9,10},{10,1... | collective-permute-start | bytes 98312 | tf_op jit(solution)/shard_map/ppermute | solution.py:325
  47.8 3.1 %collective-permute-start.5 = (bf16[32,512]{1,0:T(8,128)(2,1)S(1)}, bf16[32,512]{1,0:T(8,128)(2,1)S(1)}, u32[]{:S(2)}, u32[]{:S(2)}) collective-permute-start(bf16[32,512]{1,0:T(8,128)(2,1)S(1)} %get-tuple-element.30.refs_0_), channel_id=1, source_target_pairs={{0,3},{1,0},{2,1},{3,2},{4,7},{5,4},{6,5},{7,6},{8,11},{9,8},{10,9... | collective-permute-start | bytes 98312 | tf_op jit(solution)/shard_map/ppermute | solution.py:325
  71.1 6.4 %collective-permute-start.6 = (bf16[512,128]{1,0:T(8,128)(2,1)S(1)}, bf16[512,128]{1,0:T(8,128)(2,1)S(1)}, u32[]{:S(2)}, u32[]{:S(2)}) collective-permute-start(bf16[512,128]{1,0:T(8,128)(2,1)S(1)} %shard_map.91), channel_id=1, source_target_pairs={{0,2},{1,3},{2,0},{3,1},{4,6},{5,7},{6,4},{7,5},{8,10},{9,11},{10,... | collective-permute-start | bytes 393224 | tf_op jit(solution)/shard_map/ppermute | solution.py:325
  73.8 6.8 %collective-permute-start.7 = (bf16[512,128]{1,0:T(8,128)(2,1)S(1)}, bf16[512,128]{1,0:T(8,128)(2,1)S(1)}, u32[]{:S(2)}, u32[]{:S(2)}) collective-permute-start(bf16[512,128]{1,0:T(8,128)(2,1)S(1)} %shard_map.91), channel_id=1, source_target_pairs={{0,1},{1,2},{2,3},{3,0},{4,5},{5,6},{6,7},{7,4},{8,9},{9,10},{10,1... | collective-permute-start | bytes 393224 | tf_op jit(solution)/shard_map/ppermute | solution.py:325
  75.3 5.4 %collective-permute-start.8 = (bf16[512,128]{1,0:T(8,128)(2,1)S(1)}, bf16[512,128]{1,0:T(8,128)(2,1)S(1)}, u32[]{:S(2)}, u32[]{:S(2)}) collective-permute-start(bf16[512,128]{1,0:T(8,128)(2,1)S(1)} %shard_map.91), channel_id=1, source_target_pairs={{0,3},{1,0},{2,1},{3,2},{4,7},{5,4},{6,5},{7,6},{8,11},{9,8},{10,9... | collective-permute-start | bytes 393224 | tf_op jit(solution)/shard_map/ppermute | solution.py:325
  80.7 0.8 copy-start.2

commit v7 on v6

--- a/solution.py
+++ b/solution.py
@@ -3,6 +3,7 @@
 from jax import lax
 from jax.experimental import pallas as pl
 from jax.experimental.pallas import tpu as pltpu
+from jax.sharding import Mesh
 from jax.sharding import PartitionSpec as P
 
 LAYERS = 3
@@ -11,6 +12,7 @@
 SUBLANES = 8
 PACKED = 16
 CHUNKS = 4
+CORES = 2
 RADIX_BITS = 4
 MEBI = 1024 * 1024
 
@@ -93,7 +95,7 @@
 
 
 def plan_kernel(
-    capacity, tile_hbm, owner_ref, slot_ref, tile_ref, places_ref, slots_ref, weight_ref, mine_ref, arrived
+    capacity, cores, tile_hbm, owner_ref, slot_ref, tile_ref, places_ref, slots_ref, weight_ref, mine_ref, arrived
 ):
     tile_copy = pltpu.make_async_copy(tile_hbm, tile_ref, arrived)
     tile_copy.start()
@@ -106,7 +108,9 @@
     lists = None
     for number in range(quarters):
         lanes = slice(number * quarter, (number + 1) * quarter)
-        owner, slot = owner_ref[:, lanes], slot_ref[:, lanes]
+        named, slot = owner_ref[:, lanes], slot_ref[:, lanes]
+        other = lax.rem(named + lax.axis_index("core"), cores)
+        owner = other * (peers // cores) + lax.div(named, cores)
         hot = ids((peers, quarter), 0) == owner
         owner_hot = jnp.where(hot, 1.0, 0.0).astype(BF16)
         running = product(owner_hot, upper)
@@ -130,7 +134,8 @@
             preferred_element_type=F32,
         )
         lists = added if lists is None else lists + added
-        lane, turn = ids((LANES, places), 0), lax.rem(ids((LANES, places), 1), capacity)
+        shape = weight_ref.shape[1:]
+        lane, turn = ids(shape, 0), lax.rem(ids(shape, 1), capacity)
         turn = turn + number * capacity
         units = jnp.where(lane == turn + quarters * capacity, 1.0, 0.0)
         weight_ref[number] = jnp.where(lane == turn, float(1 << RADIX_BITS), units).astype(BF16)
@@ -140,12 +145,12 @@
     tile_copy.wait()
 
 
-def plan(adjacency, owner, slot, quarters, peers, capacity):
+def plan(adjacency, owner, slot, quarters, peers, cores, capacity):
     rows = slot.shape[1]
     places = peers * capacity
 
     def kernel(*refs):
-        plan_kernel(capacity, *refs)
+        plan_kernel(capacity, cores, *refs)
 
     return call(
         kernel,
@@ -153,8 +158,8 @@
             pltpu.VMEM(adjacency.shape, BF16),
             shaped((quarters, rows // quarters, places), BF16),
             shaped((peers, LANES), BF16),
-            shaped((quarters, LANES, places), BF16),
-            shaped((peers, places), F32),
+            shaped((quarters, LANES, places // cores), BF16),
+            shaped((peers // cores, places // cores), F32),
         ],
         [HBM, VMEM, VMEM],
         [VMEM] * 5,
@@ -185,18 +190,21 @@
         ],
         axis=0,
     )
-    peers, pairs = out_ref.shape[:2]
-    out_ref[:, : pairs - 1] = packed.T.reshape(peers, pairs - 1, 2, LANES)
+    chips, cores, pairs = out_ref.shape[:3]
+    packed = packed.T.reshape(cores, chips, pairs - 1, 2, LANES)
     lists = slots_ref[...]
-    out_ref[:, pairs - 1] = jnp.broadcast_to(lists[:, None, :], (peers, 2, LANES))
-
-
-def propagate(pieces, tile, places, slots, capacity):
-    peers = slots.shape[0]
+    for core in range(cores):
+        out_ref[:, core, : pairs - 1] = packed[core]
+        own = lists[core * chips : (core + 1) * chips]
+        out_ref[:, core, pairs - 1] = jnp.broadcast_to(own[:, None, :], (chips, 2, LANES))
+
+
+def propagate(pieces, tile, places, slots, cores, capacity):
+    chips = slots.shape[0] // cores
     rows = tile.shape[0]
     return call(
         propagate_kernel,
-        shaped((peers, capacity // 2 + 1, 2, LANES), BF16),
+        shaped((chips, cores, capacity // 2 + 1, 2, LANES), BF16),
         [VMEM] * (len(pieces) + 3),
         VMEM,
         flops=2 * LAYERS * rows * rows * LANES,
@@ -204,12 +212,14 @@
     )(*pieces, tile, places, slots)
 
 
-def accumulate_kernel(shard, message_ref, weight_ref, mine_ref, piece_ref, rows_ref):
+def accumulate_kernel(shard, message_ref, weight_ref, mine_ref, *refs):
+    *before, piece_ref, rows_ref = refs
     quarters, _, places = weight_ref.shape
-    pairs = message_ref.shape[1]
+    message = message_ref.at[:, 0]
+    pairs = message.shape[1]
     columns = LANES // quarters
-    digits = message_ref[:, pairs - 1, 0, :]
-    data = message_ref[:, : pairs - 1].reshape(places, LANES)
+    digits = message[:, pairs - 1, 0, :]
+    data = message[:, : pairs - 1].reshape(places, LANES)
     block = ids((shard, LANES), 1) // columns
     index = ids((shard, places), 0).astype(jnp.int16)
     slots = []
@@ -224,46 +234,52 @@
         receiver = jnp.where(hot, jnp.ones(hot.shape, BF16), jnp.zeros(hot.shape, BF16))
         added = product(receiver, data)
         sums = added if sums is None else jnp.where(block == number, added, sums)
-    turned = sums.T
-    whole = turned[:columns]
-    for number in range(1, quarters):
-        whole = whole + turned[number * columns : (number + 1) * columns]
-    piece_ref[...] = whole.astype(BF16)
-
-
-def accumulate(message, weight, mine, shard):
+    if before:
+        piece = before[0][...] + sums
+        turned = piece.T
+        whole = turned[:columns]
+        for number in range(1, quarters):
+            whole = whole + turned[number * columns : (number + 1) * columns]
+        piece_ref[...] = whole.astype(BF16)
+    else:
+        piece_ref[...] = sums
+
+
+def accumulate(message, weight, mine, shard, before=None):
     quarters, _, places = weight.shape
 
     def kernel(*refs):
         accumulate_kernel(shard, *refs)
 
+    piece = shaped((shard, LANES), F32)
+    if before is not None:
+        piece = shaped((LANES // quarters, shard), BF16)
+    earlier = [] if before is None else [before]
     return call(
         kernel,
-        [
-            shaped((LANES // quarters, shard), BF16),
-            shaped((quarters, SUBLANES, places), jnp.int32),
-        ],
-        [VMEM] * 3,
+        [piece, shaped((quarters, SUBLANES, places), jnp.int32)],
+        [VMEM] * (3 + len(earlier)),
         [VMEM] * 2,
         flops=2 * quarters * shard * places * LANES,
         moved=2 * places * (shard + LANES),
-    )(message, weight, mine)
-
-
-def prepare_kernel(rows_ref, sender_ref):
+    )(message, weight, mine, *earlier)
+
+
+def prepare_kernel(same_ref, other_ref, sender_ref):
     places, shard = sender_ref.shape
-    slot = rows_ref[lax.axis_index("rep")].astype(F32)
+    me = lax.axis_index("rep")
+    slot = jnp.concatenate([same_ref[me], other_ref[me]], axis=1).astype(F32)
     column = jnp.concatenate([slot] * (LANES // SUBLANES), axis=0).T.astype(jnp.int32)
     for part in range(shard // LANES):
         here = column == ids(column.shape, 1) + part * LANES
         sender_ref[:, part * LANES : (part + 1) * LANES] = jnp.where(here, 1.0, 0.0).astype(BF16)
 
 
-def prepare(rows, shard):
-    places = rows.shape[2]
+def prepare(same, other, shard):
+    places = same.shape[2] + other.shape[2]
     return call(
-        prepare_kernel, shaped((places, shard), BF16), [VMEM], VMEM, moved=2 * places * shard
-    )(rows)
+        prepare_kernel, shaped((places, shard), BF16), [VMEM] * 2, VMEM, moved=2 * places * shard
+    )(same, other)
 
 
 def update_kernel(steps, *refs):
@@ -279,10 +295,14 @@
     step = whole * (LEARN_RATE * lax.rsqrt(sums))
     new_table = table_ref[...] - step.T
     new_table_ref[...] = new_table
-    answer_ref[...] = product(sender_ref[...], new_table.astype(BF16)).astype(BF16)
-
-
-def update(steps, pieces, sender, table_rows, row_accumulators):
+    answer = product(sender_ref[...], new_table.astype(BF16)).astype(BF16)
+    chips, cores, capacity = answer_ref.shape[:3]
+    answer = answer.reshape(cores, chips, capacity, LANES)
+    for core in range(cores):
+        answer_ref[:, lax.rem(lax.axis_index("core") + core, cores)] = answer[core]
+
+
+def update(steps, pieces, sender, table_rows, row_accumulators, cores, capacity):
     places, shard = sender.shape
 
     def kernel(*refs):
@@ -293,7 +313,7 @@
         [
             pltpu.VMEM((shard, LANES), F32),
             pltpu.VMEM((1, shard), F32),
-            shaped((places, LANES), BF16),
+            shaped((places // (cores * capacity), cores, capacity, LANES), BF16),
         ],
         [VMEM] * (len(pieces) + 3),
         [VMEM] * 3,
@@ -306,7 +326,14 @@
 
 def unpack_kernel(places_ref, returned_ref, out_ref):
     matrix = places_ref[lax.axis_index("rep")]
-    out_ref[...] = product(matrix, returned_ref[...]).astype(BF16)
+    cores = returned_ref.shape[1]
+    half = matrix.shape[1] // cores
+    fresh = None
+    for core in range(cores):
+        rows = returned_ref[:, lax.rem(lax.axis_index("core") + core, cores)].reshape(half, LANES)
+        added = product(matrix[:, core * half : (core + 1) * half], rows)
+        fresh = added if fresh is None else fresh + added
+    out_ref[...] = fresh.astype(BF16)
 
 
 def unpack(matrices, returned):
@@ -330,7 +357,8 @@
 
 
 def on_device(adjacency, grad_out, row_owner, table_slot, table_rows, row_accumulators):
-    peers = lax.axis_size("dom")
+    chips, cores = lax.axis_size("chip"), lax.axis_size("core")
+    peers = chips * cores
     replicas = lax.axis_size("rep")
     rows = adjacency.shape[0]
     width = grad_out.shape[2]
@@ -342,21 +370,26 @@
 
     columns, owner, slot = split(grad_out[0], row_owner, table_slot, replicas)
     pieces = [columns[0]] + [send(columns[step], step, replicas) for step in order]
-    tile, places, slots, weight, mine = plan(adjacency, owner, slot, replicas, peers, capacity)
-    message = propagate(pieces, tile, places, slots, capacity)
-
-    incoming = lax.all_to_all(message, "dom", split_axis=0, concat_axis=0, tiled=True)
-    piece, lists = accumulate(incoming, weight, mine, shard)
+    tile, places, slots, weight, mine = plan(
+        adjacency, owner, slot, replicas, peers, cores, capacity
+    )
+    message = propagate(pieces, tile, places, slots, cores, capacity)
+
+    landed = lax.all_to_all(message, "chip", split_axis=0, concat_axis=0, tiled=True)
+    across = lax.ppermute(landed[:, 1:], "core", [(0, 1), (1, 0)])
+    sums, same = accumulate(landed, weight, mine, shard)
+    piece, other = accumulate(across, weight, mine, shard, before=sums)
     pieces = [piece] + [send(piece, step, replicas) for step in order]
-    sender = prepare(lists, shard)
+    sender = prepare(same, other, shard)
     new_table, new_accumulators, answer = update(
-        [0, *order], pieces, sender, table_rows, row_accumulators
+        [0, *order], pieces, sender, table_rows, row_accumulators, cores, capacity
     )
 
     returned = lax.all_to_all(
-        answer.reshape(peers, capacity, width), "dom", split_axis=0, concat_axis=0, tiled=True
-    )
-    fresh = unpack(places, returned.reshape(peers * capacity, width))
+        answer.reshape(peers, capacity, width),
+        ("chip", "core"), split_axis=0, concat_axis=0, tiled=True,
+    )
+    fresh = unpack(places, returned.reshape(chips, cores, capacity, width))
     pieces = [send(fresh, step, replicas) for step in order]
     fresh_rows = jnp.zeros((rows, width), BF16)
     for step, piece in zip([0, *order], [fresh, *pieces]):
@@ -366,17 +399,20 @@
 
 
 def solution(mesh):
+    dom, replicas = mesh.devices.shape
+    chips = Mesh(mesh.devices.reshape(dom // CORES, CORES, replicas), ("chip", "core", "rep"))
+    split_rows = ("chip", "core")
     return jax.shard_map(
         on_device,
-        mesh=mesh,
+        mesh=chips,
         in_specs=(
-            P("dom", None),
-            P("rep", "dom", None),
-            P("dom", None),
-            P("dom"),
-            P("dom", None),
-            P("dom"),
+            P(split_rows, None),
+            P("rep", split_rows, None),
+            P(split_rows, None),
+            P(split_rows),
+            P(split_rows, None),
+            P(split_rows),
         ),
-        out_specs=(P("dom", None), P("dom"), P("dom", None)),
+        out_specs=(P(split_rows, None), P(split_rows), P(split_rows, None)),
         check_vma=False,
     )

time: 81.7 us -> 80.8 us (0.989)
  blocking collectives: 45 us -> 40.1 us
  starting transfers between devices: 14.7 us -> 19.4 us
  waiting for transfers between devices: 6.87 us -> 5.91 us
    all_to_all x2, blocking collectives: 45 us -> 40.1 us  [the longest x1 21.3 us: on_device(): lax.all_to_all(message, 'chip', split_axis=0, concat_axis=0, tiled=True)]
    ppermute x0 -> x1, starting transfers between devices: none -> 3.6 us  [on_device(): across = lax.ppermute(landed[:, 1:], 'core', [(0, 1), (1, 0)])]
    ppermute x9, waiting for transfers between devices: 6.87 us -> 5.74 us  [send(): lax.ppermute(piece, 'rep', [(i, (i + step) % replicas) for i in range(rep...]
    ppermute x9, starting transfers between devices: 14.7 us -> 15.8 us  [send(): lax.ppermute(piece, 'rep', [(i, (i + step) % replicas) for i in range(rep...]
    pallas_call x3 -> x4, Pallas kernels: 6.12 us -> 6.34 us  [the longest x1 4.29 us: propagate(): call(propagate_kernel, shaped((chips, cores, capacity // 2 + 1, 2, LANES)...]
  transfers between devices with their start and end apart: 9 -> 10, of which waited for: 5 -> 5; matrix products, arithmetic and copies ran while one was open for 2% -> 2% of each run, Pallas kernels for 5% -> 6%
where the time goes in v7:
time: 80.8 us; the launch traced here: 80.6 us
  blocking collectives  40.1 us (50%)
  starting transfers between devices  19.4 us (24%)
  Pallas kernels  12.1 us (15%)
  waiting for transfers between devices  5.91 us (7%)
  local copies, waits for them, and re-layouts  2.34 us (3%)
    all_to_all x1, blocking collectives, on_device(): lax.all_to_all(message, 'chip', split_axis=0, concat_axis=0, tiled=True)  21.3 us
    all_to_all x1, blocking collectives, on_device(): lax.all_to_all(answer.reshape(peers, capacity, width), ('chip', 'core'),...  18.8 us
    ppermute x9, starting transfers between devices, send(): lax.ppermute(piece, 'rep', [(i, (i + step) % replicas) for i in range(rep...  15.8 us
    ppermute x9, waiting for transfers between devices, send(): lax.ppermute(piece, 'rep', [(i, (i + step) % replicas) for i in range(rep...  5.74 us
    pallas_call x1, Pallas kernels, propagate(): call(propagate_kernel, shaped((chips, cores, capacity // 2 + 1, 2, LANES)...  4.29 us
    ppermute x1, starting transfers between devices, on_device(): across = lax.ppermute(landed[:, 1:], 'core', [(0, 1), (1, 0)])  3.6 us
    pallas_call x1, Pallas kernels, plan(): call(kernel, [pltpu.VMEM(adjacency.shape, BF16), shaped((quarters, rows /...  3.39 us
    unnamed x8, local copies, waits for them, and re-layouts  2.08 us
  transfers between devices with their start and end apart: 10, of which 5 were waited for; matrix products, arithmetic and copies ran while one was open for 2% of the time, Pallas kernels for 6%

profile of v7, /device:TPU:1, one launch (start us, length us, event | category | flops | bytes accessed | tf_op | source)
XLA Modules:
  0.0 80.6 jit_solution(16319174485596844405)
XLA Ops:
  0.6 1.3 %shard_map.85 = (bf16[32,2048]{1,0:T(8,128)(2,1)S(1)}, bf16[32,2048]{1,0:T(8,128)(2,1)S(1)}, bf16[32,2048]{1,0:T(8,128)(2,1)S(1)}, bf16[32,2048]{1,0:T(8,128)(2,...) custom-call(bf16[2048,128]{1,0:T(8,128)(2,1)} %bitcast.11, s32[1,2048]{1,0:T(1,128)} %bitcast.12, s32[1,2048]{1,0:T(1,128)} %bitcast.13), custom_call_target="tpu_custom_call" | custom-call | tf_op jit(solution)/shard_map/pallas_call | solution.py:81
  2.0 3.7 %collective-permute-start = (bf16[32,2048]{1,0:T(8,128)(2,1)S(1)}, bf16[32,2048]{1,0:T(8,128)(2,1)S(1)}, u32[]{:S(2)}, u32[]{:S(2)}) collective-permute-start(bf16[32,2048]{1,0:T(8,128)(2,1)S(1)} %get-tuple-element.22), channel_id=1, source_target_pairs={{0,2},{1,3},{2,0},{3,1},{4,6},{5,7},{6,4},{7,5},{8,10},{9,11},{10,... | collective-permute-start | bytes 393224 | tf_op jit(solution)/shard_map/ppermute | solution.py:352
  5.6 0.3 collective-permute-start.1
  6.0 2.4 %collective-permute-start.2 = (bf16[32,2048]{1,0:T(8,128)(2,1)S(1)}, bf16[32,2048]{1,0:T(8,128)(2,1)S(1)}, u32[]{:S(2)}, u32[]{:S(2)}) collective-permute-start(bf16[32,2048]{1,0:T(8,128)(2,1)S(1)} %get-tuple-element.24), channel_id=1, source_target_pairs={{0,3},{1,0},{2,1},{3,2},{4,7},{5,4},{6,5},{7,6},{8,11},{9,8},{10,9... | collective-permute-start | bytes 393224 | tf_op jit(solution)/shard_map/ppermute | solution.py:352
  8.3 3.4 %shard_map.86 = (bf16[2048,2048]{1,0:T(8,128)(2,1)S(1)}, bf16[4,512,1024]{2,1,0:T(8,128)(2,1)S(1)}, bf16[64,128]{1,0:T(8,128)(2,1)S(1)}, bf16[4,128,512]{2,1,0:T(8,128)(2,1)S(1)}, f32[32,512]{1,0:T(8,128)S(1)}) custom-call(bf16[2048,2048]{1,0:T(8,128)(2,1)} %refs_0_.1, s32[1,2048]{1,0:T(1,128)S(1)} %get-tuple-element.25.refs_1_, ...), custom_call_target="tpu_custom_call" | custom-call | tf_op jit(solution)/shard_map/pallas_call | solution.py:155
  11.7 1.1 %collective-permute-done.1.refs_2_ = bf16[32,2048]{1,0:T(8,128)(2,1)S(1)} collective-permute-done((bf16[32,2048]{1,0:T(8,128)(2,1)S(1)}, bf16[32,2048]{1,0:T(8,128)(2,1)S(1)}, u32[]{:S(2)}, u32[]{:S(2)}) %collective-permute-start.1) | collective-permute-done | bytes 131104 | tf_op jit(solution)/shard_map/ppermute | solution.py:352
  12.9 4.3 %shard_map.87 = bf16[32,2,9,2,128]{4,3,2,1,0:T(2,128)(2,1)S(1)} custom-call(bf16[32,2048]{1,0:T(8,128)(2,1)S(1)} %get-tuple-element.21.refs_0_, bf16[32,2048]{1,0:T(8,128)(2,1)S(1)} %collective-permute-done.refs_1_, bf16[32,2048]{1,0:T(8,128)(2,1)S(1)} %collective-permute-done.1.refs_2_, bf16[32,2048]{1,0:T(8,128)(2,1)S(1)} %collective-permute-done.2.refs_3_, ...), custom_call_target="tpu_custom_call" | custom-call | flops 3221225472 | bytes 8388608 | tf_op jit(solution)/shard_map/pallas_call | solution.py:205
  17.2 21.3 %all_to_all.10.refs_0_ = bf16[32,2,9,2,128]{4,3,2,1,0:T(2,128)(2,1)S(1)} all-to-all(bf16[32,2,9,2,128]{4,3,2,1,0:T(2,128)(2,1)S(1)} %shard_map.87), channel_id=1, replica_groups=mesh['chip'=32,'core'=2,'rep'=4] {'chip'}, dimensions={0} | all-to-all | bytes 589824 | tf_op jit(solution)/shard_map/all_to_all | solution.py:378
  38.4 0.1 slice.4
  38.5 3.6 %collective-permute-start.3 = (bf16[32,1,9,2,128]{4,3,2,1,0:T(2,128)(2,1)S(1)}, bf16[32,1,9,2,128]{4,3,2,1,0:T(2,128)(2,1)S(1)}, u32[]{:S(2)}, u32[]{:S(2)}) collective-permute-start(bf16[32,1,9,2,128]{4,3,2,1,0:T(2,128)(2,1)S(1)} %slice.4), channel_id=1, source_target_pairs={{0,4},{4,0},{1,5},{5,1},{2,6},{6,2},{3,7},{7,3},{8,12},{12,8},{9,1... | collective-permute-start | bytes 442376 | tf_op jit(solution)/shard_map/ppermute | solution.py:379
  42.1 0.8 %shard_map.88 = (f32[512,128]{1,0:T(8,128)S(1)}, s32[4,8,512]{2,1,0:T(8,128)S(1)}) custom-call(bf16[32,2,9,2,128]{4,3,2,1,0:T(2,128)(2,1)S(1)} %all_to_all.10.refs_0_, bf16[4,128,512]{2,1,0:T(8,128)(2,1)S(1)} %get-tuple-element.30.refs_1_, f32[32,512]{1,0:T(8,128)S(1)} %get-tuple-element.31.refs_2_), custom_call_target="tpu_custom_call" | custom-call | flops 268435456 | bytes 655360 | tf_op jit(solution)/shard_map/pallas_call | solution.py:258
  43.0 0.2 collective-permute-done.3.refs_0_
  43.1 0.9 %shard_map.89 = (bf16[32,512]{1,0:T(8,128)(2,1)S(1)}, s32[4,8,512]{2,1,0:T(8,128)S(1)}) custom-call(bf16[32,1,9,2,128]{4,3,2,1,0:T(2,128)(2,1)S(1)} %collective-permute-done.3.refs_0_, bf16[4,128,512]{2,1,0:T(8,128)(2,1)S(1)} %get-tuple-element.30.refs_1_, f32[32,512]{1,0:T(8,128)S(1)} %get-tuple-element.31.refs_2_, f32[512,128]{1,0:T(8,128)S(1)} %get-tuple-element.32.refs_3_), custom_call_target="tpu_custom_call" | custom-call | flops 268435456 | bytes 655360 | tf_op jit(solution)/shard_map/pallas_call | solution.py:258
  44.0 1.8 %collective-permute-start.4 = (bf16[32,512]{1,0:T(8,128)(2,1)S(1)}, bf16[32,512]{1,0:T(8,128)(2,1)S(1)}, u32[]{:S(2)}, u32[]{:S(2)}) collective-permute-start(bf16[32,512]{1,0:T(8,128)(2,1)S(1)} %get-tuple-element.33.refs_0_), channel_id=1, source_target_pairs={{0,2},{1,3},{2,0},{3,1},{4,6},{5,7},{6,4},{7,5},{8,10},{9,11},{10,... | collective-permute-start | bytes 98312 | tf_op jit(solution)/shard_map/ppermute | solution.py:352
  45.8 1.7 %collective-permute-start.5 = (bf16[32,512]{1,0:T(8,128)(2,1)S(1)}, bf16[32,512]{1,0:T(8,128)(2,1)S(1)}, u32[]{:S(2)}, u32[]{:S(2)}) collective-permute-start(bf16[32,512]{1,0:T(8,128)(2,1)S(1)} %get-tuple-element.33.refs_0_), channel_id=1, source_target_pairs={{0,1},{1,2},{2,3},{3,0},{4,5},{5,6},{6,7},{7,4},{8,9},{9,10},{10,1... | collective-permute-start | bytes 98312 | tf_op jit(solution)/shard_map/ppermute | solution.py:352
  47.5 1.0 %collective-permute-start.6 = (bf16[32,512]{1,0:T(8,128)(2,1)S(1)}, bf16[32,512]{1,0:T(8,128)(2,1)S(1)}, u32[]{:S(2)}, u32[]{:S(2)}) collective-permute-start(bf16[32,512]{1,0:T(8,128)(2,1)S(1)} %get-tuple-element.33.refs_0_), channel_id=1, source_target_pairs={{0,3},{1,0},{2,1},{3,2},{4,7},{5,4},{6,5},{7,6},{8,11},{9,8},{10,9... | collective-permute-start | bytes 98312 | tf_op jit(solution)/shard_map/ppermute | solution.py:352
  48.5 0.3 shard_map.90.refs_4_
  48.8 1.0 %collective-permute-done.5.refs_2_ = bf16[32,512]{1,0:T(8,128)(2,1)S(1)} collective-permute-done((bf16[32,512]{1,0:T(8,128)(2,1)S(1)}, bf16[32,512]{1,0:T(8,128)(2,1)S(1)}, u32[]{:S(2)}, u32[]{:S(2)}) %collective-permute-start.5) | collective-permute-done | bytes 32800 | tf_op jit(solution)/shard_map/ppermute | solution.py:352
  49.8 0.4 collective-permute-done.6.refs_3_
  50.3 0.6 shard_map.91
  50.9 18.8 %all_to_all.11 = bf16[64,16,128]{2,1,0:T(8,128)(2,1)S(1)} all-to-all(bf16[64,16,128]{2,1,0:T(8,128)(2,1)S(1)} %bitcast.9), channel_id=1, replica_groups=mesh['chip'=32,'core'=2,'rep'=4] {'chip','core'}, dimensions={0} | all-to-all | bytes 524288 | tf_op jit(solution)/shard_map/all_to_all | solution.py:388
  69.7 0.4 shard_map.92
  70.2 2.3 %collective-permute-start.7 = (bf16[512,128]{1,0:T(8,128)(2,1)S(1)}, bf16[512,128]{1,0:T(8,128)(2,1)S(1)}, u32[]{:S(2)}, u32[]{:S(2)}) collective-permute-start(bf16[512,128]{1,0:T(8,128)(2,1)S(1)} %shard_map.92), channel_id=1, source_target_pairs={{0,2},{1,3},{2,0},{3,1},{4,6},{5,7},{6,4},{7,5},{8,10},{9,11},{10,... | collective-permute-start | bytes 393224 | tf_op jit(solution)/shard_map/ppermute | solution.py:352
  72.5 0.7 copy.13
  73.2 0.6 copy.14
  73.8 0.6 collective-permute-start.8
  74.3 2.1 %collective-permute-start.9 = (bf16[512,128]{1,0:T(8,128)(2,1)S(1)}, bf16[512,128]{1,0:T(8,128)(2,1)S(1)}, u32[]{:S(2)}, u32[]{:S(2)}) collective-permute-start(bf16[512,128]{1,0:T(8,128)(2,1)S(1)} %shard_map.92), channel_id=1, source_target_pairs={{0,3},{1,0},{2,1},{3,2},{4,7},{5,4},{6,5},{7,6},{8,11},{9,8},{10,9... | collective-permute-start | bytes 393224 | tf_op jit(solution)/shard_map/ppermute | solution.py:352
  76.4 0.1 broadcast_in_dim.3
  76.5 0.0 collective-permute-done.7
  76.6 3.1 %collective-permute-done.8 = bf16[512,128]{1,0:T(8,128)(2,1)S(1)} collective-permute-done((bf16[512,128]{1,0:T(8,128)(2,1)S(1)}, bf16[512,128]{1,0:T(8,128)(2,1)S(1)}, u32[]{:S(2)}, u32[]{:S(2)}) %collective-permute-start.8) | collective-permute-done | bytes 131104 | tf_op jit(solution)/shard_map/ppermute | solution.py:352
  79.8 0.0 copy-start.2
  79.8 0.8 copy-done.2
  (12 shorter events, 0.1 us)
Async XLA Ops:
  2.0 9.7 %collective-permute-start = (bf16[32,2048]{1,0:T(8,128)(2,1)S(1)}, bf16[32,2048]{1,0:T(8,128)(2,1)S(1)}, u32[]{:S(2)}, u32[]{:S(2)}) collective-permute-start(bf16[32,2048]{1,0:T(8,128)(2,1)S(1)} %get-tuple-element.22), channel_id=1, source_target_pairs={{0,2},{1,3},{2,0},{3,1},{4,6},{5,7},{6,4},{7,5},{8,10},{9,11},{10,... | collective-permute-start | bytes 393224 | tf_op jit(solution)/shard_map/ppermute | solution.py:352
  5.6 7.2 %collective-permute-start.1 = (bf16[32,2048]{1,0:T(8,128)(2,1)S(1)}, bf16[32,2048]{1,0:T(8,128)(2,1)S(1)}, u32[]{:S(2)}, u32[]{:S(2)}) collective-permute-start(bf16[32,2048]{1,0:T(8,128)(2,1)S(1)} %get-tuple-element.23), channel_id=1, source_target_pairs={{0,1},{1,2},{2,3},{3,0},{4,5},{5,6},{6,7},{7,4},{8,9},{9,10},{10,1... | collective-permute-start | bytes 393224 | tf_op jit(solution)/shard_map/ppermute | solution.py:352
  6.0 6.9 %collective-permute-start.2 = (bf16[32,2048]{1,0:T(8,128)(2,1)S(1)}, bf16[32,2048]{1,0:T(8,128)(2,1)S(1)}, u32[]{:S(2)}, u32[]{:S(2)}) collective-permute-start(bf16[32,2048]{1,0:T(8,128)(2,1)S(1)} %get-tuple-element.24), channel_id=1, source_target_pairs={{0,3},{1,0},{2,1},{3,2},{4,7},{5,4},{6,5},{7,6},{8,11},{9,8},{10,9... | collective-permute-start | bytes 393224 | tf_op jit(solution)/shard_map/ppermute | solution.py:352
  12.8 37.4 %copy-start = (f32[512,128]{1,0:T(8,128)S(1)}, f32[512,128]{1,0:T(8,128)}, u32[]{:S(2)}) copy-start(f32[512,128]{1,0:T(8,128)} %refs_5_.1) | copy-start | bytes 786436
  12.8 37.4 %copy-start.1 = (f32[512]{0:T(512)S(1)}, f32[512]{0:T(512)}, u32[]{:S(2)}) copy-start(f32[512]{0:T(512)} %param.11) | copy-start | bytes 6148
  38.5 4.6 %collective-permute-start.3 = (bf16[32,1,9,2,128]{4,3,2,1,0:T(2,128)(2,1)S(1)}, bf16[32,1,9,2,128]{4,3,2,1,0:T(2,128)(2,1)S(1)}, u32[]{:S(2)}, u32[]{:S(2)}) collective-permute-start(bf16[32,1,9,2,128]{4,3,2,1,0:T(2,128)(2,1)S(1)} %slice.4), channel_id=1, source_target_pairs={{0,4},{4,0},{1,5},{5,1},{2,6},{6,2},{3,7},{7,3},{8,12},{12,8},{9,1... | collective-permute-start | bytes 442376 | tf_op jit(solution)/shard_map/ppermute | solution.py:379
  44.0 4.8 %collective-permute-start.4 = (bf16[32,512]{1,0:T(8,128)(2,1)S(1)}, bf16[32,512]{1,0:T(8,128)(2,1)S(1)}, u32[]{:S(2)}, u32[]{:S(2)}) collective-permute-start(bf16[32,512]{1,0:T(8,128)(2,1)S(1)} %get-tuple-element.33.refs_0_), channel_id=1, source_target_pairs={{0,2},{1,3},{2,0},{3,1},{4,6},{5,7},{6,4},{7,5},{8,10},{9,11},{10,... | collective-permute-start | bytes 98312 | tf_op jit(solution)/shard_map/ppermute | solution.py:352
  45.8 4.0 %collective-permute-start.5 = (bf16[32,512]{1,0:T(8,128)(2,1)S(1)}, bf16[32,512]{1,0:T(8,128)(2,1)S(1)}, u32[]{:S(2)}, u32[]{:S(2)}) collective-permute-start(bf16[32,512]{1,0:T(8,128)(2,1)S(1)} %get-tuple-element.33.refs_0_), channel_id=1, source_target_pairs={{0,1},{1,2},{2,3},{3,0},{4,5},{5,6},{6,7},{7,4},{8,9},{9,10},{10,1... | collective-permute-start | bytes 98312 | tf_op jit(solution)/shard_map/ppermute | solution.py:352
  47.5 2.8 %collective-permute-start.6 = (bf16[32,512]{1,0:T(8,128)(2,1)S(1)}, bf16[32,512]{1,0:T(8,128)(2,1)S(1)}, u32[]{:S(2)}, u32[]{:S(2)}) collective-permute-start(bf16[32,512]{1,0:T(8,128)(2,1)S(1)} %get-tuple-element.33.refs_0_), channel_id=1, source_target_pairs={{0,3},{1,0},{2,1},{3,2},{4,7},{5,4},{6,5},{7,6},{8,11},{9,8},{10,9... | collective-permute-start | bytes 98312 | tf_op jit(solution)/shard_map/ppermute | solution.py:352
  70.2 6.4 %collective-permute-start.7 = (bf16[512,128]{1,0:T(8,128)(2,1)S(1)}, bf16[512,128]{1,0:T(8,128)(2,1)S(1)}, u32[]{:S(2)}, u32[]{:S(2)}) collective-permute-start(bf16[512,128]{1,0:T(8,128)(2,1)S(1)} %shard_map.92), channel_id=1, source_target_pairs={{0,2},{1,3},{2,0},{3,1},{4,6},{5,7},{6,4},{7,5},{8,10},{9,11},{10,... | collective-permute-start | bytes 393224 | tf_op jit(solution)/shard_map/ppermute | solution.py:352
  73.8 6.0 %collective-permute-start.8 = (bf16[512,128]{1,0:T(8,128)(2,1)S(1)}, bf16[512,128]{1,0:T(8,128)(2,1)S(1)}, u32[]{:S(2)}, u32[]{:S(2)}) collective-permute-start(bf16[512,128]{1,0:T(8,128)(2,1)S(1)} %shard_map.92), channel_id=1, source_target_pairs={{0,1},{1,2},{2,3},{3,0},{4,5},{5,6},{6,7},{7,4},{8,9},{9,10},{10,1... | collective-permute-start | bytes 393224 | tf_op jit(solution)/shard_map/ppermute | solution.py:352
  74.3 5.5 %collective-permute-start.9 = (bf16[512,128]{1,0:T(8,128)(2,1)S(1)}, bf16[512,128]{1,0:T(8,128)(2,1)S(1)}, u32[]{:S(2)}, u32[]{:S(2)}) collective-permute-start(bf16[512,128]{1,0:T(8,128)(2,1)S(1)} %shard_map.92), channel_id=1, source_target_pairs={{0,3},{1,0},{2,1},{3,2},{4,7},{5,4},{6,5},{7,6},{8,11},{9,8},{10,9... | collective-permute-start | bytes 393224 | tf_op jit(solution)/shard_map/ppermute | solution.py:352
  79.8 0.8 copy-start.2

commit v8 on v7

--- a/solution.py
+++ b/solution.py
@@ -299,7 +299,7 @@
     chips, cores, capacity = answer_ref.shape[:3]
     answer = answer.reshape(cores, chips, capacity, LANES)
     for core in range(cores):
-        answer_ref[:, lax.rem(lax.axis_index("core") + core, cores)] = answer[core]
+        answer_ref[:, core] = answer[core]
 
 
 def update(steps, pieces, sender, table_rows, row_accumulators, cores, capacity):
@@ -324,28 +324,36 @@
     return new_table, sums.reshape(shard), answer
 
 
-def unpack_kernel(places_ref, returned_ref, out_ref):
-    matrix = places_ref[lax.axis_index("rep")]
-    cores = returned_ref.shape[1]
-    half = matrix.shape[1] // cores
-    fresh = None
-    for core in range(cores):
-        rows = returned_ref[:, lax.rem(lax.axis_index("core") + core, cores)].reshape(half, LANES)
-        added = product(matrix[:, core * half : (core + 1) * half], rows)
-        fresh = added if fresh is None else fresh + added
-    out_ref[...] = fresh.astype(BF16)
-
-
-def unpack(matrices, returned):
+def unpack_kernel(core, places_ref, returned_ref, *refs):
+    *before, out_ref = refs
+    half = returned_ref.shape[0] * returned_ref.shape[2]
+    matrix = places_ref[lax.axis_index("rep"), :, core * half : (core + 1) * half]
+    fresh = product(matrix, returned_ref[:, 0].reshape(half, LANES))
+    if before:
+        fresh = before[0][...] + fresh
+    out_ref[...] = fresh.astype(out_ref.dtype)
+
+
+def unpack(matrices, returned, core, before=None):
     _, quarter, places = matrices.shape
+
+    def kernel(*refs):
+        unpack_kernel(core, *refs)
+
+    earlier = [] if before is None else [before]
     return call(
-        unpack_kernel,
-        shaped((quarter, LANES), BF16),
-        [VMEM] * 2,
+        kernel,
+        shaped((quarter, LANES), F32 if before is None else BF16),
+        [VMEM] * (2 + len(earlier)),
         VMEM,
-        flops=2 * quarter * places * LANES,
+        flops=quarter * places * LANES,
         moved=2 * places * (quarter + LANES),
-    )(matrices, returned)
+    )(matrices, returned, *earlier)
+
+
+def exchange(blocks):
+    landed = lax.all_to_all(blocks, "chip", split_axis=0, concat_axis=0, tiled=True)
+    return landed, lax.ppermute(landed[:, 1:], "core", [(0, 1), (1, 0)])
 
 
 def send(piece, step, replicas):
@@ -375,8 +383,7 @@
     )
     message = propagate(pieces, tile, places, slots, cores, capacity)
 
-    landed = lax.all_to_all(message, "chip", split_axis=0, concat_axis=0, tiled=True)
-    across = lax.ppermute(landed[:, 1:], "core", [(0, 1), (1, 0)])
+    landed, across = exchange(message)
     sums, same = accumulate(landed, weight, mine, shard)
     piece, other = accumulate(across, weight, mine, shard, before=sums)
     pieces = [piece] + [send(piece, step, replicas) for step in order]
@@ -385,11 +392,9 @@
         [0, *order], pieces, sender, table_rows, row_accumulators, cores, capacity
     )
 
-    returned = lax.all_to_all(
-        answer.reshape(peers, capacity, width),
-        ("chip", "core"), split_axis=0, concat_axis=0, tiled=True,
-    )
-    fresh = unpack(places, returned.reshape(chips, cores, capacity, width))
+    landed, across = exchange(answer)
+    fresh = unpack(places, landed, 0)
+    fresh = unpack(places, across, 1, before=fresh)
     pieces = [send(fresh, step, replicas) for step in order]
     fresh_rows = jnp.zeros((rows, width), BF16)
     for step, piece in zip([0, *order], [fresh, *pieces]):

time: 80.8 us -> 80 us (0.990)
  blocking collectives: 40.1 us -> 34.8 us
  starting transfers between devices: 19.4 us -> 23.2 us
    all_to_all x2, blocking collectives: 40.1 us -> 34.8 us  [exchange(): lax.all_to_all(blocks, 'chip', split_axis=0, concat_axis=0, tiled=True)]
    ppermute x1 -> x2, starting transfers between devices: 3.6 us -> 7.37 us  [exchange(): return (landed, lax.ppermute(landed[:, 1:], 'core', [(0, 1), (1, 0)]))]
  transfers between devices with their start and end apart: 10 -> 11, of which waited for: 5 -> 6; matrix products, arithmetic and copies ran while one was open for 2% -> 2% of each run, Pallas kernels for 6% -> 6%
where the time goes in v8:
time: 80 us; the launch traced here: 79.6 us
  blocking collectives  34.8 us (43%)
  starting transfers between devices  23.2 us (29%)
  Pallas kernels  12.3 us (15%)
  waiting for transfers between devices  6.2 us (8%)
  local copies, waits for them, and re-layouts  2.35 us (3%)
    all_to_all x2, blocking collectives, exchange(): lax.all_to_all(blocks, 'chip', split_axis=0, concat_axis=0, tiled=True)  34.8 us
    ppermute x9, starting transfers between devices, send(): lax.ppermute(piece, 'rep', [(i, (i + step) % replicas) for i in range(rep...  15.8 us
    ppermute x2, starting transfers between devices, exchange(): return (landed, lax.ppermute(landed[:, 1:], 'core', [(0, 1), (1, 0)]))  7.37 us
    ppermute x9, waiting for transfers between devices, send(): lax.ppermute(piece, 'rep', [(i, (i + step) % replicas) for i in range(rep...  5.34 us
    pallas_call x1, Pallas kernels, propagate(): call(propagate_kernel, shaped((chips, cores, capacity // 2 + 1, 2, LANES)...  4.29 us
    pallas_call x1, Pallas kernels, plan(): call(kernel, [pltpu.VMEM(adjacency.shape, BF16), shaped((quarters, rows /...  3.39 us
    unnamed x8, local copies, waits for them, and re-layouts  2.08 us
    pallas_call x2, Pallas kernels, accumulate(): call(kernel, [piece, shaped((quarters, SUBLANES, places), jnp.int32)], [V...  1.74 us
  transfers between devices with their start and end apart: 11, of which 6 were waited for; matrix products, arithmetic and copies ran while one was open for 2% of the time, Pallas kernels for 6%

profile of v8, /device:TPU:1, one launch (start us, length us, event | category | flops | bytes accessed | tf_op | source)
XLA Modules:
  0.0 79.6 jit_solution(4474703122821064774)
XLA Ops:
  0.6 1.3 %shard_map.85 = (bf16[32,2048]{1,0:T(8,128)(2,1)S(1)}, bf16[32,2048]{1,0:T(8,128)(2,1)S(1)}, bf16[32,2048]{1,0:T(8,128)(2,1)S(1)}, bf16[32,2048]{1,0:T(8,128)(2,...) custom-call(bf16[2048,128]{1,0:T(8,128)(2,1)} %bitcast.7, s32[1,2048]{1,0:T(1,128)} %bitcast.8, s32[1,2048]{1,0:T(1,128)} %bitcast.9), custom_call_target="tpu_custom_call" | custom-call | tf_op jit(solution)/shard_map/pallas_call | solution.py:81
  2.0 3.7 %collective-permute-start = (bf16[32,2048]{1,0:T(8,128)(2,1)S(1)}, bf16[32,2048]{1,0:T(8,128)(2,1)S(1)}, u32[]{:S(2)}, u32[]{:S(2)}) collective-permute-start(bf16[32,2048]{1,0:T(8,128)(2,1)S(1)} %get-tuple-element.22), channel_id=1, source_target_pairs={{0,2},{1,3},{2,0},{3,1},{4,6},{5,7},{6,4},{7,5},{8,10},{9,11},{10,... | collective-permute-start | bytes 393224 | tf_op jit(solution)/shard_map/ppermute | solution.py:360
  5.6 0.3 collective-permute-start.1
  6.0 2.4 %collective-permute-start.2 = (bf16[32,2048]{1,0:T(8,128)(2,1)S(1)}, bf16[32,2048]{1,0:T(8,128)(2,1)S(1)}, u32[]{:S(2)}, u32[]{:S(2)}) collective-permute-start(bf16[32,2048]{1,0:T(8,128)(2,1)S(1)} %get-tuple-element.24), channel_id=1, source_target_pairs={{0,3},{1,0},{2,1},{3,2},{4,7},{5,4},{6,5},{7,6},{8,11},{9,8},{10,9... | collective-permute-start | bytes 393224 | tf_op jit(solution)/shard_map/ppermute | solution.py:360
  8.3 3.4 %shard_map.86 = (bf16[2048,2048]{1,0:T(8,128)(2,1)S(1)}, bf16[4,512,1024]{2,1,0:T(8,128)(2,1)S(1)}, bf16[64,128]{1,0:T(8,128)(2,1)S(1)}, bf16[4,128,512]{2,1,0:T(8,128)(2,1)S(1)}, f32[32,512]{1,0:T(8,128)S(1)}) custom-call(bf16[2048,2048]{1,0:T(8,128)(2,1)} %refs_0_.1, s32[1,2048]{1,0:T(1,128)S(1)} %get-tuple-element.25.refs_1_, ...), custom_call_target="tpu_custom_call" | custom-call | tf_op jit(solution)/shard_map/pallas_call | solution.py:155
  11.7 1.1 %collective-permute-done.1.refs_2_ = bf16[32,2048]{1,0:T(8,128)(2,1)S(1)} collective-permute-done((bf16[32,2048]{1,0:T(8,128)(2,1)S(1)}, bf16[32,2048]{1,0:T(8,128)(2,1)S(1)}, u32[]{:S(2)}, u32[]{:S(2)}) %collective-permute-start.1) | collective-permute-done | bytes 131104 | tf_op jit(solution)/shard_map/ppermute | solution.py:360
  12.9 4.3 %shard_map.87 = bf16[32,2,9,2,128]{4,3,2,1,0:T(2,128)(2,1)S(1)} custom-call(bf16[32,2048]{1,0:T(8,128)(2,1)S(1)} %get-tuple-element.21.refs_0_, bf16[32,2048]{1,0:T(8,128)(2,1)S(1)} %collective-permute-done.refs_1_, bf16[32,2048]{1,0:T(8,128)(2,1)S(1)} %collective-permute-done.1.refs_2_, bf16[32,2048]{1,0:T(8,128)(2,1)S(1)} %collective-permute-done.2.refs_3_, ...), custom_call_target="tpu_custom_call" | custom-call | flops 3221225472 | bytes 8388608 | tf_op jit(solution)/shard_map/pallas_call | solution.py:205
  17.2 21.3 %all_to_all.10.refs_0_ = bf16[32,2,9,2,128]{4,3,2,1,0:T(2,128)(2,1)S(1)} all-to-all(bf16[32,2,9,2,128]{4,3,2,1,0:T(2,128)(2,1)S(1)} %shard_map.87), channel_id=1, replica_groups=mesh['chip'=32,'core'=2,'rep'=4] {'chip'}, dimensions={0} | all-to-all | bytes 589824 | tf_op jit(solution)/shard_map/all_to_all | solution.py:355
  38.4 0.1 slice.8
  38.5 3.6 %collective-permute-start.3 = (bf16[32,1,9,2,128]{4,3,2,1,0:T(2,128)(2,1)S(1)}, bf16[32,1,9,2,128]{4,3,2,1,0:T(2,128)(2,1)S(1)}, u32[]{:S(2)}, u32[]{:S(2)}) collective-permute-start(bf16[32,1,9,2,128]{4,3,2,1,0:T(2,128)(2,1)S(1)} %slice.8), channel_id=1, source_target_pairs={{0,4},{4,0},{1,5},{5,1},{2,6},{6,2},{3,7},{7,3},{8,12},{12,8},{9,1... | collective-permute-start | bytes 442376 | tf_op jit(solution)/shard_map/ppermute | solution.py:356
  42.1 0.8 %shard_map.88 = (f32[512,128]{1,0:T(8,128)S(1)}, s32[4,8,512]{2,1,0:T(8,128)S(1)}) custom-call(bf16[32,2,9,2,128]{4,3,2,1,0:T(2,128)(2,1)S(1)} %all_to_all.10.refs_0_, bf16[4,128,512]{2,1,0:T(8,128)(2,1)S(1)} %get-tuple-element.30.refs_1_, f32[32,512]{1,0:T(8,128)S(1)} %get-tuple-element.31.refs_2_), custom_call_target="tpu_custom_call" | custom-call | flops 268435456 | bytes 655360 | tf_op jit(solution)/shard_map/pallas_call | solution.py:258
  43.0 0.2 collective-permute-done.3.refs_0_
  43.1 0.9 %shard_map.89 = (bf16[32,512]{1,0:T(8,128)(2,1)S(1)}, s32[4,8,512]{2,1,0:T(8,128)S(1)}) custom-call(bf16[32,1,9,2,128]{4,3,2,1,0:T(2,128)(2,1)S(1)} %collective-permute-done.3.refs_0_, bf16[4,128,512]{2,1,0:T(8,128)(2,1)S(1)} %get-tuple-element.30.refs_1_, f32[32,512]{1,0:T(8,128)S(1)} %get-tuple-element.31.refs_2_, f32[512,128]{1,0:T(8,128)S(1)} %get-tuple-element.32.refs_3_), custom_call_target="tpu_custom_call" | custom-call | flops 268435456 | bytes 655360 | tf_op jit(solution)/shard_map/pallas_call | solution.py:258
  44.0 1.8 %collective-permute-start.4 = (bf16[32,512]{1,0:T(8,128)(2,1)S(1)}, bf16[32,512]{1,0:T(8,128)(2,1)S(1)}, u32[]{:S(2)}, u32[]{:S(2)}) collective-permute-start(bf16[32,512]{1,0:T(8,128)(2,1)S(1)} %get-tuple-element.33.refs_0_), channel_id=1, source_target_pairs={{0,2},{1,3},{2,0},{3,1},{4,6},{5,7},{6,4},{7,5},{8,10},{9,11},{10,... | collective-permute-start | bytes 98312 | tf_op jit(solution)/shard_map/ppermute | solution.py:360
  45.8 1.7 %collective-permute-start.5 = (bf16[32,512]{1,0:T(8,128)(2,1)S(1)}, bf16[32,512]{1,0:T(8,128)(2,1)S(1)}, u32[]{:S(2)}, u32[]{:S(2)}) collective-permute-start(bf16[32,512]{1,0:T(8,128)(2,1)S(1)} %get-tuple-element.33.refs_0_), channel_id=1, source_target_pairs={{0,1},{1,2},{2,3},{3,0},{4,5},{5,6},{6,7},{7,4},{8,9},{9,10},{10,1... | collective-permute-start | bytes 98312 | tf_op jit(solution)/shard_map/ppermute | solution.py:360
  47.5 1.0 %collective-permute-start.6 = (bf16[32,512]{1,0:T(8,128)(2,1)S(1)}, bf16[32,512]{1,0:T(8,128)(2,1)S(1)}, u32[]{:S(2)}, u32[]{:S(2)}) collective-permute-start(bf16[32,512]{1,0:T(8,128)(2,1)S(1)} %get-tuple-element.33.refs_0_), channel_id=1, source_target_pairs={{0,3},{1,0},{2,1},{3,2},{4,7},{5,4},{6,5},{7,6},{8,11},{9,8},{10,9... | collective-permute-start | bytes 98312 | tf_op jit(solution)/shard_map/ppermute | solution.py:360
  48.5 0.3 shard_map.90.refs_4_
  48.8 1.0 %collective-permute-done.5.refs_2_ = bf16[32,512]{1,0:T(8,128)(2,1)S(1)} collective-permute-done((bf16[32,512]{1,0:T(8,128)(2,1)S(1)}, bf16[32,512]{1,0:T(8,128)(2,1)S(1)}, u32[]{:S(2)}, u32[]{:S(2)}) %collective-permute-start.5) | collective-permute-done | bytes 32800 | tf_op jit(solution)/shard_map/ppermute | solution.py:360
  49.8 0.4 collective-permute-done.6.refs_3_
  50.3 0.6 shard_map.91
  50.9 13.6 %all_to_all.11.refs_1_ = bf16[32,2,16,128]{3,2,1,0:T(8,128)(2,1)S(1)} all-to-all(bf16[32,2,16,128]{3,2,1,0:T(8,128)(2,1)S(1)} %get-tuple-element.38), channel_id=1, replica_groups=mesh['chip'=32,'core'=2,'rep'=4] {'chip'}, dimensions={0} | all-to-all | bytes 524288 | tf_op jit(solution)/shard_map/all_to_all | solution.py:355
  64.4 3.8 %collective-permute-start.7 = (bf16[32,1,16,128]{3,2,1,0:T(8,128)(2,1)S(1)}, bf16[32,1,16,128]{3,2,1,0:T(8,128)(2,1)S(1)}, u32[]{:S(2)}, u32[]{:S(2)}) collective-permute-start(bf16[32,1,16,128]{3,2,1,0:T(8,128)(2,1)S(1)} %slice.9), channel_id=1, source_target_pairs={{0,4},{4,0},{1,5},{5,1},{2,6},{6,2},{3,7},{7,3},{8,12},{12,8},{9,1... | collective-permute-start | bytes 393224 | tf_op jit(solution)/shard_map/ppermute | solution.py:356
  68.2 0.3 shard_map.92.refs_2_
  68.5 0.7 collective-permute-done.7.refs_1_
  69.2 0.3 shard_map.93
  69.5 2.3 %collective-permute-start.8 = (bf16[512,128]{1,0:T(8,128)(2,1)S(1)}, bf16[512,128]{1,0:T(8,128)(2,1)S(1)}, u32[]{:S(2)}, u32[]{:S(2)}) collective-permute-start(bf16[512,128]{1,0:T(8,128)(2,1)S(1)} %shard_map.93), channel_id=1, source_target_pairs={{0,2},{1,3},{2,0},{3,1},{4,6},{5,7},{6,4},{7,5},{8,10},{9,11},{10,... | collective-permute-start | bytes 393224 | tf_op jit(solution)/shard_map/ppermute | solution.py:360
  71.8 0.7 copy.13
  72.5 0.6 copy.14
  73.1 0.7 collective-permute-start.9
  73.8 2.0 %collective-permute-start.10 = (bf16[512,128]{1,0:T(8,128)(2,1)S(1)}, bf16[512,128]{1,0:T(8,128)(2,1)S(1)}, u32[]{:S(2)}, u32[]{:S(2)}) collective-permute-start(bf16[512,128]{1,0:T(8,128)(2,1)S(1)} %shard_map.93), channel_id=1, source_target_pairs={{0,3},{1,0},{2,1},{3,2},{4,7},{5,4},{6,5},{7,6},{8,11},{9,8},{10,9... | collective-permute-start | bytes 393224 | tf_op jit(solution)/shard_map/ppermute | solution.py:360
  75.9 2.8 %collective-permute-done.9 = bf16[512,128]{1,0:T(8,128)(2,1)S(1)} collective-permute-done((bf16[512,128]{1,0:T(8,128)(2,1)S(1)}, bf16[512,128]{1,0:T(8,128)(2,1)S(1)}, u32[]{:S(2)}, u32[]{:S(2)}) %collective-permute-start.9) | collective-permute-done | bytes 131104 | tf_op jit(solution)/shard_map/ppermute | solution.py:360
  78.8 0.8 copy-done.2
  (16 shorter events, 0.2 us)
Async XLA Ops:
  2.0 9.7 %collective-permute-start = (bf16[32,2048]{1,0:T(8,128)(2,1)S(1)}, bf16[32,2048]{1,0:T(8,128)(2,1)S(1)}, u32[]{:S(2)}, u32[]{:S(2)}) collective-permute-start(bf16[32,2048]{1,0:T(8,128)(2,1)S(1)} %get-tuple-element.22), channel_id=1, source_target_pairs={{0,2},{1,3},{2,0},{3,1},{4,6},{5,7},{6,4},{7,5},{8,10},{9,11},{10,... | collective-permute-start | bytes 393224 | tf_op jit(solution)/shard_map/ppermute | solution.py:360
  5.6 7.2 %collective-permute-start.1 = (bf16[32,2048]{1,0:T(8,128)(2,1)S(1)}, bf16[32,2048]{1,0:T(8,128)(2,1)S(1)}, u32[]{:S(2)}, u32[]{:S(2)}) collective-permute-start(bf16[32,2048]{1,0:T(8,128)(2,1)S(1)} %get-tuple-element.23), channel_id=1, source_target_pairs={{0,1},{1,2},{2,3},{3,0},{4,5},{5,6},{6,7},{7,4},{8,9},{9,10},{10,1... | collective-permute-start | bytes 393224 | tf_op jit(solution)/shard_map/ppermute | solution.py:360
  6.0 6.9 %collective-permute-start.2 = (bf16[32,2048]{1,0:T(8,128)(2,1)S(1)}, bf16[32,2048]{1,0:T(8,128)(2,1)S(1)}, u32[]{:S(2)}, u32[]{:S(2)}) collective-permute-start(bf16[32,2048]{1,0:T(8,128)(2,1)S(1)} %get-tuple-element.24), channel_id=1, source_target_pairs={{0,3},{1,0},{2,1},{3,2},{4,7},{5,4},{6,5},{7,6},{8,11},{9,8},{10,9... | collective-permute-start | bytes 393224 | tf_op jit(solution)/shard_map/ppermute | solution.py:360
  12.8 37.4 %copy-start = (f32[512,128]{1,0:T(8,128)S(1)}, f32[512,128]{1,0:T(8,128)}, u32[]{:S(2)}) copy-start(f32[512,128]{1,0:T(8,128)} %refs_5_.1) | copy-start | bytes 786436
  12.8 37.4 %copy-start.1 = (f32[512]{0:T(512)S(1)}, f32[512]{0:T(512)}, u32[]{:S(2)}) copy-start(f32[512]{0:T(512)} %param.11) | copy-start | bytes 6148
  38.5 4.6 %collective-permute-start.3 = (bf16[32,1,9,2,128]{4,3,2,1,0:T(2,128)(2,1)S(1)}, bf16[32,1,9,2,128]{4,3,2,1,0:T(2,128)(2,1)S(1)}, u32[]{:S(2)}, u32[]{:S(2)}) collective-permute-start(bf16[32,1,9,2,128]{4,3,2,1,0:T(2,128)(2,1)S(1)} %slice.8), channel_id=1, source_target_pairs={{0,4},{4,0},{1,5},{5,1},{2,6},{6,2},{3,7},{7,3},{8,12},{12,8},{9,1... | collective-permute-start | bytes 442376 | tf_op jit(solution)/shard_map/ppermute | solution.py:356
  44.0 4.8 %collective-permute-start.4 = (bf16[32,512]{1,0:T(8,128)(2,1)S(1)}, bf16[32,512]{1,0:T(8,128)(2,1)S(1)}, u32[]{:S(2)}, u32[]{:S(2)}) collective-permute-start(bf16[32,512]{1,0:T(8,128)(2,1)S(1)} %get-tuple-element.33.refs_0_), channel_id=1, source_target_pairs={{0,2},{1,3},{2,0},{3,1},{4,6},{5,7},{6,4},{7,5},{8,10},{9,11},{10,... | collective-permute-start | bytes 98312 | tf_op jit(solution)/shard_map/ppermute | solution.py:360
  45.8 4.0 %collective-permute-start.5 = (bf16[32,512]{1,0:T(8,128)(2,1)S(1)}, bf16[32,512]{1,0:T(8,128)(2,1)S(1)}, u32[]{:S(2)}, u32[]{:S(2)}) collective-permute-start(bf16[32,512]{1,0:T(8,128)(2,1)S(1)} %get-tuple-element.33.refs_0_), channel_id=1, source_target_pairs={{0,1},{1,2},{2,3},{3,0},{4,5},{5,6},{6,7},{7,4},{8,9},{9,10},{10,1... | collective-permute-start | bytes 98312 | tf_op jit(solution)/shard_map/ppermute | solution.py:360
  47.5 2.8 %collective-permute-start.6 = (bf16[32,512]{1,0:T(8,128)(2,1)S(1)}, bf16[32,512]{1,0:T(8,128)(2,1)S(1)}, u32[]{:S(2)}, u32[]{:S(2)}) collective-permute-start(bf16[32,512]{1,0:T(8,128)(2,1)S(1)} %get-tuple-element.33.refs_0_), channel_id=1, source_target_pairs={{0,3},{1,0},{2,1},{3,2},{4,7},{5,4},{6,5},{7,6},{8,11},{9,8},{10,9... | collective-permute-start | bytes 98312 | tf_op jit(solution)/shard_map/ppermute | solution.py:360
  64.4 4.8 %collective-permute-start.7 = (bf16[32,1,16,128]{3,2,1,0:T(8,128)(2,1)S(1)}, bf16[32,1,16,128]{3,2,1,0:T(8,128)(2,1)S(1)}, u32[]{:S(2)}, u32[]{:S(2)}) collective-permute-start(bf16[32,1,16,128]{3,2,1,0:T(8,128)(2,1)S(1)} %slice.9), channel_id=1, source_target_pairs={{0,4},{4,0},{1,5},{5,1},{2,6},{6,2},{3,7},{7,3},{8,12},{12,8},{9,1... | collective-permute-start | bytes 393224 | tf_op jit(solution)/shard_map/ppermute | solution.py:356
  69.5 6.4 %collective-permute-start.8 = (bf16[512,128]{1,0:T(8,128)(2,1)S(1)}, bf16[512,128]{1,0:T(8,128)(2,1)S(1)}, u32[]{:S(2)}, u32[]{:S(2)}) collective-permute-start(bf16[512,128]{1,0:T(8,128)(2,1)S(1)} %shard_map.93), channel_id=1, source_target_pairs={{0,2},{1,3},{2,0},{3,1},{4,6},{5,7},{6,4},{7,5},{8,10},{9,11},{10,... | collective-permute-start | bytes 393224 | tf_op jit(solution)/shard_map/ppermute | solution.py:360
  73.1 5.6 %collective-permute-start.9 = (bf16[512,128]{1,0:T(8,128)(2,1)S(1)}, bf16[512,128]{1,0:T(8,128)(2,1)S(1)}, u32[]{:S(2)}, u32[]{:S(2)}) collective-permute-start(bf16[512,128]{1,0:T(8,128)(2,1)S(1)} %shard_map.93), channel_id=1, source_target_pairs={{0,1},{1,2},{2,3},{3,0},{4,5},{5,6},{6,7},{7,4},{8,9},{9,10},{10,1... | collective-permute-start | bytes 393224 | tf_op jit(solution)/shard_map/ppermute | solution.py:360
  73.8 4.9 %collective-permute-start.10 = (bf16[512,128]{1,0:T(8,128)(2,1)S(1)}, bf16[512,128]{1,0:T(8,128)(2,1)S(1)}, u32[]{:S(2)}, u32[]{:S(2)}) collective-permute-start(bf16[512,128]{1,0:T(8,128)(2,1)S(1)} %shard_map.93), channel_id=1, source_target_pairs={{0,3},{1,0},{2,1},{3,2},{4,7},{5,4},{6,5},{7,6},{8,11},{9,8},{10,9... | collective-permute-start | bytes 393224 | tf_op jit(solution)/shard_map/ppermute | solution.py:360
  78.8 0.8 %copy-start.2 = (bf16[2048,128]{1,0:T(8,128)(2,1)}, bf16[2048,128]{1,0:T(8,128)(2,1)S(1)}, u32[]{:S(2)}) copy-start(bf16[2048,128]{1,0:T(8,128)(2,1)S(1)} %constant_dynamic-update-slice_fusion) | copy-start | bytes 1572868
